TPU v7x, 32 devices: a whole 2x2x4 slice. The times are simulated.
32 devices in a mesh: dp: 8 (over z, x), fsdp: 4 (over y, core).
Axes of the slice: x: 2, y: 2, z: 4, core: 2. Of those that a mesh axis runs over, the one named last changes fastest.
Arguments:
- tokens: bfloat16 [32768, 768], P(('dp', 'fsdp')), may hold values from -6 to 6
- w_query: float32 [768, 768], P(('dp', 'fsdp')), may hold values from -0.21875 to 0.21875
- w_pair: float32 [768, 128], P(('dp', 'fsdp')), may hold values from -0.21875 to 0.21875
- w_attn_out: float32 [768, 768], P(('dp', 'fsdp')), may hold values from -1.75 to 1.75
- w_up: float32 [768, 3072], P(('dp', 'fsdp')), may hold values from -0.21875 to 0.21875
- w_down: float32 [3072, 768], P(('dp', 'fsdp')), may hold values from -0.109375 to 0.109375
- ln_gains: float32 [2, 768], P(None, ('dp', 'fsdp')), may hold values from 0.5 to 1.5
- ln_biases: float32 [2, 768], P(None, ('dp', 'fsdp')), may hold values from -1.8 to 1.8
- cotangent: bfloat16 [32768, 768], P(('dp', 'fsdp')), may hold values from -6 to 6
- subset_tags: int32 [32], P(('dp', 'fsdp')), may hold values from 0 to 21
- subset_weights: float32 [22], replicated, may hold values from 0.25 to 4
Outputs:
- mixed: bfloat16 [32768, 768], P(('dp', 'fsdp'))
- grad_tokens: bfloat16 [32768, 768], P(('dp', 'fsdp'))
- grad_query: float32 [768, 768], P(('dp', 'fsdp'))
- grad_pair: float32 [768, 128], P(('dp', 'fsdp'))
- grad_attn_out: float32 [768, 768], P(('dp', 'fsdp'))
- grad_up: float32 [768, 3072], P(('dp', 'fsdp'))
- grad_down: float32 [3072, 768], P(('dp', 'fsdp'))
- grad_gains: float32 [2, 768], P(None, ('dp', 'fsdp'))
- grad_biases: float32 [2, 768], P(None, ('dp', 'fsdp'))
All inputs are finite; a program needn't handle non-finite values.
Results may differ from a plain program's by a relative error of at most 0.012.
The roundings to bfloat16 on the way count: a program that leaves them out, or rounds other values in their place, can miss the bound.
Values may be sent and summed in bfloat16 or wider, within the bound.
A program may use at most 192 MiB of HBM per device.

v0:
```python
import jax
import jax.numpy as jnp
from jax import lax
from jax.sharding import PartitionSpec as P

D = 768
H = 12
HD = 64
ROT = 16
SUBSETS = 22
SEQ = 1024


eps_norm = 1e-05


def angles(length):
    inverse = 10000.0 ** (-(jnp.arange(ROT // 2, dtype=jnp.float32) * 2.0) / ROT)
    phase = jnp.arange(length, dtype=jnp.float32)[:, None] * inverse[None, :]
    return (jnp.cos(phase), jnp.sin(phase))


def rotate(field, cos_table, sin_table):
    half = ROT // 2
    first = field[..., :half]
    second = field[..., half:ROT]
    return jnp.concatenate(
        [
            first * cos_table - second * sin_table,
            second * cos_table + first * sin_table,
            field[..., ROT:],
        ],
        axis=-1,
    )


def unrotate(field, cos_table, sin_table):
    half = ROT // 2
    first = field[..., :half]
    second = field[..., half:ROT]
    return jnp.concatenate(
        [
            first * cos_table + second * sin_table,
            second * cos_table - first * sin_table,
            field[..., ROT:],
        ],
        axis=-1,
    )


def gelu_exact(inputs):
    return jax.nn.gelu(inputs, approximate=False)


def fetch_weights(query_w, pair_w, out_w, up_w, down_w, gain_rows, bias_rows):
    return (
        lax.all_gather(query_w, ("dp", "fsdp"), axis=0, tiled=True),
        lax.all_gather(pair_w, ("dp", "fsdp"), axis=0, tiled=True),
        lax.all_gather(out_w, ("dp", "fsdp"), axis=0, tiled=True),
        lax.all_gather(up_w, ("dp", "fsdp"), axis=0, tiled=True),
        lax.all_gather(down_w, ("dp", "fsdp"), axis=0, tiled=True),
        lax.all_gather(gain_rows, ("dp", "fsdp"), axis=1, tiled=True),
        lax.all_gather(bias_rows, ("dp", "fsdp"), axis=1, tiled=True),
    )


def send_grads(query_g, pair_g, out_g, up_g, down_g, gain_g, bias_g):
    return (
        lax.psum_scatter(query_g, ("dp", "fsdp"), scatter_dimension=0, tiled=True),
        lax.psum_scatter(pair_g, ("dp", "fsdp"), scatter_dimension=0, tiled=True),
        lax.psum_scatter(out_g, ("dp", "fsdp"), scatter_dimension=0, tiled=True),
        lax.psum_scatter(up_g, ("dp", "fsdp"), scatter_dimension=0, tiled=True),
        lax.psum_scatter(down_g, ("dp", "fsdp"), scatter_dimension=0, tiled=True),
        lax.psum_scatter(gain_g, ("dp", "fsdp"), scatter_dimension=1, tiled=True),
        lax.psum_scatter(bias_g, ("dp", "fsdp"), scatter_dimension=1, tiled=True),
    )


def body(
    tokens,
    w_query,
    w_pair,
    w_attn_out,
    w_up,
    w_down,
    ln_gains,
    ln_biases,
    cotangent,
    subset_tags,
    subset_weights,
):
    bf16 = jnp.bfloat16
    f32 = jnp.float32
    rows_here = subset_tags.shape[0]
    token_count = rows_here * SEQ
    onehot = (subset_tags[:, None] == jnp.arange(SUBSETS, dtype=jnp.int32)[None, :]).astype(f32)
    counts = lax.psum(jnp.sum(onehot, axis=0), ("dp", "fsdp"))
    masters = (
        w_query.astype(bf16),
        w_pair.astype(bf16),
        w_attn_out.astype(bf16),
        w_up.astype(bf16),
        w_down.astype(bf16),
        ln_gains.astype(bf16),
        ln_biases.astype(bf16),
    )
    gathered = fetch_weights(
        masters[0], masters[1], masters[2], masters[3], masters[4], masters[5], masters[6]
    )
    query_w, pair_w, out_w, up_w, down_w, gain_rows, bias_rows = gathered
    inputs = tokens.astype(f32)
    row_mean = jnp.mean(inputs, axis=-1, keepdims=True)
    centred = inputs - row_mean
    inv_std = lax.rsqrt(jnp.mean(centred * centred, axis=-1, keepdims=True) + eps_norm)
    normed = centred * inv_std
    gain_f = gain_rows.astype(f32)
    bias_f = bias_rows.astype(f32)
    first_in = (normed * gain_f[0] + bias_f[0]).astype(bf16)
    second_in = (normed * gain_f[1] + bias_f[1]).astype(bf16)
    cos_table, sin_table = angles(SEQ)
    query = jnp.dot(first_in, query_w, preferred_element_type=f32).reshape(rows_here, SEQ, H, HD)
    query = rotate(query, cos_table[:, None, :], sin_table[:, None, :]).astype(bf16)
    paired = jnp.dot(first_in, pair_w, preferred_element_type=f32).reshape(rows_here, SEQ, 2 * HD)
    key_rows = rotate(paired[..., :HD], cos_table, sin_table).astype(bf16)
    values = paired[..., HD:].astype(bf16)
    block_len = min(512, SEQ)
    block_count = SEQ // block_len

    def block_scores(block_start, block_stop):
        scores = (
            jnp.einsum(
                "rqhd,rkd->rhqk",
                query[:, block_start:block_stop],
                key_rows[:, :block_stop],
                preferred_element_type=f32,
            )
            * 0.125
        )
        causal = jnp.arange(block_stop)[None, :] <= (block_start + jnp.arange(block_len))[:, None]
        return jnp.where(causal[None, None], scores, -jnp.inf)

    outputs = []
    logsums = []
    for block_number in range(block_count):
        block_start = block_number * block_len
        block_stop = block_start + block_len
        scores = block_scores(block_start, block_stop)
        row_peak = jnp.max(scores, axis=-1, keepdims=True)
        weights_exp = jnp.exp(scores - row_peak)
        row_total = jnp.sum(weights_exp, axis=-1, keepdims=True)
        prob_rows = (weights_exp / row_total).astype(bf16)
        outputs.append(
            jnp.einsum(
                "rhqk,rkd->rqhd", prob_rows, values[:, :block_stop], preferred_element_type=f32
            )
        )
        logsums.append(row_peak + jnp.log(row_total))
    attended = jnp.concatenate(outputs, axis=1).reshape(token_count, D).astype(bf16)
    up_pre = jnp.dot(second_in, up_w, preferred_element_type=f32)
    hidden = gelu_exact(up_pre).astype(bf16)
    branch = jnp.dot(attended, out_w, preferred_element_type=f32) + jnp.dot(
        hidden, down_w, preferred_element_type=f32
    )
    mixed = (inputs + branch).astype(bf16)
    query_w, pair_w, out_w, up_w, down_w, gain_rows, bias_rows = fetch_weights(
        masters[0], masters[1], masters[2], masters[3], masters[4], masters[5], masters[6]
    )
    gain_f = gain_rows.astype(f32)
    row_count = jnp.sum(onehot * counts[None, :], axis=1)
    row_weight = jnp.sum(onehot * subset_weights[None, :], axis=1)
    total_rows = rows_here * lax.axis_size("dp") * lax.axis_size("fsdp")
    row_scale = row_weight / row_count * (total_rows / SUBSETS)
    grad_out = (
        cotangent.astype(f32).reshape(rows_here, SEQ, D) * row_scale[:, None, None]
    ).reshape(token_count, D)
    grad_branch = grad_out.astype(bf16)
    grad_down = jnp.einsum("nf,nd->fd", hidden, grad_branch, preferred_element_type=f32)
    d_hidden = jnp.einsum("nd,fd->nf", grad_branch, down_w, preferred_element_type=f32)
    gelu_pull = jax.vjp(gelu_exact, up_pre)[1]
    d_up = gelu_pull(d_hidden)[0].astype(bf16)
    grad_up = jnp.einsum("nd,nf->df", second_in, d_up, preferred_element_type=f32)
    d_second = jnp.einsum("nf,df->nd", d_up, up_w, preferred_element_type=f32)
    grad_attn = jnp.einsum("nd,ne->de", attended, grad_branch, preferred_element_type=f32)
    d_attended = (
        jnp.einsum("ne,de->nd", grad_branch, out_w, preferred_element_type=f32)
        .astype(bf16)
        .reshape(rows_here, SEQ, H, HD)
    )
    query_grads = []
    d_keys = jnp.zeros((rows_here, SEQ, HD), f32)
    d_values = jnp.zeros((rows_here, SEQ, HD), f32)
    for block_number in range(block_count):
        block_start = block_number * block_len
        block_stop = block_start + block_len
        scores = block_scores(block_start, block_stop)
        prob_rows = jnp.exp(scores - logsums[block_number])
        d_probs = jnp.einsum(
            "rqhd,rkd->rhqk",
            d_attended[:, block_start:block_stop],
            values[:, :block_stop],
            preferred_element_type=f32,
        )
        d_scores = (
            prob_rows * (d_probs - jnp.sum(d_probs * prob_rows, axis=-1, keepdims=True))
        ).astype(bf16)
        query_grads.append(
            jnp.einsum(
                "rhqk,rkd->rqhd", d_scores, key_rows[:, :block_stop], preferred_element_type=f32
            )
            * 0.125
        )
        d_keys = d_keys.at[:, :block_stop].add(
            jnp.einsum(
                "rhqk,rqhd->rkd",
                d_scores,
                query[:, block_start:block_stop],
                preferred_element_type=f32,
            )
            * 0.125
        )
        d_values = d_values.at[:, :block_stop].add(
            jnp.einsum(
                "rhqk,rqhd->rkd",
                prob_rows.astype(bf16),
                d_attended[:, block_start:block_stop],
                preferred_element_type=f32,
            )
        )
    d_query = jnp.concatenate(query_grads, axis=1)
    d_query = (
        unrotate(d_query, cos_table[:, None, :], sin_table[:, None, :])
        .reshape(token_count, D)
        .astype(bf16)
    )
    d_pair = (
        jnp.concatenate([unrotate(d_keys, cos_table, sin_table), d_values], axis=-1)
        .reshape(token_count, 2 * HD)
        .astype(bf16)
    )
    grad_query = jnp.einsum("nd,ne->de", first_in, d_query, preferred_element_type=f32)
    grad_pair = jnp.einsum("nd,ne->de", first_in, d_pair, preferred_element_type=f32)
    d_first = jnp.einsum("ne,de->nd", d_query, query_w, preferred_element_type=f32) + jnp.einsum(
        "ne,de->nd", d_pair, pair_w, preferred_element_type=f32
    )
    grad_gains = jnp.stack([jnp.sum(d_first * normed, axis=0), jnp.sum(d_second * normed, axis=0)])
    grad_biases = jnp.stack([jnp.sum(d_first, axis=0), jnp.sum(d_second, axis=0)])
    d_normed = d_first * gain_f[0] + d_second * gain_f[1]
    d_inputs = inv_std * (
        d_normed
        - jnp.mean(d_normed, axis=-1, keepdims=True)
        - normed * jnp.mean(d_normed * normed, axis=-1, keepdims=True)
    )
    grad_tokens = (grad_out + d_inputs).astype(bf16)
    shards = send_grads(
        grad_query, grad_pair, grad_attn, grad_up, grad_down, grad_gains, grad_biases
    )
    return (
        mixed,
        grad_tokens,
        shards[0],
        shards[1],
        shards[2],
        shards[3],
        shards[4],
        shards[5],
        shards[6],
    )


def solution(mesh):
    in_specs = (
        P(("dp", "fsdp"), None),
        P(("dp", "fsdp"), None),
        P(("dp", "fsdp"), None),
        P(("dp", "fsdp"), None),
        P(("dp", "fsdp"), None),
        P(("dp", "fsdp"), None),
        P(None, ("dp", "fsdp")),
        P(None, ("dp", "fsdp")),
        P(("dp", "fsdp"), None),
        P(("dp", "fsdp")),
        P(),
    )
    out_specs = (
        P(("dp", "fsdp"), None),
        P(("dp", "fsdp"), None),
        P(("dp", "fsdp"), None),
        P(("dp", "fsdp"), None),
        P(("dp", "fsdp"), None),
        P(("dp", "fsdp"), None),
        P(("dp", "fsdp"), None),
        P(None, ("dp", "fsdp")),
        P(None, ("dp", "fsdp")),
    )
    return jax.shard_map(body, mesh=mesh, in_specs=in_specs, out_specs=out_specs, check_vma=False)
```

profile of v0, /device:TPU:25, one launch (start us, length us, event | category | flops | bytes accessed | tf_op | source)
XLA Modules:
  0.0 892.4 jit_solution(17904681205967156884)
XLA Ops:
  7.2 1.6 convert_element_type.128
  8.9 1.5 convert_element_type.132
  10.5 1.6 convert_element_type.134
  12.2 1.6 convert_element_type.136
  15.4 1.7 convert_reduce_fusion
  17.8 33.6 %all-gather.1 = bf16[32,24,2]{1,2,0:T(2,128)(2,1)S(1)} all-gather(bf16[1,24,2]{1,2,0:T(2,128)(2,1)S(1)} %convert_bitcast_fusion), channel_id=1, replica_groups=mesh['dp'=8,'fsdp'=4] {'dp','fsdp'}, dimensions={0}, use_global_device_ids=true | all-gather | bytes 3168 | tf_op jit(solution)/shard_map/all_gather | solution.py:63
  51.5 37.2 %all-gather = bf16[32,24,2]{1,2,0:T(2,128)(2,1)S(1)} all-gather(bf16[1,24,2]{1,2,0:T(2,128)(2,1)S(1)} %convert_bitcast_fusion.1), channel_id=1, replica_groups=mesh['dp'=8,'fsdp'=4] {'dp','fsdp'}, dimensions={0}, use_global_device_ids=true | all-gather | bytes 3168 | tf_op jit(solution)/shard_map/all_gather | solution.py:62
  91.2 37.9 %all_gather.29 = bf16[768,128]{1,0:T(8,128)(2,1)S(1)} all-gather(bf16[24,128]{1,0:T(8,128)(2,1)S(1)} %convert_element_type.127), channel_id=1, replica_groups=mesh['dp'=8,'fsdp'=4] {'dp','fsdp'}, dimensions={0}, use_global_device_ids=true | all-gather | bytes 202752 | tf_op jit(solution)/shard_map/all_gather | solution.py:58
  132.0 44.2 %psum.7 = f32[22]{0:T(128)S(1)} all-reduce(f32[22]{0:T(128)S(1)} %fusion.95), channel_id=1, replica_groups=mesh['dp'=8,'fsdp'=4] {'dp','fsdp'}, use_global_device_ids=true, to_apply=%region_7.8 | all-reduce | flops 22 | bytes 176 | tf_op jit(solution)/shard_map/psum | solution.py:97
  180.0 2.7 fusion.114
  183.2 2.0 fusion.113
  185.2 1.8 fusion.21
  187.0 2.6 copy-done.1
  190.0 3.2 convolution_convert_fusion
  193.2 11.7 %fusion.10 = (f32[12,512]{1,0:T(8,128)S(1)}, f32[512,512,12]{1,0,2:T(8,128)}) fusion(f32[1,12,512,512]{2,3,1,0:T(8,128)} %copy-done.1, f32[12,512]{1,0:T(8,128)S(1)} %log_add_fusion.1, bf16[1,1024,12,64]{1,3,2,0:T(8,128)(2,1)S(1)} %bitcast.226, bf16[1,1024,128]{1,2,0:T(8,128)(2,1)S(1)} %get-tuple-element.106), kind=kOutput, calls=%fused_computation.19 | convolution fusion | flops 412084224 | bytes 26075136 | tf_op jit(solution)/shard_map/rqhd,rkd->rhqk/dot_general | solution.py:197
  204.9 1.5 slice-done.2
  206.4 7.1 fusion.26
  213.5 2.7 fusion.70
  216.2 5.3 fusion.111
  221.5 4.8 fusion.3
  226.3 3.7 copy-done
  230.1 18.2 %fusion = (f32[12,512]{1,0:T(8,128)S(1)}, f32[1024,512,12]{1,0,2:T(8,128)}) fusion(f32[1,12,512,1024]{2,3,1,0:T(8,128)} %copy-done, f32[12,512]{1,0:T(8,128)S(1)} %log_add_fusion, bf16[1,1024,12,64]{1,3,2,0:T(8,128)(2,1)} %bitcast.227, bf16[1,1024,128]{1,2,0:T(8,128)(2,1)S(1)} %copy-done.21), kind=kOutput, calls=%fused_computation.3 | convolution fusion | flops 824174592 | bytes 51306496 | tf_op jit(solution)/shard_map/rqhd,rkd->rhqk/dot_general | solution.py:197
  248.2 17.2 %fusion.9 = bf16[12,512,1024]{1,2,0:T(8,128)(2,1)S(1)} fusion(f32[1024,512,12]{1,0,2:T(8,128)} %get-tuple-element.111, f32[1,12,512,1024]{2,3,1,0:T(8,128)} %copy-done, f32[12,512]{1,0:T(8,128)S(1)} %get-tuple-element.110, f32[12,512]{1,0:T(8,128)S(1)} %log_add_fusion), kind=kLoop, calls=%fused_computation.15 | loop fusion | flops 25165824 | bytes 62963712 | tf_op jit(solution)/shard_map/reshape.160
  265.5 3.9 fusion.68
  270.5 6.6 fusion.71
  277.2 10.4 %fusion.77 = bf16[1,1024,64]{1,2,0:T(8,128)(2,1)S(1)} fusion(f32[1,12,512,1024]{2,3,1,0:T(8,128)} %copy-done, f32[12,512]{1,0:T(8,128)S(1)} %log_add_fusion, bf16[1,1024,12,64]{1,3,2,0:T(8,128)(2,1)S(1)} %bitcast.229, f32[1,512,64]{1,2,0:T(8,128)S(1)} %fusion.71), kind=kOutput, calls=%fused_computation.110 | convolution fusion | flops 818020352 | bytes 26247168 | tf_op jit(solution)/shard_map/rhqk,rqhd->rkd/dot_general | solution.py:222
  288.9 11.5 %fusion.60 = bf16[64,12,512]{2,0,1:T(8,128)(2,1)} fusion(f32[12,512]{1,0:T(8,128)S(1)} %fusion.3, f32[1,12,512,1024]{2,3,1,0:T(8,128)} %copy-done, f32[12,512]{1,0:T(8,128)S(1)} %copy-done.38, bf16[1,1024,128]{1,2,0:T(8,128)(2,1)S(1)} %copy-done.22), kind=kOutput, calls=%fused_computation.98 | convolution fusion | flops 824573952 | bytes 26148864 | tf_op jit(solution)/shard_map/rhqk,rkd->rqhd/dot_general | solution.py:153
  300.5 7.0 fusion.57
  308.5 2.8 fusion.53
  311.5 4.0 multiply_bitcast_fusion.1
  315.6 6.9 multiply_bitcast_fusion
  324.8 2.9 fusion.118
  327.9 35.7 %multiply_convert_fusion = (bf16[1024,3072]{1,0:T(8,128)(2,1)}, f32[1024,3072]{1,0:T(8,128)}, f32[1024,3072]{1,0:T(8,128)}) fusion(bf16[768,3072]{1,0:T(8,128)(2,1)} %all-gather.11.cloned.1.call-done, bf16[1024,768]{1,0:T(8,128)(2,1)S(1)} %copy-done.5, f32[768]{0:T(1024)S(1)} %copy-done.59, f32[768]{0:T(1024)S(1)} %copy-done.58, f32[1024]{0:T(1024)S(1)} %copy-done.48, ...), kind=kOutput, calls=%fused_computation.27 | convolution fusion | flops 5041029120 | bytes 37763072 | tf_op jit(solution)/shard_map/dot_general | solution.py:159
  363.6 15.7 %add_convert_fusion = bf16[1024,3072]{1,0:T(8,128)(2,1)} fusion(f32[1024,3072]{1,0:T(8,128)} %get-tuple-element.87, f32[1024,3072]{1,0:T(8,128)} %get-tuple-element.103, bf16[3072,768]{1,0:T(8,128)(2,1)} %all-gather.13.cloned.1.call-done, bf16[1024,768]{1,0:T(8,128)(2,1)S(1)} %copy-done.15, f32[]{:T(128)S(6)} %mul.464), kind=kOutput, calls=%fused_computation.24 | convolution fusion | flops 4878237696 | bytes 37748740 | tf_op jit(solution)/shard_map/nd,fd->nf/dot_general | solution.py:178
  379.2 10.7 %fusion.103 = f32[768,3072]{1,0:T(8,128)} fusion(bf16[1024,3072]{1,0:T(8,128)(2,1)} %add_convert_fusion, bf16[1024,768]{1,0:T(8,128)(2,1)S(1)} %copy-done.5, f32[768]{0:T(1024)S(1)} %copy-done.59, f32[768]{0:T(1024)S(1)} %copy-done.58, f32[1024]{0:T(1024)S(1)} %copy-done.48, f32[1024]{0:T(1024)S(1)} %copy-done.46), kind=kOutput, calls=%fused_computation.172 | convolution fusion | flops 4836556800 | bytes 17315840 | tf_op jit(solution)/shard_map/nd,nf->df/dot_general | solution.py:181
  390.2 10.3 %fusion.80 = f32[3072,768]{1,0:T(8,128)} fusion(bf16[1024,3072]{1,0:T(8,128)(2,1)} %get-tuple-element.86, bf16[1024,768]{1,0:T(8,128)(2,1)S(1)} %copy-done.15, f32[]{:T(128)S(6)} %mul.464), kind=kOutput, calls=%fused_computation.112 | convolution fusion | flops 4834197504 | bytes 17301508 | tf_op jit(solution)/shard_map/nf,nd->fd/dot_general | solution.py:177
  400.5 2.8 pad_maximum_fusion.2
  403.3 1.5 fusion.116
  404.9 8.7 fusion.117
  413.7 3.7 fusion.107
  417.5 40.3 %all-reduce.5 = (f32[2,768]{1,0:T(2,128)S(1)}, f32[2,768]{1,0:T(2,128)S(1)}) all-reduce(f32[2,768]{1,0:T(2,128)S(1)} %pad_maximum_fusion.6, f32[2,768]{1,0:T(2,128)S(1)} %pad_maximum_fusion.7), channel_id=7, replica_groups=mesh['dp'=8,'fsdp'=4] {'dp','fsdp'}, use_global_device_ids=true, to_apply=%region_20.21.clone | all-reduce | flops 3072 | bytes 24576
  458.4 3.6 fusion.46
  462.0 8.7 fusion.115
  470.7 2.6 fusion.50
  473.3 25.4 %reduce-scatter.12.cloned.1.call-done = f32[24,768]{1,0:T(8,128)} async-done(((f32[768,768]{1,0:T(8,128)}), f32[24,768]{1,0:T(8,128)}) %reduce-scatter.12.cloned.1.call-update) | async-done | bytes 73744 | tf_op jit(solution)/shard_map/reduce_scatter | solution.py:71
  498.8 103.9 %reduce-scatter.10.cloned.1.call-done = f32[24,768]{1,0:T(8,128)} async-done(((f32[768,768]{1,0:T(8,128)}), f32[24,768]{1,0:T(8,128)}) %reduce-scatter.10.cloned.1.call-update) | async-done | bytes 73744 | tf_op jit(solution)/shard_map/reduce_scatter | solution.py:69
  602.7 141.9 %reduce-scatter.14.cloned.1.call-done = f32[24,3072]{1,0:T(8,128)} async-done(((f32[768,3072]{1,0:T(8,128)}), f32[24,3072]{1,0:T(8,128)}) %reduce-scatter.14.cloned.1.call-update) | async-done | bytes 294928 | tf_op jit(solution)/shard_map/reduce_scatter | solution.py:72
  744.5 141.1 %reduce-scatter.16.cloned.1.call-done = f32[96,768]{1,0:T(8,128)} async-done(((f32[3072,768]{1,0:T(8,128)}), f32[96,768]{1,0:T(8,128)}) %reduce-scatter.16.cloned.1.call-update) | async-done | bytes 294928 | tf_op jit(solution)/shard_map/reduce_scatter | solution.py:73
  (199 shorter events, 17.3 us)
Async XLA Ops:
  7.2 9.9 %copy-start.4 = (bf16[1024,768]{1,0:T(8,128)(2,1)S(1)}, bf16[1024,768]{1,0:T(8,128)(2,1)}, u32[]{:S(2)}) copy-start(bf16[1024,768]{1,0:T(8,128)(2,1)} %param.23) | copy-start | bytes 4718596
  7.2 10.6 %copy-start.55 = (f32[24,128]{1,0:T(8,128)S(1)}, f32[24,128]{1,0:T(8,128)}, u32[]{:S(2)}) copy-start(f32[24,128]{1,0:T(8,128)} %param.25) | copy-start | bytes 36868
  7.2 172.8 %all-gather.7.cloned.1.call-start = ((), (), s32[]{:S(2)}) async-start(), calls=%async_computation.5 | async-start | bytes 1216512 | tf_op jit(solution)/shard_map/all_gather | solution.py:57
  8.9 181.1 %all-gather.9.cloned.1.call-start = ((), (), s32[]{:S(2)}) async-start(), calls=%async_computation.6 | async-start | bytes 1216512 | tf_op jit(solution)/shard_map/all_gather | solution.py:59
  10.5 317.3 %all-gather.11.cloned.1.call-start = ((), (), s32[]{:S(2)}) async-start(), calls=%async_computation.7 | async-start | bytes 4866048 | tf_op jit(solution)/shard_map/all_gather | solution.py:60
  12.2 351.4 %all-gather.13.cloned.1.call-start = ((), (), s32[]{:S(2)}) async-start(), calls=%async_computation.8 | async-start | bytes 4866048 | tf_op jit(solution)/shard_map/all_gather | solution.py:61
  13.9 459.5 %reduce-scatter.18.cloned.1.call-start = ((), (), s32[]{:S(2)}) async-start(), calls=%async_computation.13 | async-start | bytes 405504
  13.9 116.5 %copy-start.56 = (f32[8]{0:T(128)}, f32[8]{0:T(128)S(1)}, u32[]{:S(2)}) copy-start(f32[8]{0:T(128)S(1)} %multiply_power_fusion) | copy-start | bytes 100
  17.1 113.2 %copy-start.45 = (f32[1024]{0:T(1024)}, f32[1024]{0:T(1024)S(1)}, u32[]{:S(2)}) copy-start(f32[1024]{0:T(1024)S(1)} %broadcast_multiply_fusion.2) | copy-start | bytes 12292
  17.8 112.6 %copy-start.47 = (f32[1024]{0:T(1024)}, f32[1024]{0:T(1024)S(1)}, u32[]{:S(2)}) copy-start(f32[1024]{0:T(1024)S(1)} %add_rsqrt_fusion) | copy-start | bytes 12292
  89.6 41.7 %copy-start.49 = (f32[768]{0:T(1024)}, f32[768]{0:T(1024)S(1)}, u32[]{:S(2)}) copy-start(f32[768]{0:T(1024)S(1)} %get-tuple-element.79) | copy-start | bytes 9220
  91.2 91.8 %copy-start.34 = (f32[1024,8]{0,1:T(8,128)}, f32[1024,8]{0,1:T(8,128)S(1)}, u32[]{:S(2)}) copy-start(f32[1024,8]{0,1:T(8,128)S(1)} %get-tuple-element.101) | copy-start | bytes 98308
  129.7 53.1 %copy-start.8 = (bf16[1024,768]{1,0:T(8,128)(2,1)}, bf16[1024,768]{1,0:T(8,128)(2,1)S(1)}, u32[]{:S(2)}) copy-start(bf16[1024,768]{1,0:T(8,128)(2,1)S(1)} %fusion.39) | copy-start | bytes 4718596
  129.7 47.7 %copy-start.62 = (f32[22]{0:T(128)S(1)}, f32[22]{0:T(128)}, u32[]{:S(2)}) copy-start(f32[22]{0:T(128)} %param.33) | copy-start | bytes 268
  130.4 62.8 %copy-start.20 = (bf16[1,1024,128]{1,2,0:T(8,128)(2,1)}, bf16[1,1024,128]{1,2,0:T(8,128)(2,1)S(1)}, u32[]{:S(2)}) copy-start(bf16[1,1024,128]{1,2,0:T(8,128)(2,1)S(1)} %get-tuple-element.106) | copy-start | bytes 786436
  130.6 52.6 %copy-start.28 = (bf16[1,1024,8]{1,2,0:T(8,128)(2,1)}, bf16[1,1024,8]{1,2,0:T(8,128)(2,1)S(1)}, u32[]{:S(2)}) copy-start(bf16[1,1024,8]{1,2,0:T(8,128)(2,1)S(1)} %get-tuple-element.97) | copy-start | bytes 49156
  130.6 52.6 %copy-start.30 = (bf16[1,1024,8]{1,2,0:T(8,128)(2,1)}, bf16[1,1024,8]{1,2,0:T(8,128)(2,1)S(1)}, u32[]{:S(2)}) copy-start(bf16[1,1024,8]{1,2,0:T(8,128)(2,1)S(1)} %get-tuple-element.98) | copy-start | bytes 49156
  189.9 15.0 %copy-start.18 = (f32[12,512]{1,0:T(8,128)}, f32[12,512]{1,0:T(8,128)S(1)}, u32[]{:S(2)}) copy-start(f32[12,512]{1,0:T(8,128)S(1)} %log_add_fusion.1) | copy-start | bytes 73732
  193.2 11.7 %copy-start.6 = (bf16[1024,768]{0,1:T(8,128)(2,1)}, bf16[1024,768]{0,1:T(8,128)(2,1)S(1)}, u32[]{:S(2)}) copy-start(bf16[1024,768]{0,1:T(8,128)(2,1)S(1)} %convolution_convert_fusion) | copy-start | bytes 4718596
  193.2 11.7 %slice-start = ((s8[12582912]{0:T(1024)(128)(4,1)}), s8[4194304]{0:T(1024)(128)(4,1)S(1)}, s32[]{:S(2)}) async-start(s8[12582912]{0:T(1024)(128)(4,1)} %bitcast.224), calls=%async_computation.14 | async-start | bytes 8388608
  193.2 11.7 %slice-start.1 = ((s8[12582912]{0:T(1024)(128)(4,1)}), s8[4194304]{0:T(1024)(128)(4,1)S(1)}, s32[]{:S(2)}) async-start(s8[12582912]{0:T(1024)(128)(4,1)} %bitcast.224), calls=%async_computation.15 | async-start | bytes 8388608
  193.2 13.2 %slice-start.2 = ((s8[12582912]{0:T(1024)(128)(4,1)}), s8[4194304]{0:T(1024)(128)(4,1)S(1)}, s32[]{:S(2)}) async-start(s8[12582912]{0:T(1024)(128)(4,1)} %bitcast.224), calls=%async_computation.16 | async-start | bytes 8388608
  221.5 8.6 copy-start
  221.5 8.6 copy-start.38
  221.5 8.6 copy-start.21
  248.2 17.2 %copy-start.27 = (f32[1,512,64]{1,2,0:T(8,128)S(1)}, f32[1,512,64]{1,2,0:T(8,128)}, u32[]{:S(2)}) copy-start(f32[1,512,64]{1,2,0:T(8,128)} %fusion.70) | copy-start | bytes 393220
  270.3 17.3 %copy-start.43 = (bf16[1,1024,48]{1,2,0:T(8,128)(2,1)}, bf16[1,1024,48]{1,2,0:T(8,128)(2,1)S(1)}, u32[]{:S(2)}) copy-start(bf16[1,1024,48]{1,2,0:T(8,128)(2,1)S(1)} %slice.281) | copy-start | bytes 294916
  270.5 17.1 %copy-start.51 = (bf16[1,1024,8]{1,2,0:T(8,128)(2,1)}, bf16[1,1024,8]{1,2,0:T(8,128)(2,1)S(1)}, u32[]{:S(2)}) copy-start(bf16[1,1024,8]{1,2,0:T(8,128)(2,1)S(1)} %get-tuple-element.99) | copy-start | bytes 49156
  270.5 17.1 %copy-start.53 = (bf16[1,1024,8]{1,2,0:T(8,128)(2,1)}, bf16[1,1024,8]{1,2,0:T(8,128)(2,1)S(1)}, u32[]{:S(2)}) copy-start(bf16[1,1024,8]{1,2,0:T(8,128)(2,1)S(1)} %get-tuple-element.100) | copy-start | bytes 49156
  277.1 10.4 %copy-start.9 = (bf16[1024,768]{1,0:T(8,128)(2,1)S(1)}, bf16[1024,768]{1,0:T(8,128)(2,1)}, u32[]{:S(2)}) copy-start(bf16[1024,768]{1,0:T(8,128)(2,1)} %copy-done.8) | copy-start | bytes 4718596
  277.1 11.8 %copy-start.22 = (bf16[1,1024,128]{1,2,0:T(8,128)(2,1)S(1)}, bf16[1,1024,128]{1,2,0:T(8,128)(2,1)}, u32[]{:S(2)}) copy-start(bf16[1,1024,128]{1,2,0:T(8,128)(2,1)} %copy-done.20) | copy-start | bytes 786436
  287.5 12.9 %copy-start.39 = (bf16[1,1024,64]{1,2,0:T(8,128)(2,1)}, bf16[1,1024,64]{1,2,0:T(8,128)(2,1)S(1)}, u32[]{:S(2)}) copy-start(bf16[1,1024,64]{1,2,0:T(8,128)(2,1)S(1)} %fusion.77) | copy-start | bytes 393220
  288.9 11.6 %copy-start.33 = (f32[12,512]{1,0:T(8,128)S(1)}, f32[12,512]{1,0:T(8,128)}, u32[]{:S(2)}) copy-start(f32[12,512]{1,0:T(8,128)} %copy-done.32) | copy-start | bytes 73732
  288.9 11.6 %copy-start.42 = (f32[12,512]{1,0:T(8,128)S(1)}, f32[12,512]{1,0:T(8,128)}, u32[]{:S(2)}) copy-start(f32[12,512]{1,0:T(8,128)} %copy-done.41) | copy-start | bytes 73732
  300.4 198.3 %reduce-scatter.12.cloned.1.call-start = ((), (), s32[]{:S(2)}) async-start(), calls=%async_computation.10 | async-start | bytes 2433024 | tf_op jit(solution)/shard_map/reduce_scatter | solution.py:71
  311.3 291.4 %reduce-scatter.10.cloned.1.call-start = ((), (), s32[]{:S(2)}) async-start(), calls=%async_computation.9 | async-start | bytes 2433024 | tf_op jit(solution)/shard_map/reduce_scatter | solution.py:69
  327.7 416.8 %reduce-scatter.14.cloned.1.call-start = ((), (), s32[]{:S(2)}) async-start(), calls=%async_computation.11 | async-start | bytes 9732096 | tf_op jit(solution)/shard_map/reduce_scatter | solution.py:72
  327.8 35.7 %copy-start.15 = (bf16[1024,768]{1,0:T(8,128)(2,1)S(1)}, bf16[1024,768]{1,0:T(8,128)(2,1)}, u32[]{:S(2)}) copy-start(bf16[1024,768]{1,0:T(8,128)(2,1)} %param.31) | copy-start | bytes 4718596
  389.9 495.7 %reduce-scatter.16.cloned.1.call-start = ((), (), s32[]{:S(2)}) async-start(), calls=%async_computation.12 | async-start | bytes 9732096 | tf_op jit(solution)/shard_map/reduce_scatter | solution.py:73
  404.8 8.8 copy-start.24
  404.8 8.8 copy-start.40
  404.8 8.8 copy-start.44
  404.8 8.8 copy-start.50
  404.9 8.8 copy-start.52
  404.9 8.8 copy-start.54
  413.6 44.8 %copy-start.16 = (bf16[1024,768]{1,0:T(8,128)(2,1)S(1)}, bf16[1024,768]{1,0:T(8,128)(2,1)}, u32[]{:S(2)}) copy-start(bf16[1024,768]{1,0:T(8,128)(2,1)} %param.31) | copy-start | bytes 4718596
  462.0 8.7 copy-start.13
  462.0 8.7 copy-start.60
  (27 other events, 94.0 us)
Sparse Core Ops, SparseCore 0:
  11.5 54.4 all-gather.6
  69.5 53.0 all-gather.8
  126.0 63.0 all-gather.10
  191.9 62.3 all-gather.12
  300.5 92.7 reduce-scatter.17
  399.9 98.8 reduce-scatter.11
  504.6 97.9 reduce-scatter.9
  610.1 134.3 reduce-scatter.13
  751.0 134.5 reduce-scatter.15
where the time goes:
time: 902 us; the launch traced here: 892 us
  waiting for transfers between devices  412 us (46%)
  matrix products  201 us (22%)
  blocking collectives  193 us (21%)
  other arithmetic  52.5 us (6%)
  between operations  17.2 us (2%)
  local copies, waits for them, and re-layouts  15.1 us (2%)
    reduce_scatter x1, waiting for transfers between devices, send_grads(): lax.psum_scatter(up_g, ('dp', 'fsdp'), scatter_dimension=0, tiled=True)  142 us
    reduce_scatter x1, waiting for transfers between devices, send_grads(): lax.psum_scatter(down_g, ('dp', 'fsdp'), scatter_dimension=0, tiled=True)  141 us
    reduce_scatter x1, waiting for transfers between devices, send_grads(): lax.psum_scatter(query_g, ('dp', 'fsdp'), scatter_dimension=0, tiled=True)  104 us
    psum x1, blocking collectives, body(): counts = lax.psum(jnp.sum(onehot, axis=0), ('dp', 'fsdp'))  44.2 us
    unnamed x1, blocking collectives  40.3 us
    all_gather x1, blocking collectives, fetch_weights(): lax.all_gather(pair_w, ('dp', 'fsdp'), axis=0, tiled=True)  37.9 us
    all_gather x1, blocking collectives, fetch_weights(): lax.all_gather(gain_rows, ('dp', 'fsdp'), axis=1, tiled=True)  37.2 us
    dot_general x1, matrix products, body(): up_pre = jnp.dot(second_in, up_w, preferred_element_type=f32)  35.7 us
  transfers between devices with their start and end apart: 9, of which 4 were waited for; matrix products, arithmetic and copies ran while one was open for 29% of the time, Pallas kernels for 0%

commit v1 on v0

--- a/solution.py
+++ b/solution.py
@@ -1,6 +1,10 @@
+import functools
+
 import jax
 import jax.numpy as jnp
 from jax import lax
+from jax.experimental import pallas as pl
+from jax.experimental.pallas import tpu as pltpu
 from jax.sharding import PartitionSpec as P
 
 D = 768
@@ -9,9 +13,374 @@
 ROT = 16
 SUBSETS = 22
 SEQ = 1024
+PACK = 1024
+MESH = pl.DeviceIdType.MESH
 
 
 eps_norm = 1e-05
+
+
+def place():
+    dp, fs = lax.axis_index("dp"), lax.axis_index("fsdp")
+    return dp // 2, dp % 2, fs // 2, fs % 2
+
+
+def device(z, x, y, c):
+    return (z * 2 + x, y * 2 + c)
+
+
+def partners():
+    z, x, y, c = place()
+    xa, ya = jnp.where(c == 0, 1 - x, x), jnp.where(c == 0, y, 1 - y)
+    xb, yb = jnp.where(c == 0, x, 1 - x), jnp.where(c == 0, 1 - y, y)
+    return xa, ya, xb, yb
+
+
+def greet(lines):
+    z, x, y, c = place()
+    barrier = pltpu.get_barrier_semaphore()
+    others = [device(lax.rem(z + d, lines), x, y, c) for d in range(1, lines)]
+    others += [device(z, 1 - x, y, c), device(z, x, 1 - y, c), device(z, x, y, 1 - c)]
+    for other in others:
+        pl.semaphore_signal(barrier, inc=1, device_id=other, device_id_type=MESH)
+    pl.semaphore_wait(barrier, len(others))
+
+
+def remote(src, dst, send, recv, where):
+    return pltpu.make_async_remote_copy(
+        src_ref=src, dst_ref=dst, send_sem=send, recv_sem=recv, device_id=where, device_id_type=MESH
+    )
+
+
+def layout(rows, rows_down):
+    blocks = [(1, 2 * rows, PACK), (1, 2 * rows, D), (1, 2 * rows, 4 * D), (2, rows_down, D)]
+    return blocks
+
+
+def pieces_of(blocks):
+    (_, r0, _), (_, r1, _), (_, r2, _), (_, r3, _) = blocks
+    return [
+        (0, 0, r0, 0, PACK // 2),
+        (1, 0, r1, 0, D // 2),
+        (2, 0, r2, 0, D),
+        (2, 0, r2, D, D),
+        (3, 0, r3 // 2, 0, D // 2),
+        (3, r3 // 2, r3 // 2, 0, D // 2),
+    ]
+
+
+def lanes(start, size):
+    return pl.ds(pl.multiple_of(start, 128), size)
+
+
+def part(piece, halves, ref, z, x, y, c):
+    t, r0, nr, c0, w = piece
+    return ref.at[z, x, y, :, pl.ds(r0, nr), lanes(c * halves[t] + c0, w)]
+
+
+def gather_kernel(lines, rows, blocks, *refs):
+    query, pair, small, out, up, down = refs[:6]
+    whole = refs[6:10]
+    packed, stages = refs[10], refs[11:15]
+    swap_send, swap_recv, send, recv = refs[15:19]
+    pieces = pieces_of(blocks)
+    halves = [b[2] // 2 for b in blocks]
+    z, x, y, c = place()
+    xa, ya, xb, yb = partners()
+    sibling = device(z, x, y, 1 - c)
+    packed[:, :D] = query[...]
+    packed[:, D : D + 2 * HD] = pair[...]
+    packed[:, D + 2 * HD :] = small[...]
+    greet(lines)
+    sources = [packed, out, up, down]
+
+    def stage_rows(t, core):
+        if blocks[t][0] == 2:
+            return stages[t].at[core]
+        return stages[t].at[0, pl.ds(pl.multiple_of(core * rows, 8), rows)]
+
+    swaps = []
+    for t in range(4):
+        swaps.append(
+            remote(
+                sources[t].at[:, lanes((1 - c) * halves[t], halves[t])],
+                stage_rows(t, c),
+                swap_send.at[t],
+                swap_recv.at[t],
+                sibling,
+            )
+        )
+        swaps[-1].start()
+    started = []
+    for t in range(4):
+        h = halves[t]
+        stage_rows(t, c)[...] = jnp.where(c == 0, sources[t][:, :h], sources[t][:, h:])
+        swaps[t].wait_recv()
+        whole[t][z, x, y, :, :, lanes(c * h, h)] = stages[t][...].astype(jnp.bfloat16)
+        for p, piece in enumerate(pieces):
+            if piece[0] != t:
+                continue
+            for d in range(1, lines):
+                block = part(piece, halves, whole[t], z, x, y, c)
+                copy = remote(
+                    block, block, send.at[p, d - 1], recv.at[p, d - 1], device(lax.rem(z + d, lines), x, y, c)
+                )
+                copy.start()
+                started.append(copy)
+
+    n = lines - 1
+
+    def share(p, k, sx, sy, half, where):
+        column = part(pieces[p], halves, whole[pieces[p][0]], slice(None), sx, sy, half)
+        return remote(column, column, send.at[p, k], recv.at[p, k], where)
+
+    def go(copy):
+        copy.start()
+        started.append(copy)
+
+    def first(p):
+        t = pieces[p][0]
+        for d in range(1, lines):
+            block = part(pieces[p], halves, whole[t], lax.rem(z + lines - d, lines), x, y, c)
+            remote(block, block, send.at[p, d - 1], recv.at[p, d - 1], sibling).wait_recv()
+        go(share(p, n, x, y, c, device(z, xa, ya, c)))
+        go(share(p, n + 1, x, y, c, device(z, xb, yb, c)))
+        go(share(p, n + 3, x, y, c, sibling))
+
+    def second(p):
+        share(p, n, xa, ya, c, sibling).wait_recv()
+        go(share(p, n + 2, xa, ya, c, device(z, xb, yb, c)))
+        go(share(p, n + 4, xa, ya, c, sibling))
+
+    def third(p):
+        share(p, n + 1, xb, yb, c, sibling).wait_recv()
+        go(share(p, n + 5, xb, yb, c, sibling))
+        share(p, n + 2, 1 - x, 1 - y, c, sibling).wait_recv()
+        go(share(p, n + 6, 1 - x, 1 - y, c, sibling))
+
+    def fourth(p):
+        for k, sx, sy in ((3, x, y), (4, xb, yb), (5, xa, ya), (6, 1 - x, 1 - y)):
+            share(p, n + k, sx, sy, 1 - c, sibling).wait_recv()
+
+    count = len(pieces)
+    for s in range(count + 3):
+        if s < count:
+            first(s)
+        if 0 <= s - 1 < count:
+            second(s - 1)
+        if 0 <= s - 2 < count:
+            third(s - 2)
+        if 0 <= s - 3 < count:
+            fourth(s - 3)
+    for copy in swaps + started:
+        copy.wait_send()
+
+
+def gather(lines, query, pair, small, out, up, down):
+    rows, rows_down = query.shape[0], down.shape[0]
+    blocks = layout(rows, rows_down)
+    count, kinds = len(pieces_of(blocks)), lines + 6
+    vmem = pl.BlockSpec(memory_space=pltpu.VMEM)
+    f32 = jnp.float32
+    scratch = [pltpu.VMEM((rows, PACK), f32)]
+    scratch += [pltpu.VMEM((g, r, k // 2), f32) for g, r, k in blocks]
+    scratch += [pltpu.SemaphoreType.DMA((4,))] * 2 + [pltpu.SemaphoreType.DMA((count, kinds))] * 2
+    got = pl.pallas_call(
+        functools.partial(gather_kernel, lines, rows, blocks),
+        out_shape=[jax.ShapeDtypeStruct((lines, 2, 2, g, r, k), jnp.bfloat16) for g, r, k in blocks],
+        in_specs=[vmem] * 6,
+        out_specs=[vmem] * 4,
+        scratch_shapes=scratch,
+        compiler_params=pltpu.CompilerParams(
+            collective_id=0, has_side_effects=True, vmem_limit_bytes=60 * 2**20
+        ),
+        name="gather",
+    )(query, pair, small, out, up, down)
+    return [a.reshape(-1, a.shape[-1]) for a in got]
+
+
+def scatter_kernel(lines, rows, blocks, *refs):
+    f32, bf16 = jnp.float32, jnp.bfloat16
+    grads, outs = refs[:4], refs[4:8]
+    near, to_b, from_b, to_a, from_a, to_z, from_z, total, last = (refs[8 + 4 * i : 12 + 4 * i] for i in range(9))
+    send, recv = refs[44:46]
+    pieces = pieces_of(blocks)
+    halves = [b[2] // 2 for b in blocks]
+    z, x, y, c = place()
+    xa, ya, xb, yb = partners()
+    sibling = device(z, x, y, 1 - c)
+    greet(lines)
+    started = []
+
+    def go(copy):
+        copy.start()
+        started.append(copy)
+
+    def cut(piece, ref, *lead):
+        t, r0, nr, c0, w = piece
+        return ref.at[(*lead, slice(None), pl.ds(r0, nr), pl.ds(c0, w))]
+
+    def near_copy(p):
+        t = pieces[p][0]
+        r0, nr, c0, w = pieces[p][1:]
+        return remote(
+            grads[t].at[:, :, :, :, pl.ds(r0, nr), lanes((1 - c) * halves[t] + c0, w)],
+            near[t].at[:, :, :, :, pl.ds(r0, nr), pl.ds(c0, w)],
+            send.at[p, 0],
+            recv.at[p, 0],
+            sibling,
+        )
+
+    def b_copy(p):
+        t = pieces[p][0]
+        return remote(
+            cut(pieces[p], to_b[t], slice(None), slice(None)),
+            cut(pieces[p], from_b[t], slice(None), slice(None)),
+            send.at[p, 1],
+            recv.at[p, 1],
+            device(z, xb, yb, c),
+        )
+
+    def a_copy(p):
+        t = pieces[p][0]
+        return remote(
+            cut(pieces[p], to_a[t], slice(None)),
+            cut(pieces[p], from_a[t], slice(None)),
+            send.at[p, 2],
+            recv.at[p, 2],
+            device(z, xa, ya, c),
+        )
+
+    def z_copy(p, d):
+        t = pieces[p][0]
+        other = lax.rem(z + d, lines)
+        return remote(
+            cut(pieces[p], to_z[t], other),
+            cut(pieces[p], from_z[t], d - 1),
+            send.at[p, 2 + d],
+            recv.at[p, 2 + d],
+            device(other, x, y, c),
+        )
+
+    def last_copy(p):
+        t, r0, nr, c0, w = pieces[p]
+        if blocks[t][0] == 2:
+            src = total[t].at[1 - c, pl.ds(r0, nr), pl.ds(c0, w)]
+            dst = last[t].at[pl.ds(r0, nr), pl.ds(c0, w)]
+        else:
+            src = total[t].at[0, pl.ds(pl.multiple_of((1 - c) * rows, 8), rows), pl.ds(c0, w)]
+            dst = last[t].at[:, pl.ds(c0, w)]
+        return remote(src, dst, send.at[p, 2 + lines], recv.at[p, 2 + lines], sibling)
+
+    def own(p, k, sx, sy):
+        t = pieces[p][0]
+        a = part(pieces[p], halves, grads[t], k, sx, sy, c)[...].astype(f32)
+        return a + cut(pieces[p], near[t], k, sx, sy)[...].astype(f32)
+
+    def first(p):
+        go(near_copy(p))
+
+    def second(p):
+        t = pieces[p][0]
+        near_copy(p).wait_recv()
+
+        @pl.loop(0, lines)
+        def _(k):
+            cut(pieces[p], to_b[t], 0, k)[...] = own(p, k, xb, yb).astype(bf16)
+            cut(pieces[p], to_b[t], 1, k)[...] = own(p, k, 1 - x, 1 - y).astype(bf16)
+
+        go(b_copy(p))
+
+    def third(p):
+        t = pieces[p][0]
+        b_copy(p).wait_recv()
+
+        @pl.loop(0, lines)
+        def _(k):
+            got = cut(pieces[p], from_b[t], 1, k)[...].astype(f32)
+            cut(pieces[p], to_a[t], k)[...] = (own(p, k, xa, ya) + got).astype(bf16)
+
+        go(a_copy(p))
+
+    def mine(p, k):
+        t = pieces[p][0]
+        got = cut(pieces[p], from_b[t], 0, k)[...].astype(f32) + cut(pieces[p], from_a[t], k)[...].astype(f32)
+        return own(p, k, x, y) + got
+
+    def fourth(p):
+        t = pieces[p][0]
+        a_copy(p).wait_recv()
+
+        @pl.loop(1, lines)
+        def _(d):
+            k = lax.rem(z + d, lines)
+            cut(pieces[p], to_z[t], k)[...] = mine(p, k).astype(bf16)
+
+        for d in range(1, lines):
+            go(z_copy(p, d))
+        cut(pieces[p], total[t])[...] = mine(p, z)
+
+    def fifth(p):
+        t = pieces[p][0]
+        for d in range(1, lines):
+            z_copy(p, d).wait_recv()
+        acc = cut(pieces[p], total[t])[...]
+        for d in range(1, lines):
+            acc = acc + cut(pieces[p], from_z[t], d - 1)[...].astype(f32)
+        cut(pieces[p], total[t])[...] = acc
+        go(last_copy(p))
+
+    def sixth(p):
+        t, r0, nr, c0, w = pieces[p]
+        last_copy(p).wait_recv()
+        if blocks[t][0] == 2:
+            kept = total[t].at[c, pl.ds(r0, nr), pl.ds(c0, w)]
+            got = last[t].at[pl.ds(r0, nr), pl.ds(c0, w)]
+            dst = outs[t].at[pl.ds(r0, nr)]
+        else:
+            kept = total[t].at[0, pl.ds(pl.multiple_of(c * rows, 8), rows), pl.ds(c0, w)]
+            got = last[t].at[:, pl.ds(c0, w)]
+            dst = outs[t]
+        kept, got = kept[...], got[...]
+        h = halves[t]
+        dst[:, c0 : c0 + w] = jnp.where(c == 0, kept, got)
+        dst[:, h + c0 : h + c0 + w] = jnp.where(c == 0, got, kept)
+
+    count = len(pieces)
+    stages = [first, second, third, fourth, fifth, sixth]
+    order = [count - 1 - i for i in range(count)]
+    for s in range(count + len(stages) - 1):
+        for k, stage in enumerate(stages):
+            if 0 <= s - k < count:
+                stage(order[s - k])
+    for copy in started:
+        copy.wait_send()
+
+
+def scatter(lines, rows, rows_down, grads):
+    blocks = layout(rows, rows_down)
+    grads = [a.reshape(lines, 2, 2, g, r, k) for a, (g, r, k) in zip(grads, blocks)]
+    count = len(pieces_of(blocks))
+    vmem = pl.BlockSpec(memory_space=pltpu.VMEM)
+    f32, bf16 = jnp.float32, jnp.bfloat16
+    own_rows = [r if g == 2 else rows for g, r, k in blocks]
+    scratch = []
+    for lead in ((lines, 2, 2), (2, lines), (2, lines), (lines,), (lines,), (lines,), (lines - 1,)):
+        scratch += [pltpu.VMEM((*lead, g, r, k // 2), bf16) for g, r, k in blocks]
+    scratch += [pltpu.VMEM((g, r, k // 2), f32) for g, r, k in blocks]
+    scratch += [pltpu.VMEM((o, k // 2), f32) for o, (g, r, k) in zip(own_rows, blocks)]
+    scratch += [pltpu.SemaphoreType.DMA((count, lines + 3))] * 2
+    return pl.pallas_call(
+        functools.partial(scatter_kernel, lines, rows, blocks),
+        out_shape=[jax.ShapeDtypeStruct((o, k), f32) for o, (g, r, k) in zip(own_rows, blocks)],
+        in_specs=[vmem] * 4,
+        out_specs=[vmem] * 4,
+        scratch_shapes=scratch,
+        compiler_params=pltpu.CompilerParams(
+            collective_id=1, has_side_effects=True, vmem_limit_bytes=60 * 2**20
+        ),
+        name="scatter",
+    )(*grads)
 
 
 def angles(length):
@@ -52,28 +421,23 @@
     return jax.nn.gelu(inputs, approximate=False)
 
 
-def fetch_weights(query_w, pair_w, out_w, up_w, down_w, gain_rows, bias_rows):
-    return (
-        lax.all_gather(query_w, ("dp", "fsdp"), axis=0, tiled=True),
-        lax.all_gather(pair_w, ("dp", "fsdp"), axis=0, tiled=True),
-        lax.all_gather(out_w, ("dp", "fsdp"), axis=0, tiled=True),
-        lax.all_gather(up_w, ("dp", "fsdp"), axis=0, tiled=True),
-        lax.all_gather(down_w, ("dp", "fsdp"), axis=0, tiled=True),
-        lax.all_gather(gain_rows, ("dp", "fsdp"), axis=1, tiled=True),
-        lax.all_gather(bias_rows, ("dp", "fsdp"), axis=1, tiled=True),
-    )
-
-
-def send_grads(query_g, pair_g, out_g, up_g, down_g, gain_g, bias_g):
-    return (
-        lax.psum_scatter(query_g, ("dp", "fsdp"), scatter_dimension=0, tiled=True),
-        lax.psum_scatter(pair_g, ("dp", "fsdp"), scatter_dimension=0, tiled=True),
-        lax.psum_scatter(out_g, ("dp", "fsdp"), scatter_dimension=0, tiled=True),
-        lax.psum_scatter(up_g, ("dp", "fsdp"), scatter_dimension=0, tiled=True),
-        lax.psum_scatter(down_g, ("dp", "fsdp"), scatter_dimension=0, tiled=True),
-        lax.psum_scatter(gain_g, ("dp", "fsdp"), scatter_dimension=1, tiled=True),
-        lax.psum_scatter(bias_g, ("dp", "fsdp"), scatter_dimension=1, tiled=True),
-    )
+def fetch_weights(query_w, pair_w, small_w, out_w, up_w, down_w):
+    lines, per_line = lax.axis_size("dp") // 2, lax.axis_size("fsdp")
+    if lines >= 2 and per_line == 4 and query_w.shape[0] % 8 == 0:
+        packed, out_w, up_w, down_w = gather(lines, query_w, pair_w, small_w, out_w, up_w, down_w)
+        return packed, out_w, up_w, down_w
+    packed = jnp.concatenate([query_w, pair_w, small_w], axis=1)
+    return tuple(
+        lax.all_gather(a.astype(jnp.bfloat16), ("dp", "fsdp"), axis=0, tiled=True)
+        for a in (packed, out_w, up_w, down_w)
+    )
+
+
+def send_grads(rows, rows_down, grads):
+    lines, per_line = lax.axis_size("dp") // 2, lax.axis_size("fsdp")
+    if lines >= 2 and per_line == 4 and rows % 8 == 0:
+        return scatter(lines, rows, rows_down, [g.astype(jnp.bfloat16) for g in grads])
+    return [lax.psum_scatter(g, ("dp", "fsdp"), scatter_dimension=0, tiled=True) for g in grads]
 
 
 def body(
@@ -94,27 +458,21 @@
     rows_here = subset_tags.shape[0]
     token_count = rows_here * SEQ
     onehot = (subset_tags[:, None] == jnp.arange(SUBSETS, dtype=jnp.int32)[None, :]).astype(f32)
-    counts = lax.psum(jnp.sum(onehot, axis=0), ("dp", "fsdp"))
-    masters = (
-        w_query.astype(bf16),
-        w_pair.astype(bf16),
-        w_attn_out.astype(bf16),
-        w_up.astype(bf16),
-        w_down.astype(bf16),
-        ln_gains.astype(bf16),
-        ln_biases.astype(bf16),
-    )
-    gathered = fetch_weights(
-        masters[0], masters[1], masters[2], masters[3], masters[4], masters[5], masters[6]
-    )
-    query_w, pair_w, out_w, up_w, down_w, gain_rows, bias_rows = gathered
+    first_row = (jnp.arange(w_query.shape[0]) == 0)[:, None]
+    own_counts = jnp.where(first_row, jnp.sum(onehot, axis=0)[None, :], 0.0)
+    small = jnp.concatenate([ln_gains.T, ln_biases.T, own_counts], axis=1)
+    small = jnp.pad(small, ((0, 0), (0, 128 - small.shape[1])))
+    packed, out_w, up_w, down_w = fetch_weights(w_query, w_pair, small, w_attn_out, w_up, w_down)
+    query_w, pair_w = packed[:, :D], packed[:, D : D + 2 * HD]
+    small = packed[:, D + 2 * HD :].astype(f32)
+    counts = jnp.sum(small[:, 4 : 4 + SUBSETS], axis=0)
+    gain_rows, bias_rows = small[:, 0:2].T, small[:, 2:4].T
     inputs = tokens.astype(f32)
     row_mean = jnp.mean(inputs, axis=-1, keepdims=True)
     centred = inputs - row_mean
     inv_std = lax.rsqrt(jnp.mean(centred * centred, axis=-1, keepdims=True) + eps_norm)
     normed = centred * inv_std
-    gain_f = gain_rows.astype(f32)
-    bias_f = bias_rows.astype(f32)
+    gain_f, bias_f = gain_rows, bias_rows
     first_in = (normed * gain_f[0] + bias_f[0]).astype(bf16)
     second_in = (normed * gain_f[1] + bias_f[1]).astype(bf16)
     cos_table, sin_table = angles(SEQ)
@@ -162,10 +520,6 @@
         hidden, down_w, preferred_element_type=f32
     )
     mixed = (inputs + branch).astype(bf16)
-    query_w, pair_w, out_w, up_w, down_w, gain_rows, bias_rows = fetch_weights(
-        masters[0], masters[1], masters[2], masters[3], masters[4], masters[5], masters[6]
-    )
-    gain_f = gain_rows.astype(f32)
     row_count = jnp.sum(onehot * counts[None, :], axis=1)
     row_weight = jnp.sum(onehot * subset_weights[None, :], axis=1)
     total_rows = rows_here * lax.axis_size("dp") * lax.axis_size("fsdp")
@@ -251,19 +605,22 @@
         - normed * jnp.mean(d_normed * normed, axis=-1, keepdims=True)
     )
     grad_tokens = (grad_out + d_inputs).astype(bf16)
-    shards = send_grads(
-        grad_query, grad_pair, grad_attn, grad_up, grad_down, grad_gains, grad_biases
-    )
+    small_g = jnp.pad(jnp.concatenate([grad_gains, grad_biases], axis=0).T, ((0, 0), (0, 124)))
+    packed_g = jnp.concatenate([grad_query, grad_pair, small_g], axis=1)
+    packed_g, out_g, up_g, down_g = send_grads(
+        w_query.shape[0], w_down.shape[0], [packed_g, grad_attn, grad_up, grad_down]
+    )
+    small_g = packed_g[:, D + 2 * HD : D + 2 * HD + 4].T
     return (
         mixed,
         grad_tokens,
-        shards[0],
-        shards[1],
-        shards[2],
-        shards[3],
-        shards[4],
-        shards[5],
-        shards[6],
+        packed_g[:, :D],
+        packed_g[:, D : D + 2 * HD],
+        out_g,
+        up_g,
+        down_g,
+        small_g[:2],
+        small_g[2:],
     )
 
 

time: 902 us -> 393 us (0.44)
  waiting for transfers between devices: 412 us -> 0 us
  blocking collectives: 193 us -> 0 us
  Pallas kernels: 0 us -> 148 us
  matrix products: 201 us -> 170 us
  between operations: 17.2 us -> 4.15 us
    reduce_scatter x4 -> x0, waiting for transfers between devices: 412 us -> none  [the longest x1 142 us: send_grads(): lax.psum_scatter(up_g, ('dp', 'fsdp'), scatter_dimension=0, tiled=True)]
    pallas_call x0 -> x2, Pallas kernels: none -> 148 us  [the longest x1 73.8 us: scatter(): pl.pallas_call(functools.partial(scatter_kernel, lines, rows, blocks), ou...]
    all_gather x3 -> x0, blocking collectives: 109 us -> none  [the longest x1 37.9 us: fetch_weights(): lax.all_gather(pair_w, ('dp', 'fsdp'), axis=0, tiled=True)]
    psum x1 -> x0, blocking collectives: 44.2 us -> none  [body(): counts = lax.psum(jnp.sum(onehot, axis=0), ('dp', 'fsdp'))]
    unnamed x1 -> x0, blocking collectives: 40.3 us -> none
    another operation x9 -> x5, other arithmetic: 25.1 us -> 25.1 us
  transfers between devices with their start and end apart: 9 -> 0, of which waited for: 4 -> 0; matrix products, arithmetic and copies ran while one was open for 29% -> 0% of each run, Pallas kernels for 0% -> 0%
where the time goes in v1:
time: 393 us; the launch traced here: 386 us
  matrix products  170 us (43%)
  Pallas kernels  148 us (38%)
  other arithmetic  43.6 us (11%)
  local copies, waits for them, and re-layouts  20.4 us (5%)
  between operations  4.15 us (1%)
    pallas_call x1, Pallas kernels, scatter(): pl.pallas_call(functools.partial(scatter_kernel, lines, rows, blocks), ou...  73.8 us
    pallas_call x1, Pallas kernels, gather(): pl.pallas_call(functools.partial(gather_kernel, lines, rows, blocks), out...  73.7 us
    dot_general x1, matrix products, body(): up_pre = jnp.dot(second_in, up_w, preferred_element_type=f32)  34.9 us
    another operation x5, other arithmetic  25.1 us
    dot_general x2, matrix products, body(): jnp.einsum('rqhd,rkd->rhqk', d_attended[:, block_start:block_stop], value...  21.5 us
    dot_general x1, matrix products, body(): jnp.einsum('nd,fd->nf', grad_branch, down_w, preferred_element_type=f32)  15.9 us
    dot_general x2, matrix products, body(): jnp.einsum('rhqk,rqhd->rkd', prob_rows.astype(bf16), d_attended[:, block_...  15 us
    dot_general x2, matrix products, body(): jnp.einsum('rhqk,rkd->rqhd', prob_rows, values[:, :block_stop], preferred...  13.8 us

profile of v1, /device:TPU:25, one launch (start us, length us, event | category | flops | bytes accessed | tf_op | source)
XLA Modules:
  0.0 385.5 jit_solution(13905139017486781146)
XLA Ops:
  1.4 1.8 convert_reduce_fusion
  3.2 2.0 fusion.49
  6.2 0.8 fusion.105
  7.1 1.2 iota_compare_fusion.1
  8.3 73.7 %gather.1 = (bf16[4,2,2,1,48,1024]{5,4,3,2,1,0:T(8,128)(2,1)}, bf16[4,2,2,1,48,768]{5,4,3,2,1,0:T(8,128)(2,1)}, bf16[4,2,2,1,48,3072]{5,4,3,2,1,0:T(8,128)(2,1)}, bf16[4,2,2,2,96,768]{5,4,3,2,1,0:T(8,128)(2,1)}) custom-call(f32[24,768]{1,0:T(8,128)} %refs_0_.1, f32[24,128]{1,0:T(8,128)} %refs_1_.1, f32[24,128]{1,0:T(8,128)} %select_maximum_fusion.1.refs_2_, ...), custom_call_target="tpu_custom_call" | custom-call | tf_op jit(solution)/shard_map/gather/pallas_call | solution.py:188
  82.0 0.9 slice.234
  85.9 2.6 fusion.124
  90.0 1.3 fusion.148
  91.3 1.8 copy.47
  93.2 3.3 convolution_convert_fusion.2
  96.5 1.8 fusion.81
  99.1 2.0 fusion.125
  101.1 1.8 fusion.21
  102.9 2.7 fusion.70
  105.6 3.2 fusion.54
  108.7 5.8 %fusion.10 = (f32[12,512]{1,0:T(8,128)S(1)}, f32[512,512,12]{1,0,2:T(8,128)}) fusion(f32[1,12,512,512]{2,3,1,0:T(8,128)S(1)} %get-tuple-element.145, f32[12,512]{1,0:T(8,128)S(1)} %log_add_fusion.1, bf16[1,1024,12,64]{1,3,2,0:T(8,128)(2,1)S(1)} %bitcast.234, bf16[1,1024,128]{1,2,0:T(8,128)(2,1)S(1)} %copy-done.26), kind=kOutput, calls=%fused_computation.19 | convolution fusion | flops 412084224 | bytes 26075136 | tf_op jit(solution)/shard_map/rqhd,rkd->rhqk/dot_general | solution.py:551
  114.6 7.3 %fusion.26 = bf16[12,512,512]{1,2,0:T(8,128)(2,1)S(1)} fusion(f32[512,512,12]{1,0,2:T(8,128)} %get-tuple-element.149, f32[1,12,512,512]{2,3,1,0:T(8,128)S(1)} %get-tuple-element.145, f32[12,512]{1,0:T(8,128)S(1)} %get-tuple-element.148, f32[12,512]{1,0:T(8,128)S(1)} %log_add_fusion.1), kind=kLoop, calls=%fused_computation.47 | loop fusion | flops 12582912 | bytes 31506432 | tf_op jit(solution)/shard_map/reshape.161
  121.9 2.7 fusion.69
  124.5 2.3 multiply_bitcast_fusion.1
  126.9 4.7 %fusion.123 = (f32[12,512]{1,0:T(8,128)S(1)}, f32[1,12,512,1024]{2,3,1,0:T(8,128)S(1)}) fusion(bf16[1,1024,12,64]{1,3,2,0:T(8,128)(2,1)S(1)} %pad_maximum_fusion, bf16[1024,48]{0,1:T(8,128)(2,1)} %slice_bitcast_fusion.21, bf16[1024,8]{0,1:T(8,128)(2,1)} %bitcast.249, bf16[1024,8]{0,1:T(8,128)(2,1)} %bitcast.247, pred[512,1024]{0,1:T(8,128)(4,1)S(1)} %copy-done.6), kind=kOutput, calls=%fused_computation.198 | convolution fusion | flops 824567808 | bytes 26632192 | tf_op jit(solution)/shard_map/rqhd,rkd->rhqk/dot_general | solution.py:489
  131.6 3.7 fusion.3
  135.3 4.6 %copy-done = f32[1,12,512,1024]{2,3,1,0:T(8,128)} copy-done((f32[1,12,512,1024]{2,3,1,0:T(8,128)}, f32[1,12,512,1024]{2,3,1,0:T(8,128)S(1)}, u32[]{:S(2)}) %copy-start) | copy-done | bytes 25165848
  140.0 12.3 %fusion.76 = bf16[1,1024,64]{1,2,0:T(8,128)(2,1)S(1)} fusion(f32[1,12,512,1024]{2,3,1,0:T(8,128)} %copy-done, f32[12,512]{1,0:T(8,128)S(1)} %log_add_fusion, bf16[1,1024,12,64]{1,3,2,0:T(8,128)(2,1)} %bitcast.235, f32[1,512,64]{1,2,0:T(8,128)S(1)} %copy-done.12), kind=kOutput, calls=%fused_computation.111 | convolution fusion | flops 818020352 | bytes 26238976 | tf_op jit(solution)/shard_map/rhqk,rqhd->rkd/dot_general | solution.py:576
  152.3 10.7 %fusion.58 = bf16[64,12,512]{2,0,1:T(8,128)(2,1)S(1)} fusion(f32[12,512]{1,0:T(8,128)S(1)} %fusion.3, f32[1,12,512,1024]{2,3,1,0:T(8,128)} %copy-done, f32[12,512]{1,0:T(8,128)S(1)} %get-tuple-element.140, bf16[1,1024,128]{1,2,0:T(8,128)(2,1)S(1)} %copy-done.27), kind=kOutput, calls=%fused_computation.97 | convolution fusion | flops 824573952 | bytes 26148864 | tf_op jit(solution)/shard_map/rhqk,rkd->rqhd/dot_general | solution.py:511
  163.0 2.4 convolution_convert_fusion.3
  165.5 15.7 %fusion = (f32[12,512]{1,0:T(8,128)S(1)}, f32[1024,512,12]{1,0,2:T(8,128)}) fusion(f32[1,12,512,1024]{2,3,1,0:T(8,128)} %copy-done, f32[12,512]{1,0:T(8,128)S(1)} %log_add_fusion, bf16[1,1024,12,64]{1,3,2,0:T(8,128)(2,1)S(1)} %bitcast.236, bf16[1,1024,128]{1,2,0:T(8,128)(2,1)S(1)} %copy-done.27), kind=kOutput, calls=%fused_computation.3 | convolution fusion | flops 824174592 | bytes 51306496 | tf_op jit(solution)/shard_map/rqhd,rkd->rhqk/dot_general | solution.py:551
  181.1 16.6 %fusion.9 = bf16[12,512,1024]{1,2,0:T(8,128)(2,1)S(1)} fusion(f32[1024,512,12]{1,0,2:T(8,128)} %get-tuple-element.147, f32[1,12,512,1024]{2,3,1,0:T(8,128)} %copy-done, f32[12,512]{1,0:T(8,128)S(1)} %get-tuple-element.146, f32[12,512]{1,0:T(8,128)S(1)} %log_add_fusion), kind=kLoop, calls=%fused_computation.15 | loop fusion | flops 25165824 | bytes 62963712 | tf_op jit(solution)/shard_map/reshape.169
  197.8 3.9 %fusion.67 = f32[1,1024,64]{1,2,0:T(8,128)S(1)} fusion(bf16[12,512,1024]{1,2,0:T(8,128)(2,1)S(1)} %fusion.9, bf16[1,1024,12,64]{1,3,2,0:T(8,128)(2,1)S(1)} %pad_maximum_fusion, f32[1,512,64]{1,2,0:T(8,128)S(1)} %copy-done.13), kind=kOutput, calls=%fused_computation.105 | convolution fusion | flops 805437440 | bytes 13762560 | tf_op jit(solution)/shard_map/rhqk,rqhd->rkd/dot_general | solution.py:567
  201.8 2.3 multiply_bitcast_fusion
  205.0 1.3 fusion.64
  206.7 2.4 fusion.57
  209.2 3.1 fusion.79
  212.3 34.9 %multiply_convert_fusion = (bf16[1024,3072]{1,0:T(8,128)(2,1)}, f32[1024,3072]{1,0:T(8,128)}, f32[1024,3072]{1,0:T(8,128)}) fusion(bf16[768,3072]{1,0:T(8,128)(2,1)S(1)} %bitcast.263, bf16[1024,768]{1,0:T(8,128)(2,1)S(1)} %copy-done.2, f32[768]{0:T(1024)S(1)} %copy-done.48, f32[768]{0:T(1024)S(1)} %copy-done.49, f32[1024]{0:T(1024)S(1)} %copy-done.34, ...), kind=kOutput, calls=%fused_computation.27 | convolution fusion | flops 5041029120 | bytes 37763072 | tf_op jit(solution)/shard_map/dot_general | solution.py:517
  247.3 15.9 %add_convert_fusion = bf16[1024,3072]{1,0:T(8,128)(2,1)} fusion(f32[1024,3072]{1,0:T(8,128)} %get-tuple-element.126, f32[1024,3072]{1,0:T(8,128)} %get-tuple-element.139, bf16[3072,768]{1,0:T(8,128)(2,1)} %bitcast.267, bf16[1024,768]{1,0:T(8,128)(2,1)S(1)} %copy-done.9, f32[]{:T(128)S(6)} %mul.464), kind=kOutput, calls=%fused_computation.24 | convolution fusion | flops 4878237696 | bytes 37748740 | tf_op jit(solution)/shard_map/nd,fd->nf/dot_general | solution.py:532
  263.2 8.7 %fusion.126 = f32[1024,768]{1,0:T(8,128)S(1)} fusion(bf16[1024,3072]{1,0:T(8,128)(2,1)} %get-tuple-element.125, bf16[3072,768]{1,0:T(8,128)(2,1)} %bitcast.268), kind=kOutput, calls=%fused_computation.203 | convolution fusion | flops 4831838208 | bytes 14155776 | tf_op jit(solution)/shard_map/dot_general | solution.py:519
  271.9 2.7 fusion.50
  274.6 7.2 %convolution_convert_fusion = bf16[3072,768]{1,0:T(8,128)(2,1)} fusion(bf16[1024,3072]{1,0:T(8,128)(2,1)S(1)} %copy-done.59, bf16[1024,768]{1,0:T(8,128)(2,1)S(1)} %copy-done.9, f32[]{:T(128)S(6)} %mul.464), kind=kOutput, calls=%fused_computation.51 | convolution fusion | flops 4836556800 | bytes 12582916 | tf_op jit(solution)/shard_map/nf,nd->fd/dot_general | solution.py:531
  282.0 5.1 %fusion.127 = f32[1024,768]{1,0:T(8,128)S(1)} fusion(bf16[1024,3072]{1,0:T(8,128)(2,1)S(1)} %bitcast.276, bf16[768,3072]{1,0:T(8,128)(2,1)S(1)} %bitcast.266), kind=kOutput, calls=%fused_computation.204 | convolution fusion | flops 4831838208 | bytes 14155776 | tf_op jit(solution)/shard_map/nf,df->nd/dot_general | solution.py:536
  287.1 2.5 fusion.120
  289.6 7.9 %convolution_convert_fusion.1 = bf16[768,3072]{1,0:T(8,128)(2,1)} fusion(bf16[1024,3072]{1,0:T(8,128)(2,1)S(1)} %bitcast.276, bf16[1024,768]{1,0:T(8,128)(2,1)S(1)} %copy-done.2, f32[768]{0:T(1024)S(1)} %copy-done.48, f32[768]{0:T(1024)S(1)} %copy-done.49, f32[1024]{0:T(1024)S(1)} %copy-done.34, f32[1024]{0:T(1024)S(1)} %copy-done.31), kind=kOutput, calls=%fused_computation.52 | convolution fusion | flops 4838916096 | bytes 12597248 | tf_op jit(solution)/shard_map/nd,nf->df/dot_general | solution.py:535
  297.6 2.2 fusion.46
  300.1 1.4 pad_maximum_fusion.2.refs_0_
  301.5 73.8 %scatter.1 = (f32[24,1024]{1,0:T(8,128)}, f32[24,768]{1,0:T(8,128)}, f32[24,3072]{1,0:T(8,128)}, f32[96,768]{1,0:T(8,128)}) custom-call(bf16[4,2,2,1,48,1024]{5,4,3,2,1,0:T(8,128)(2,1)} %pad_maximum_fusion.2.refs_0_, bf16[4,2,2,1,48,768]{5,4,3,2,1,0:T(8,128)(2,1)} %bitcast.245, bf16[4,2,2,1,48,3072]{5,4,3,2,1,0:T(8,128)(2,1)} %bitcast.238, ...), custom_call_target="tpu_custom_call" | custom-call | tf_op jit(solution)/shard_map/scatter/pallas_call | solution.py:373
  376.0 1.3 slice.230
  377.3 1.5 slice.229
  380.2 1.5 copy.71
  381.7 1.7 copy.72
  383.4 1.7 copy.73
  (178 shorter events, 8.6 us)
Async XLA Ops:
  0.6 4.8 %copy-start.51 = (f32[2,24]{1,0:T(2,128)S(1)}, f32[2,24]{1,0:T(2,128)}, u32[]{:S(2)}) copy-start(f32[2,24]{1,0:T(2,128)} %param.30) | copy-start | bytes 580
  0.7 4.7 %copy-start.50 = (f32[2,24]{1,0:T(2,128)S(1)}, f32[2,24]{1,0:T(2,128)}, u32[]{:S(2)}) copy-start(f32[2,24]{1,0:T(2,128)} %param.29) | copy-start | bytes 580
  1.3 87.1 %copy-start.46 = (f32[8]{0:T(128)}, f32[8]{0:T(128)S(1)}, u32[]{:S(2)}) copy-start(f32[8]{0:T(128)S(1)} %multiply_power_fusion) | copy-start | bytes 100
  1.4 81.9 %copy-start.52 = (f32[22]{0:T(128)S(1)}, f32[22]{0:T(128)}, u32[]{:S(2)}) copy-start(f32[22]{0:T(128)} %param.33) | copy-start | bytes 268
  1.4 84.5 %copy-start.1 = (bf16[1024,768]{1,0:T(8,128)(2,1)S(1)}, bf16[1024,768]{1,0:T(8,128)(2,1)}, u32[]{:S(2)}) copy-start(bf16[1024,768]{1,0:T(8,128)(2,1)} %param.23) | copy-start | bytes 4718596
  3.2 85.3 %copy-start.29 = (f32[1024]{0:T(1024)}, f32[1024]{0:T(1024)S(1)}, u32[]{:S(2)}) copy-start(f32[1024]{0:T(1024)S(1)} %broadcast_multiply_fusion.2) | copy-start | bytes 12292
  5.3 83.2 %copy-start.32 = (f32[1024]{0:T(1024)}, f32[1024]{0:T(1024)S(1)}, u32[]{:S(2)}) copy-start(f32[1024]{0:T(1024)S(1)} %add_rsqrt_fusion) | copy-start | bytes 12292
  7.0 91.3 %copy-start.14 = (f32[1024,8]{0,1:T(8,128)}, f32[1024,8]{0,1:T(8,128)S(1)}, u32[]{:S(2)}) copy-start(f32[1024,8]{0,1:T(8,128)S(1)} %get-tuple-element.137) | copy-start | bytes 98308
  85.9 4.1 %copy-start.37 = (f32[768]{0:T(1024)}, f32[768]{0:T(1024)S(1)}, u32[]{:S(2)}) copy-start(f32[768]{0:T(1024)S(1)} %get-tuple-element.153) | copy-start | bytes 9220
  85.9 4.1 %copy-start.40 = (f32[768]{0:T(1024)}, f32[768]{0:T(1024)S(1)}, u32[]{:S(2)}) copy-start(f32[768]{0:T(1024)S(1)} %get-tuple-element.119) | copy-start | bytes 9220
  89.3 9.5 %copy-start.18 = (bf16[1,1024,8]{1,2,0:T(8,128)(2,1)}, bf16[1,1024,8]{1,2,0:T(8,128)(2,1)S(1)}, u32[]{:S(2)}) copy-start(bf16[1,1024,8]{1,2,0:T(8,128)(2,1)S(1)} %get-tuple-element.129) | copy-start | bytes 49156
  93.2 3.3 copy-start.30
  93.2 3.3 copy-start.33
  93.2 3.3 copy-start.35
  93.2 3.4 copy-start.38
  93.2 3.4 copy-start.41
  96.5 12.3 %copy-start.4 = (bf16[1024,768]{0,1:T(8,128)(2,1)}, bf16[1024,768]{0,1:T(8,128)(2,1)S(1)}, u32[]{:S(2)}) copy-start(bf16[1024,768]{0,1:T(8,128)(2,1)S(1)} %convolution_convert_fusion.2) | copy-start | bytes 4718596
  131.6 8.4 %copy-start = (f32[1,12,512,1024]{2,3,1,0:T(8,128)}, f32[1,12,512,1024]{2,3,1,0:T(8,128)S(1)}, u32[]{:S(2)}) copy-start(f32[1,12,512,1024]{2,3,1,0:T(8,128)S(1)} %get-tuple-element.141) | copy-start | bytes 75497472
  131.6 8.4 %copy-start.12 = (f32[1,512,64]{1,2,0:T(8,128)S(1)}, f32[1,512,64]{1,2,0:T(8,128)}, u32[]{:S(2)}) copy-start(f32[1,512,64]{1,2,0:T(8,128)} %fusion.70) | copy-start | bytes 393220
  140.0 12.3 %copy-start.27 = (bf16[1,1024,128]{1,2,0:T(8,128)(2,1)S(1)}, bf16[1,1024,128]{1,2,0:T(8,128)(2,1)}, u32[]{:S(2)}) copy-start(bf16[1,1024,128]{1,2,0:T(8,128)(2,1)} %get-tuple-element.142) | copy-start | bytes 786436
  152.3 52.8 %copy-start.23 = (bf16[1,1024,64]{1,2,0:T(8,128)(2,1)}, bf16[1,1024,64]{1,2,0:T(8,128)(2,1)S(1)}, u32[]{:S(2)}) copy-start(bf16[1,1024,64]{1,2,0:T(8,128)(2,1)S(1)} %fusion.76) | copy-start | bytes 393220
  152.3 10.7 %copy-start.8 = (bf16[1024,768]{1,0:T(8,128)(2,1)S(1)}, bf16[1024,768]{1,0:T(8,128)(2,1)}, u32[]{:S(2)}) copy-start(bf16[1024,768]{1,0:T(8,128)(2,1)} %param.31) | copy-start | bytes 4718596
  152.3 10.7 %copy-start.54 = (bf16[64,12,512]{2,0,1:T(8,128)(2,1)S(1)}, bf16[64,12,512]{2,0,1:T(8,128)(2,1)}, u32[]{:S(2)}) copy-start(bf16[64,12,512]{2,0,1:T(8,128)(2,1)} %fusion.54) | copy-start | bytes 2359300
  181.1 16.7 %copy-start.13 = (f32[1,512,64]{1,2,0:T(8,128)S(1)}, f32[1,512,64]{1,2,0:T(8,128)}, u32[]{:S(2)}) copy-start(f32[1,512,64]{1,2,0:T(8,128)} %fusion.69) | copy-start | bytes 393220
  197.8 3.9 %copy-start.11 = (bf16[1024,48]{0,1:T(8,128)(2,1)S(1)}, bf16[1024,48]{0,1:T(8,128)(2,1)}, u32[]{:S(2)}) copy-start(bf16[1024,48]{0,1:T(8,128)(2,1)} %slice_bitcast_fusion.21) | copy-start | bytes 294916
  197.8 3.9 %copy-start.20 = (bf16[1,1024,8]{1,2,0:T(8,128)(2,1)S(1)}, bf16[1,1024,8]{1,2,0:T(8,128)(2,1)}, u32[]{:S(2)}) copy-start(bf16[1,1024,8]{1,2,0:T(8,128)(2,1)} %copy-done.18) | copy-start | bytes 49156
  197.8 3.9 %copy-start.22 = (bf16[1,1024,8]{1,2,0:T(8,128)(2,1)S(1)}, bf16[1,1024,8]{1,2,0:T(8,128)(2,1)}, u32[]{:S(2)}) copy-start(bf16[1,1024,8]{1,2,0:T(8,128)(2,1)} %get-tuple-element.130) | copy-start | bytes 49156
  201.8 3.3 copy-start.7
  206.7 5.6 %slice-start = ((s8[4718592]{0:T(1024)(128)(4,1)}), s8[4194304]{0:T(1024)(128)(4,1)S(1)}, s32[]{:S(2)}) async-start(s8[4718592]{0:T(1024)(128)(4,1)} %bitcast.261), calls=%async_computation | async-start | bytes 8388608
  209.2 3.1 copy-start.2
  209.2 3.1 copy-start.31
  209.2 3.1 copy-start.34
  209.2 3.1 copy-start.48
  212.3 35.0 %copy-start.9 = (bf16[1024,768]{1,0:T(8,128)(2,1)S(1)}, bf16[1024,768]{1,0:T(8,128)(2,1)}, u32[]{:S(2)}) copy-start(bf16[1024,768]{1,0:T(8,128)(2,1)} %param.31) | copy-start | bytes 4718596
  263.2 8.7 %copy-start.53 = (bf16[4,2,2,1,48,768]{5,4,3,2,1,0:T(8,128)(2,1)S(1)}, bf16[4,2,2,1,48,768]{5,4,3,2,1,0:T(8,128)(2,1)}, u32[]{:S(2)}) copy-start(bf16[4,2,2,1,48,768]{5,4,3,2,1,0:T(8,128)(2,1)} %get-tuple-element.82) | copy-start | bytes 3538948
  263.2 8.7 %copy-start.55 = (bf16[64,12,512]{2,0,1:T(8,128)(2,1)S(1)}, bf16[64,12,512]{2,0,1:T(8,128)(2,1)}, u32[]{:S(2)}) copy-start(bf16[64,12,512]{2,0,1:T(8,128)(2,1)} %fusion.54) | copy-start | bytes 2359300
  263.2 8.7 %copy-start.57 = (bf16[64,12,512]{2,0,1:T(8,128)(2,1)S(1)}, bf16[64,12,512]{2,0,1:T(8,128)(2,1)}, u32[]{:S(2)}) copy-start(bf16[64,12,512]{2,0,1:T(8,128)(2,1)} %copy-done.56) | copy-start | bytes 2359300
  263.2 11.4 %copy-start.59 = (bf16[1024,3072]{1,0:T(8,128)(2,1)S(1)}, bf16[1024,3072]{1,0:T(8,128)(2,1)}, u32[]{:S(2)}) copy-start(bf16[1024,3072]{1,0:T(8,128)(2,1)} %get-tuple-element.125) | copy-start | bytes 18874372
  271.9 10.0 %slice-start.2 = ((s8[4718592]{0:T(1024)(128)(4,1)}), s8[4194304]{0:T(1024)(128)(4,1)S(1)}, s32[]{:S(2)}) async-start(s8[4718592]{0:T(1024)(128)(4,1)} %bitcast.264), calls=%async_computation.2 | async-start | bytes 8388608
  271.9 10.0 %slice-start.4 = ((s8[6291456]{0:T(1024)(128)(4,1)}), s8[4194304]{0:T(1024)(128)(4,1)S(1)}, s32[]{:S(2)}) async-start(s8[6291456]{0:T(1024)(128)(4,1)} %bitcast.275), calls=%async_computation.4 | async-start | bytes 8388608
  274.6 7.3 %slice-start.3 = ((s8[4718592]{0:T(1024)(128)(4,1)}), s8[524288]{0:T(1024)(128)(4,1)S(1)}, s32[]{:S(2)}) async-start(s8[4718592]{0:T(1024)(128)(4,1)} %bitcast.264), calls=%async_computation.3 | async-start | bytes 1048576
  274.6 7.3 %slice-start.5 = ((s8[6291456]{0:T(1024)(128)(4,1)}), s8[2097152]{0:T(1024)(128)(4,1)S(1)}, s32[]{:S(2)}) async-start(s8[6291456]{0:T(1024)(128)(4,1)} %bitcast.275), calls=%async_computation.5 | async-start | bytes 4194304
  281.9 5.1 %copy-start.24 = (bf16[1,1024,64]{1,2,0:T(8,128)(2,1)S(1)}, bf16[1,1024,64]{1,2,0:T(8,128)(2,1)}, u32[]{:S(2)}) copy-start(bf16[1,1024,64]{1,2,0:T(8,128)(2,1)} %copy-done.23) | copy-start | bytes 393220
  281.9 5.1 %copy-start.28 = (bf16[1,1024,48]{1,2,0:T(8,128)(2,1)S(1)}, bf16[1,1024,48]{1,2,0:T(8,128)(2,1)}, u32[]{:S(2)}) copy-start(bf16[1,1024,48]{1,2,0:T(8,128)(2,1)} %slice.311) | copy-start | bytes 294916
  281.9 5.1 %copy-start.39 = (f32[768]{0:T(1024)S(1)}, f32[768]{0:T(1024)}, u32[]{:S(2)}) copy-start(f32[768]{0:T(1024)} %copy-done.37) | copy-start | bytes 9220
  281.9 5.1 %copy-start.43 = (bf16[1,1024,8]{1,2,0:T(8,128)(2,1)S(1)}, bf16[1,1024,8]{1,2,0:T(8,128)(2,1)}, u32[]{:S(2)}) copy-start(bf16[1,1024,8]{1,2,0:T(8,128)(2,1)} %copy-done.42) | copy-start | bytes 49156
  281.9 5.1 %copy-start.45 = (bf16[1,1024,8]{1,2,0:T(8,128)(2,1)S(1)}, bf16[1,1024,8]{1,2,0:T(8,128)(2,1)}, u32[]{:S(2)}) copy-start(bf16[1,1024,8]{1,2,0:T(8,128)(2,1)} %copy-done.44) | copy-start | bytes 49156
  282.0 5.1 %copy-start.58 = (f32[1024,768]{1,0:T(8,128)S(1)}, f32[1024,768]{1,0:T(8,128)}, u32[]{:S(2)}) copy-start(f32[1024,768]{1,0:T(8,128)} %fusion.79) | copy-start | bytes 9437188
  (18 other events, 40.5 us)

commit v2 on v1

--- a/solution.py
+++ b/solution.py
@@ -14,6 +14,8 @@
 SUBSETS = 22
 SEQ = 1024
 PACK = 1024
+TILE = 256
+LOG2E = 1.4426950408889634
 MESH = pl.DeviceIdType.MESH
 
 
@@ -59,14 +61,14 @@
 
 def pieces_of(blocks):
     (_, r0, _), (_, r1, _), (_, r2, _), (_, r3, _) = blocks
-    return [
-        (0, 0, r0, 0, PACK // 2),
-        (1, 0, r1, 0, D // 2),
-        (2, 0, r2, 0, D),
-        (2, 0, r2, D, D),
-        (3, 0, r3 // 2, 0, D // 2),
-        (3, r3 // 2, r3 // 2, 0, D // 2),
-    ]
+    up, third = D // 2, r3 // 3 // 16 * 16
+    downs = [(0, third), (third, third), (2 * third, r3 - 2 * third)]
+    return (
+        [(0, 0, r0, 0, PACK // 2)]
+        + [(2, 0, r2, k * up, up) for k in range(4)]
+        + [(1, 0, r1, 0, D // 2)]
+        + [(3, r, n, 0, D // 2) for r, n in downs]
+    )
 
 
 def lanes(start, size):
@@ -78,125 +80,309 @@
     return ref.at[z, x, y, :, pl.ds(r0, nr), lanes(c * halves[t] + c0, w)]
 
 
-def gather_kernel(lines, rows, blocks, *refs):
-    query, pair, small, out, up, down = refs[:6]
-    whole = refs[6:10]
-    packed, stages = refs[10], refs[11:15]
-    swap_send, swap_recv, send, recv = refs[15:19]
-    pieces = pieces_of(blocks)
-    halves = [b[2] // 2 for b in blocks]
-    z, x, y, c = place()
-    xa, ya, xb, yb = partners()
-    sibling = device(z, x, y, 1 - c)
-    packed[:, :D] = query[...]
-    packed[:, D : D + 2 * HD] = pair[...]
-    packed[:, D + 2 * HD :] = small[...]
-    greet(lines)
-    sources = [packed, out, up, down]
-
-    def stage_rows(t, core):
-        if blocks[t][0] == 2:
-            return stages[t].at[core]
-        return stages[t].at[0, pl.ds(pl.multiple_of(core * rows, 8), rows)]
-
-    swaps = []
-    for t in range(4):
-        swaps.append(
-            remote(
-                sources[t].at[:, lanes((1 - c) * halves[t], halves[t])],
-                stage_rows(t, c),
-                swap_send.at[t],
-                swap_recv.at[t],
-                sibling,
-            )
-        )
-        swaps[-1].start()
-    started = []
-    for t in range(4):
-        h = halves[t]
-        stage_rows(t, c)[...] = jnp.where(c == 0, sources[t][:, :h], sources[t][:, h:])
-        swaps[t].wait_recv()
-        whole[t][z, x, y, :, :, lanes(c * h, h)] = stages[t][...].astype(jnp.bfloat16)
-        for p, piece in enumerate(pieces):
-            if piece[0] != t:
-                continue
-            for d in range(1, lines):
-                block = part(piece, halves, whole[t], z, x, y, c)
-                copy = remote(
-                    block, block, send.at[p, d - 1], recv.at[p, d - 1], device(lax.rem(z + d, lines), x, y, c)
-                )
-                copy.start()
-                started.append(copy)
-
-    n = lines - 1
-
-    def share(p, k, sx, sy, half, where):
-        column = part(pieces[p], halves, whole[pieces[p][0]], slice(None), sx, sy, half)
-        return remote(column, column, send.at[p, k], recv.at[p, k], where)
-
-    def go(copy):
-        copy.start()
-        started.append(copy)
-
-    def first(p):
-        t = pieces[p][0]
-        for d in range(1, lines):
-            block = part(pieces[p], halves, whole[t], lax.rem(z + lines - d, lines), x, y, c)
-            remote(block, block, send.at[p, d - 1], recv.at[p, d - 1], sibling).wait_recv()
-        go(share(p, n, x, y, c, device(z, xa, ya, c)))
-        go(share(p, n + 1, x, y, c, device(z, xb, yb, c)))
-        go(share(p, n + 3, x, y, c, sibling))
-
-    def second(p):
-        share(p, n, xa, ya, c, sibling).wait_recv()
-        go(share(p, n + 2, xa, ya, c, device(z, xb, yb, c)))
-        go(share(p, n + 4, xa, ya, c, sibling))
-
-    def third(p):
-        share(p, n + 1, xb, yb, c, sibling).wait_recv()
-        go(share(p, n + 5, xb, yb, c, sibling))
-        share(p, n + 2, 1 - x, 1 - y, c, sibling).wait_recv()
-        go(share(p, n + 6, 1 - x, 1 - y, c, sibling))
-
-    def fourth(p):
-        for k, sx, sy in ((3, x, y), (4, xb, yb), (5, xa, ya), (6, 1 - x, 1 - y)):
-            share(p, n + k, sx, sy, 1 - c, sibling).wait_recv()
-
-    count = len(pieces)
-    for s in range(count + 3):
-        if s < count:
-            first(s)
-        if 0 <= s - 1 < count:
-            second(s - 1)
-        if 0 <= s - 2 < count:
-            third(s - 2)
-        if 0 <= s - 3 < count:
-            fourth(s - 3)
-    for copy in swaps + started:
-        copy.wait_send()
-
-
-def gather(lines, query, pair, small, out, up, down):
-    rows, rows_down = query.shape[0], down.shape[0]
+class Gather:
+    def __init__(self, lines, rows, blocks, sources, stages, whole, sems):
+        self.lines, self.rows, self.blocks = lines, rows, blocks
+        self.sources, self.stages, self.whole = sources, stages, whole
+        self.swap_send, self.swap_recv, self.send, self.recv = sems
+        self.pieces = pieces_of(blocks)
+        self.halves = [b[2] // 2 for b in blocks]
+        self.z, self.x, self.y, self.c = place()
+        self.xa, self.ya, self.xb, self.yb = partners()
+        self.sibling = device(self.z, self.x, self.y, 1 - self.c)
+        self.started = []
+
+    def go(self, make):
+        make().start()
+        self.started.append(make)
+
+    def stage_rows(self, t, core):
+        if self.blocks[t][0] == 2:
+            return self.stages[t].at[core]
+        return self.stages[t].at[0, pl.ds(pl.multiple_of(core * self.rows, 8), self.rows)]
+
+    def swap(self, t):
+        h = self.halves[t]
+        return remote(
+            self.sources[t].at[:, lanes((1 - self.c) * h, h)],
+            self.stage_rows(t, self.c),
+            self.swap_send.at[t],
+            self.swap_recv.at[t],
+            self.sibling,
+        )
+
+    def direct(self, p, d, received=False):
+        z, n = self.z, self.lines
+        at = lax.rem(z + n - d, n) if received else z
+        block = part(self.pieces[p], self.halves, self.whole[self.pieces[p][0]], at, self.x, self.y, self.c)
+        where = device(lax.rem(z + d, n), self.x, self.y, self.c)
+        return remote(block, block, self.send.at[p, d - 1], self.recv.at[p, d - 1], where)
+
+    def share(self, p, k, sx, sy, half, where):
+        column = part(self.pieces[p], self.halves, self.whole[self.pieces[p][0]], slice(None), sx, sy, half)
+        k = k + self.lines - 1
+        return remote(column, column, self.send.at[p, k], self.recv.at[p, k], where)
+
+    def begin(self):
+        for t in (0, 2, 1, 3):
+            self.go(functools.partial(self.swap, t))
+        for t in (0, 2, 1, 3):
+            h = self.halves[t]
+            self.stage_rows(t, self.c)[...] = jnp.where(self.c == 0, self.sources[t][:, :h], self.sources[t][:, h:])
+            self.swap(t).wait_recv()
+            self.whole[t][self.z, self.x, self.y, :, :, lanes(self.c * h, h)] = self.stages[t][...].astype(jnp.bfloat16)
+            for p, piece in enumerate(self.pieces):
+                if piece[0] == t:
+                    for d in range(1, self.lines):
+                        self.go(functools.partial(self.direct, p, d))
+
+    def first(self, p):
+        for d in range(1, self.lines):
+            self.direct(p, d, received=True).wait_recv()
+        x, y, c, z = self.x, self.y, self.c, self.z
+        self.go(lambda: self.share(p, 0, x, y, c, device(z, self.xa, self.ya, c)))
+        self.go(lambda: self.share(p, 1, x, y, c, device(z, self.xb, self.yb, c)))
+        self.go(lambda: self.share(p, 3, x, y, c, self.sibling))
+
+    def second(self, p):
+        c, z = self.c, self.z
+        self.share(p, 0, self.xa, self.ya, c, self.sibling).wait_recv()
+        self.go(lambda: self.share(p, 2, self.xa, self.ya, c, device(z, self.xb, self.yb, c)))
+        self.go(lambda: self.share(p, 4, self.xa, self.ya, c, self.sibling))
+
+    def third(self, p):
+        x, y, c = self.x, self.y, self.c
+        self.share(p, 1, self.xb, self.yb, c, self.sibling).wait_recv()
+        self.go(lambda: self.share(p, 5, self.xb, self.yb, c, self.sibling))
+        self.share(p, 2, 1 - x, 1 - y, c, self.sibling).wait_recv()
+        self.go(lambda: self.share(p, 6, 1 - x, 1 - y, c, self.sibling))
+
+    def fourth(self, p):
+        x, y, c = self.x, self.y, 1 - self.c
+        for k, sx, sy in ((3, x, y), (4, self.xb, self.yb), (5, self.xa, self.ya), (6, 1 - x, 1 - y)):
+            self.share(p, k, sx, sy, c, self.sibling).wait_recv()
+
+    def events(self):
+        count, order = len(self.pieces), []
+        for s in range(count + 3):
+            for k, step in enumerate((self.first, self.second, self.third, self.fourth)):
+                if 0 <= s - k < count:
+                    order.append((functools.partial(step, s - k), (k, s - k)))
+        cut = order.index(next(o for o in order if o[1] == (3, 0))) + 1
+        return order[:cut], order[cut:]
+
+
+def spread(events, slots):
+    plan = [[] for _ in range(slots)]
+    for k, event in enumerate(events):
+        plan[k * slots // max(len(events), 1)].append(event)
+    return plan
+
+
+def run_at(index, values):
+    for value, events in values:
+        if events:
+
+            @pl.when(index == value)
+            def _(events=events):
+                for event in events:
+                    event()
+
+
+def columns(ref, start, size):
+    return ref[:, :, :, :, :, pl.ds(start, size)].reshape(-1, size)
+
+
+def turned(a, b):
+    return lax.dot_general(a, b, (((1,), (1,)), ((), ())), preferred_element_type=jnp.float32)
+
+
+def swapped(block, cosine, sine):
+    lane = lax.broadcasted_iota(jnp.int32, block.shape, 1)
+    other = jnp.where(lane % 16 < 8, pltpu.roll(block, 120, 1), pltpu.roll(block, 8, 1))
+    return block * cosine + other * sine
+
+
+def forward_kernel(lines, rows, blocks, linked, *refs):
+    f32, bf16 = jnp.float32, jnp.bfloat16
+    tokens, cosine, sine = refs[:3]
+    given = refs[3:9] if linked else refs[3:7]
+    refs = refs[9:] if linked else refs[7:]
+    results, refs = refs[: 9 + 4 * linked], refs[9 + 4 * linked :]
+    small, first_in, second_in, queries, kv, attended, logsums, hidden, slope, *rest = refs
+    normed, keys, values_t, mask, out_sems, *rest = rest
+    held = [small, first_in, second_in, queries, kv, attended, logsums, hidden, slope]
+    flushed = []
+
+    def flush(*which):
+        for k in which:
+            copy = pltpu.make_async_copy(held[k], results[k], out_sems.at[k])
+            copy.start()
+            flushed.append(copy)
+
+    if linked:
+        query, pair, extra, out, up, down = given
+        whole, packed, stages, sems = rest[:4], rest[4], rest[5:9], rest[9:13]
+        held += whole
+        packed[:, :D] = query[...]
+        packed[:, D : D + 2 * HD] = pair[...]
+        packed[:, D + 2 * HD :] = extra[...]
+        greet(lines)
+        gather = Gather(lines, rows, blocks, [packed, out, up, down], stages, whole, sems)
+        gather.begin()
+        urgent, later = gather.events()
+        cut = later.index(next(e for e in later if e[1] == (3, 4))) + 1
+        early, late = [e[0] for e in later[:cut]], [e[0] for e in later[cut:]]
+    else:
+        whole, early, late = given, [], []
+    packed_w, up_w = whole[0], whole[2]
+
+    row = lax.broadcasted_iota(jnp.int32, (TILE, TILE), 0)
+    column = lax.broadcasted_iota(jnp.int32, (TILE, TILE), 1)
+    mask[...] = jnp.where(row <= column, 0.0, -1e30)
+    tiles = SEQ // TILE
+
+    def tile(k):
+        return pl.ds(pl.multiple_of(k * TILE, TILE), TILE)
+
+    @pl.loop(0, tiles)
+    def _(k):
+        inputs = tokens[tile(k), :].astype(f32)
+        centred = inputs - jnp.mean(inputs, axis=-1, keepdims=True)
+        normed[tile(k), :] = centred * lax.rsqrt(jnp.mean(centred * centred, axis=-1, keepdims=True) + eps_norm)
+
+    if linked:
+        for event, _ in urgent:
+            event()
+    small[...] = columns(packed_w, D + 2 * HD, 128).astype(f32).T
+    plan = spread(early, 28)
+
+    @pl.loop(0, tiles)
+    def _(k):
+        norm = normed[tile(k), :]
+        a1 = (norm * small[0:1, :] + small[2:3, :]).astype(bf16)
+        first_in[tile(k), :] = a1
+        second_in[tile(k), :] = (norm * small[1:2, :] + small[3:4, :]).astype(bf16)
+        mixed = jnp.dot(a1, columns(packed_w, 0, D + 2 * HD), preferred_element_type=f32)
+        cos_t, sin_t = cosine[tile(k), :], sine[tile(k), :]
+        left = lax.broadcasted_iota(jnp.int32, (TILE, 2 * HD), 1) < HD
+        for p in range(H // 2):
+            turn = swapped(mixed[:, 2 * HD * p : 2 * HD * (p + 1)], cos_t, sin_t).astype(bf16).astype(f32)
+            turn = turn * (LOG2E / 8)
+            high = turn.astype(bf16).astype(f32)
+            low = turn - high
+            queries[2 * p, tile(k), :] = jnp.where(left, high, pltpu.roll(low, HD, 1)).astype(bf16)
+            queries[2 * p + 1, tile(k), :] = jnp.where(left, pltpu.roll(high, HD, 1), low).astype(bf16)
+        pair_t = mixed[:, D : D + 2 * HD]
+        pair_t = jnp.where(left, swapped(pair_t, cos_t, sin_t), pair_t).astype(bf16).astype(f32)
+        kv[tile(k), :] = pair_t.astype(bf16)
+        other = pltpu.roll(pair_t, HD, 1)
+        keys[tile(k), :] = jnp.where(left, pair_t, other).astype(bf16)
+        lane = lax.broadcasted_iota(jnp.int32, (TILE, 2 * HD), 1)
+        ones = jnp.where(lane == HD, 1.0, 0.0)
+        values_t[:, tile(k)] = jnp.where(left, other, ones).T.astype(bf16)
+        run_at(k, [(v, plan[v]) for v in range(tiles)])
+
+    flush(0, 1, 2, 3, 4)
+    plan = plan[tiles:]
+
+    @pl.loop(0, H // 2)
+    def _(pr):
+        for i in range(tiles):
+            count = TILE * (i + 1)
+            heads = []
+            for hh in range(2):
+                head = pr * 2 + hh
+                scores = turned(keys[0:count, :], queries[head, i * TILE : count, :])
+                last = scores[count - TILE :] + mask[...]
+                peak = jnp.max(last, axis=0, keepdims=True)
+                if i:
+                    peak = jnp.maximum(peak, jnp.max(scores[: count - TILE], axis=0, keepdims=True))
+                probs = jnp.exp2(last - peak).astype(bf16)
+                if i:
+                    probs = jnp.concatenate([jnp.exp2(scores[: count - TILE] - peak).astype(bf16), probs], axis=0)
+                got = jnp.dot(values_t[:, 0:count], probs, preferred_element_type=f32)
+                total = got[HD : HD + 1]
+                heads.append(got[:HD] * (1.0 / total))
+                logsums[head, :, i * TILE : count] = peak + jnp.log2(total)
+            both = jnp.concatenate(heads, axis=0).T
+            attended[i * TILE : count, lanes(pr * 2 * HD, 2 * HD)] = both.astype(bf16)
+            run_at(pr, [(v, plan[v * tiles + i]) for v in range(H // 2)])
+
+    flush(5, 6)
+    plan = spread(late, 4 * tiles)
+
+    @pl.loop(0, 4 * tiles)
+    def _(s):
+        chunk, k = s // tiles, s % tiles
+        pre = jnp.dot(second_in[tile(k), :], columns(up_w, pl.multiple_of(chunk * D, D), D), preferred_element_type=f32)
+        cdf = 0.5 + 0.5 * lax.erf(pre * 0.7071067811865476)
+        hidden[tile(k), lanes(chunk * D, D)] = (pre * cdf).astype(bf16)
+        density = jnp.exp2(pre * pre * (-0.5 * LOG2E)) * 0.3989422804014327
+        slope[tile(k), lanes(chunk * D, D)] = (cdf + pre * density).astype(bf16)
+        run_at(s, [(v, plan[v]) for v in range(4 * tiles)])
+
+    flush(7, 8)
+    if linked:
+        flush(9, 10, 11, 12)
+        for make in gather.started:
+            make().wait_send()
+    for copy in flushed:
+        copy.wait()
+
+
+def tables():
+    cos_t, sin_t = angles(SEQ)
+    rest = jnp.zeros((SEQ, HD - ROT), jnp.float32)
+    cosine = jnp.concatenate([cos_t, cos_t, rest + 1.0] * 2, axis=1)
+    sine = jnp.concatenate([-sin_t, sin_t, rest] * 2, axis=1)
+    return cosine, sine
+
+
+def forward(linked, lines, rows, rows_down, tokens, cosine, sine, weights):
     blocks = layout(rows, rows_down)
-    count, kinds = len(pieces_of(blocks)), lines + 6
-    vmem = pl.BlockSpec(memory_space=pltpu.VMEM)
-    f32 = jnp.float32
-    scratch = [pltpu.VMEM((rows, PACK), f32)]
-    scratch += [pltpu.VMEM((g, r, k // 2), f32) for g, r, k in blocks]
-    scratch += [pltpu.SemaphoreType.DMA((4,))] * 2 + [pltpu.SemaphoreType.DMA((count, kinds))] * 2
+    f32, bf16 = jnp.float32, jnp.bfloat16
+    shapes = [(lines, 2, 2, g, r, k) for g, r, k in blocks]
+    if not linked:
+        weights = [a.reshape(shape) for a, shape in zip(weights, shapes)]
+    held = [
+        ((128, D), f32),
+        ((SEQ, D), bf16),
+        ((SEQ, D), bf16),
+        ((H, SEQ, 2 * HD), bf16),
+        ((SEQ, 2 * HD), bf16),
+        ((SEQ, D), bf16),
+        ((H, 1, SEQ), f32),
+        ((SEQ, 4 * D), bf16),
+        ((SEQ, 4 * D), bf16),
+    ]
+    scratch = [pltpu.VMEM(shape, kind) for shape, kind in held]
+    scratch += [
+        pltpu.VMEM((SEQ, D), f32),
+        pltpu.VMEM((SEQ, 2 * HD), bf16),
+        pltpu.VMEM((2 * HD, SEQ), bf16),
+        pltpu.VMEM((TILE, TILE), f32),
+        pltpu.SemaphoreType.DMA((13,)),
+    ]
+    if linked:
+        held += [(shape, bf16) for shape in shapes]
+        scratch += [pltpu.VMEM(shape, bf16) for shape in shapes]
+        scratch += [pltpu.VMEM((rows, PACK), f32)]
+        scratch += [pltpu.VMEM((g, r, k // 2), f32) for g, r, k in blocks]
+        count, kinds = len(pieces_of(blocks)), lines + 6
+        scratch += [pltpu.SemaphoreType.DMA((4,))] * 2 + [pltpu.SemaphoreType.DMA((count, kinds))] * 2
     got = pl.pallas_call(
-        functools.partial(gather_kernel, lines, rows, blocks),
-        out_shape=[jax.ShapeDtypeStruct((lines, 2, 2, g, r, k), jnp.bfloat16) for g, r, k in blocks],
-        in_specs=[vmem] * 6,
-        out_specs=[vmem] * 4,
+        functools.partial(forward_kernel, lines, rows, blocks, linked),
+        out_shape=[jax.ShapeDtypeStruct(shape, kind) for shape, kind in held],
+        in_specs=[pl.BlockSpec(memory_space=pltpu.VMEM)] * (3 + len(weights)),
+        out_specs=[pl.BlockSpec(memory_space=pl.ANY)] * len(held),
         scratch_shapes=scratch,
         compiler_params=pltpu.CompilerParams(
-            collective_id=0, has_side_effects=True, vmem_limit_bytes=60 * 2**20
+            collective_id=0 if linked else None, has_side_effects=linked, vmem_limit_bytes=60 * 2**20
         ),
-        name="gather",
-    )(query, pair, small, out, up, down)
-    return [a.reshape(-1, a.shape[-1]) for a in got]
+        name="forward",
+    )(tokens, cosine, sine, *weights)
+    return got[:9], list(got[9:]) if linked else weights
 
 
 def scatter_kernel(lines, rows, blocks, *refs):
@@ -417,26 +603,21 @@
     )
 
 
-def gelu_exact(inputs):
-    return jax.nn.gelu(inputs, approximate=False)
+def is_linked(rows):
+    return lax.axis_size("dp") >= 4 and lax.axis_size("fsdp") == 4 and rows % 8 == 0
 
 
 def fetch_weights(query_w, pair_w, small_w, out_w, up_w, down_w):
-    lines, per_line = lax.axis_size("dp") // 2, lax.axis_size("fsdp")
-    if lines >= 2 and per_line == 4 and query_w.shape[0] % 8 == 0:
-        packed, out_w, up_w, down_w = gather(lines, query_w, pair_w, small_w, out_w, up_w, down_w)
-        return packed, out_w, up_w, down_w
     packed = jnp.concatenate([query_w, pair_w, small_w], axis=1)
-    return tuple(
+    return [
         lax.all_gather(a.astype(jnp.bfloat16), ("dp", "fsdp"), axis=0, tiled=True)
         for a in (packed, out_w, up_w, down_w)
-    )
+    ]
 
 
 def send_grads(rows, rows_down, grads):
-    lines, per_line = lax.axis_size("dp") // 2, lax.axis_size("fsdp")
-    if lines >= 2 and per_line == 4 and rows % 8 == 0:
-        return scatter(lines, rows, rows_down, [g.astype(jnp.bfloat16) for g in grads])
+    if is_linked(rows):
+        return scatter(lax.axis_size("dp") // 2, rows, rows_down, [g.astype(jnp.bfloat16) for g in grads])
     return [lax.psum_scatter(g, ("dp", "fsdp"), scatter_dimension=0, tiled=True) for g in grads]
 
 
@@ -462,27 +643,32 @@
     own_counts = jnp.where(first_row, jnp.sum(onehot, axis=0)[None, :], 0.0)
     small = jnp.concatenate([ln_gains.T, ln_biases.T, own_counts], axis=1)
     small = jnp.pad(small, ((0, 0), (0, 128 - small.shape[1])))
-    packed, out_w, up_w, down_w = fetch_weights(w_query, w_pair, small, w_attn_out, w_up, w_down)
+    cosine, sine = tables()
+    cos_table, sin_table = angles(SEQ)
+    linked = is_linked(w_query.shape[0])
+    shards = (w_query, w_pair, small, w_attn_out, w_up, w_down)
+    if linked:
+        lines, rows, rows_down = lax.axis_size("dp") // 2, w_query.shape[0], w_down.shape[0]
+    else:
+        lines, rows, rows_down = 4, D // 32, 4 * D // 32
+        shards = fetch_weights(*shards)
+    kept, whole = forward(linked, lines, rows, rows_down, tokens, cosine, sine, shards)
+    small, first_in, second_in, queries, kv, attended, logsums, hidden, slope = kept
+    packed, out_w, up_w, down_w = [a.reshape(-1, a.shape[-1]) for a in whole]
     query_w, pair_w = packed[:, :D], packed[:, D : D + 2 * HD]
-    small = packed[:, D + 2 * HD :].astype(f32)
-    counts = jnp.sum(small[:, 4 : 4 + SUBSETS], axis=0)
-    gain_rows, bias_rows = small[:, 0:2].T, small[:, 2:4].T
+    counts = jnp.sum(small[4 : 4 + SUBSETS], axis=1)
+    gain_f = small[0:2]
     inputs = tokens.astype(f32)
     row_mean = jnp.mean(inputs, axis=-1, keepdims=True)
     centred = inputs - row_mean
     inv_std = lax.rsqrt(jnp.mean(centred * centred, axis=-1, keepdims=True) + eps_norm)
     normed = centred * inv_std
-    gain_f, bias_f = gain_rows, bias_rows
-    first_in = (normed * gain_f[0] + bias_f[0]).astype(bf16)
-    second_in = (normed * gain_f[1] + bias_f[1]).astype(bf16)
-    cos_table, sin_table = angles(SEQ)
-    query = jnp.dot(first_in, query_w, preferred_element_type=f32).reshape(rows_here, SEQ, H, HD)
-    query = rotate(query, cos_table[:, None, :], sin_table[:, None, :]).astype(bf16)
-    paired = jnp.dot(first_in, pair_w, preferred_element_type=f32).reshape(rows_here, SEQ, 2 * HD)
-    key_rows = rotate(paired[..., :HD], cos_table, sin_table).astype(bf16)
-    values = paired[..., HD:].astype(bf16)
+    query = (queries[:, :, :HD].astype(f32) + queries[:, :, HD:].astype(f32)) * (8 / LOG2E)
+    query = query.astype(bf16).transpose(1, 0, 2)[None]
+    key_rows, values = kv[None, :, :HD], kv[None, :, HD:]
     block_len = min(512, SEQ)
     block_count = SEQ // block_len
+    logsums = logsums[:, 0, :] / LOG2E
 
     def block_scores(block_start, block_stop):
         scores = (
@@ -497,25 +683,6 @@
         causal = jnp.arange(block_stop)[None, :] <= (block_start + jnp.arange(block_len))[:, None]
         return jnp.where(causal[None, None], scores, -jnp.inf)
 
-    outputs = []
-    logsums = []
-    for block_number in range(block_count):
-        block_start = block_number * block_len
-        block_stop = block_start + block_len
-        scores = block_scores(block_start, block_stop)
-        row_peak = jnp.max(scores, axis=-1, keepdims=True)
-        weights_exp = jnp.exp(scores - row_peak)
-        row_total = jnp.sum(weights_exp, axis=-1, keepdims=True)
-        prob_rows = (weights_exp / row_total).astype(bf16)
-        outputs.append(
-            jnp.einsum(
-                "rhqk,rkd->rqhd", prob_rows, values[:, :block_stop], preferred_element_type=f32
-            )
-        )
-        logsums.append(row_peak + jnp.log(row_total))
-    attended = jnp.concatenate(outputs, axis=1).reshape(token_count, D).astype(bf16)
-    up_pre = jnp.dot(second_in, up_w, preferred_element_type=f32)
-    hidden = gelu_exact(up_pre).astype(bf16)
     branch = jnp.dot(attended, out_w, preferred_element_type=f32) + jnp.dot(
         hidden, down_w, preferred_element_type=f32
     )
@@ -530,8 +697,7 @@
     grad_branch = grad_out.astype(bf16)
     grad_down = jnp.einsum("nf,nd->fd", hidden, grad_branch, preferred_element_type=f32)
     d_hidden = jnp.einsum("nd,fd->nf", grad_branch, down_w, preferred_element_type=f32)
-    gelu_pull = jax.vjp(gelu_exact, up_pre)[1]
-    d_up = gelu_pull(d_hidden)[0].astype(bf16)
+    d_up = (d_hidden * slope.astype(f32)).astype(bf16)
     grad_up = jnp.einsum("nd,nf->df", second_in, d_up, preferred_element_type=f32)
     d_second = jnp.einsum("nf,df->nd", d_up, up_w, preferred_element_type=f32)
     grad_attn = jnp.einsum("nd,ne->de", attended, grad_branch, preferred_element_type=f32)
@@ -547,7 +713,7 @@
         block_start = block_number * block_len
         block_stop = block_start + block_len
         scores = block_scores(block_start, block_stop)
-        prob_rows = jnp.exp(scores - logsums[block_number])
+        prob_rows = jnp.exp(scores - logsums[None, :, block_start:block_stop, None])
         d_probs = jnp.einsum(
             "rqhd,rkd->rhqk",
             d_attended[:, block_start:block_stop],

time: 393 us -> 352 us (0.90)
  matrix products: 170 us -> 117 us
  Pallas kernels: 148 us -> 161 us
    dot_general x5 -> x0, matrix products: 53.2 us -> none  [the longest x1 34.9 us: body(): up_pre = jnp.dot(second_in, up_w, preferred_element_type=f32)]
    pallas_call x1, Pallas kernels: 73.7 us -> 88.5 us  [forward(): pl.pallas_call(functools.partial(forward_kernel, lines, rows, blocks, lin...]
    dot_general x1, matrix products: 15.9 us -> 8.99 us  [body(): jnp.einsum('nd,fd->nf', grad_branch, down_w, preferred_element_type=f32)]
    dot_general x2, matrix products: 6.67 us -> 13.5 us  [block_scores(): jnp.einsum('rqhd,rkd->rhqk', query[:, block_start:block_stop], key_rows[:...]
    dot_general x2, matrix products: 21.5 us -> 27.7 us  [body(): jnp.einsum('rqhd,rkd->rhqk', d_attended[:, block_start:block_stop], value...]
    reduce_sum x3 -> x1, other arithmetic: 5.64 us -> 1.01 us  [body(): counts = jnp.sum(small[4:4 + SUBSETS], axis=1)]
    unnamed x141 -> x87, local copies, waits for them, and re-layouts: 11.8 us -> 8.88 us
    another operation x5 -> x3, other arithmetic: 25.1 us -> 24.5 us
where the time goes in v2:
time: 352 us; the launch traced here: 346 us
  Pallas kernels  161 us (46%)
  matrix products  117 us (33%)
  other arithmetic  40.5 us (12%)
  local copies, waits for them, and re-layouts  23.6 us (7%)
  between operations  3.52 us (1%)
    pallas_call x1, Pallas kernels, forward(): pl.pallas_call(functools.partial(forward_kernel, lines, rows, blocks, lin...  88.5 us
    pallas_call x1, Pallas kernels, scatter(): pl.pallas_call(functools.partial(scatter_kernel, lines, rows, blocks), ou...  72.1 us
    dot_general x2, matrix products, body(): jnp.einsum('rqhd,rkd->rhqk', d_attended[:, block_start:block_stop], value...  27.7 us
    another operation x3, other arithmetic  24.5 us
    dot_general x2, matrix products, body(): jnp.einsum('rhqk,rqhd->rkd', prob_rows.astype(bf16), d_attended[:, block_...  15 us
    dot_general x2, matrix products, block_scores(): jnp.einsum('rqhd,rkd->rhqk', query[:, block_start:block_stop], key_rows[:...  13.5 us
    dot_general x1, matrix products, body(): jnp.einsum('nd,fd->nf', grad_branch, down_w, preferred_element_type=f32)  8.99 us
    unnamed x87, local copies, waits for them, and re-layouts  8.88 us

profile of v2, /device:TPU:25, one launch (start us, length us, event | category | flops | bytes accessed | tf_op | source)
XLA Modules:
  0.0 345.7 jit_solution(5134566213722362043)
XLA Ops:
  1.4 1.7 convert_reduce_fusion
  3.1 2.0 fusion.35
  6.6 0.8 iota_compare_fusion.2
  7.5 1.2 iota_compare_fusion.1
  8.6 2.0 fusion.74
  10.6 1.9 concatenate.67.refs_2_
  12.6 0.8 copy.86
  13.4 1.7 concatenate.66.refs_1_
  15.2 0.8 copy.85
  15.9 88.5 %forward.1 = (f32[128,768]{1,0:T(8,128)}, bf16[1024,768]{1,0:T(8,128)(2,1)}, bf16[1024,768]{1,0:T(8,128)(2,1)}, bf16[12,1024,128]{2,1,0:T(8,128)(2,1)}, bf16[102...) custom-call(bf16[1024,768]{1,0:T(8,128)(2,1)} %refs_0_.1, ...), custom_call_target="tpu_custom_call" | custom-call | tf_op jit(solution)/shard_map/forward/pallas_call | solution.py:374
  104.4 1.0 slice_reduce_fusion
  105.4 1.4 slice_reduce_fusion.2
  108.8 9.0 %multiply_convert_fusion = bf16[1024,3072]{1,0:T(8,128)(2,1)S(1)} fusion(bf16[1024,3072]{1,0:T(8,128)(2,1)} %get-tuple-element.99, bf16[3072,768]{1,0:T(8,128)(2,1)} %bitcast.279, bf16[1024,768]{1,0:T(8,128)(2,1)S(1)} %copy-done.10, f32[]{:T(128)S(6)} %mul.366), kind=kOutput, calls=%fused_computation.19 | convolution fusion | flops 4843634688 | bytes 18874372 | tf_op jit(solution)/shard_map/nd,fd->nf/dot_general | solution.py:699
  117.8 5.0 %fusion.108 = f32[1024,768]{1,0:T(8,128)S(1)} fusion(bf16[1024,3072]{1,0:T(8,128)(2,1)S(1)} %copy-done.29, bf16[3072,768]{1,0:T(8,128)(2,1)S(1)} %bitcast.280), kind=kOutput, calls=%fused_computation.162 | convolution fusion | flops 4831838208 | bytes 14155776 | tf_op jit(solution)/shard_map/dot_general | solution.py:686
  122.9 7.0 %convolution_convert_fusion = bf16[3072,768]{1,0:T(8,128)(2,1)} fusion(bf16[1024,3072]{1,0:T(8,128)(2,1)S(1)} %copy-done.29, bf16[1024,768]{1,0:T(8,128)(2,1)S(1)} %copy-done.10, f32[]{:T(128)S(6)} %mul.366), kind=kOutput, calls=%fused_computation.28 | convolution fusion | flops 4836556800 | bytes 12582916 | tf_op jit(solution)/shard_map/nf,nd->fd/dot_general | solution.py:698
  129.9 2.6 fusion.36
  132.5 6.7 %fusion.109 = f32[1024,768]{1,0:T(8,128)} fusion(bf16[1024,3072]{1,0:T(8,128)(2,1)S(1)} %multiply_convert_fusion, bf16[768,3072]{1,0:T(8,128)(2,1)S(1)} %bitcast.278), kind=kOutput, calls=%fused_computation.163 | convolution fusion | flops 4831838208 | bytes 14155776 | tf_op jit(solution)/shard_map/nf,df->nd/dot_general | solution.py:702
  139.2 7.3 %convolution_convert_fusion.1 = bf16[768,3072]{1,0:T(8,128)(2,1)} fusion(bf16[1024,768]{1,0:T(8,128)(2,1)S(1)} %copy-done.33, bf16[1024,3072]{1,0:T(8,128)(2,1)S(1)} %multiply_convert_fusion), kind=kOutput, calls=%fused_computation.29 | convolution fusion | flops 4834197504 | bytes 12582912 | tf_op jit(solution)/shard_map/nd,nf->df/dot_general | solution.py:701
  146.5 2.5 convolution_convert_fusion.3
  149.7 2.6 convolution_convert_fusion.2
  152.3 0.9 slice_bitcast_fusion.27
  153.2 2.8 copy.93
  156.0 1.3 fusion.37
  157.4 1.8 fusion.43
  159.2 0.8 copy-done.8
  160.0 3.1 fusion.65
  163.1 6.7 %fusion.10 = (f32[12,512]{1,0:T(8,128)S(1)}, f32[512,512,12]{1,0,2:T(8,128)}) fusion(f32[512,512,12]{1,0,2:T(8,128)S(1)} %fusion.43, f32[12,512]{1,0:T(8,128)S(1)} %get-tuple-element.154, pred[512,512]{0,1:T(8,128)(4,1)S(1)} %copy-done.7, bf16[1,1024,12,64]{1,3,2,0:T(8,128)(2,1)S(1)} %bitcast.261, bf16[1,1024,64]{2,1,0:T(8,128)(2,1)S(1)} %copy-done.14), kind=kOutput, calls=%fused_computation.16 | convolution fusion | flops 418375680 | bytes 26402816 | tf_op jit(solution)/shard_map/rqhd,rkd->rhqk/dot_general | solution.py:717
  169.8 6.9 %fusion.18 = bf16[12,512,512]{1,2,0:T(8,128)(2,1)S(1)} fusion(f32[512,512,12]{1,0,2:T(8,128)} %get-tuple-element.164, f32[512,512,12]{1,0,2:T(8,128)S(1)} %fusion.43, f32[12,512]{1,0:T(8,128)S(1)} %get-tuple-element.163, f32[12,512]{1,0:T(8,128)S(1)} %get-tuple-element.154, pred[512,512]{0,1:T(8,128)(4,1)S(1)} %copy-done.7), kind=kLoop, calls=%fused_computation.24 | loop fusion | flops 18874368 | bytes 31768576 | tf_op jit(solution)/shard_map/reshape.140
  176.8 2.0 fusion.64
  178.8 2.4 multiply_bitcast_fusion.1
  181.2 11.7 %fusion.45 = f32[1024,512,12]{1,0,2:T(8,128)} fusion(bf16[1,1024,12,64]{3,1,2,0:T(8,128)(2,1)S(1)} %fusion.37, bf16[1024,128]{1,0:T(8,128)(2,1)S(1)} %copy-done.5), kind=kOutput, calls=%fused_computation.70 | convolution fusion | flops 805306368 | bytes 27000832 | tf_op jit(solution)/shard_map/rqhd,rkd->rhqk/dot_general | solution.py:675
  192.9 11.9 %fusion.59 = bf16[1,1024,64]{1,2,0:T(8,128)(2,1)} fusion(f32[1024,512,12]{1,0,2:T(8,128)} %fusion.45, f32[12,512]{1,0:T(8,128)S(1)} %copy-done.15, pred[512,1024]{0,1:T(8,128)(4,1)S(1)} %copy-done.6, bf16[1,1024,12,64]{1,3,2,0:T(8,128)(2,1)S(1)} %bitcast.262, f32[1,512,64]{1,2,0:T(8,128)S(1)} %fusion.65), kind=kOutput, calls=%fused_computation.81 | convolution fusion | flops 830603264 | bytes 26771456 | tf_op jit(solution)/shard_map/rhqk,rqhd->rkd/dot_general | solution.py:742
  204.8 21.0 %fusion.2 = (f32[12,512]{1,0:T(8,128)S(1)}, f32[1024,512,12]{1,0,2:T(8,128)}) fusion(f32[1024,512,12]{1,0,2:T(8,128)} %fusion.45, f32[12,512]{1,0:T(8,128)S(1)} %copy-done.15, pred[512,1024]{0,1:T(8,128)(4,1)S(1)} %copy-done.6, bf16[1,1024,12,64]{1,3,2,0:T(8,128)(2,1)S(1)} %bitcast.263, bf16[1024,128]{1,0:T(8,128)(2,1)S(1)} %copy-done.5), kind=kOutput, calls=%fused_computation.5 | convolution fusion | flops 836757504 | bytes 51961856 | tf_op jit(solution)/shard_map/rqhd,rkd->rhqk/dot_general | solution.py:717
  225.8 17.4 %fusion.7 = bf16[12,512,1024]{1,2,0:T(8,128)(2,1)S(1)} fusion(f32[1024,512,12]{1,0,2:T(8,128)} %get-tuple-element.162, f32[1024,512,12]{1,0,2:T(8,128)} %fusion.45, f32[12,512]{1,0:T(8,128)S(1)} %get-tuple-element.161, f32[12,512]{1,0:T(8,128)S(1)} %copy-done.15, pred[512,1024]{0,1:T(8,128)(4,1)} %iota_compare_fusion.1), kind=kLoop, calls=%fused_computation.10 | loop fusion | flops 37748736 | bytes 63488000 | tf_op jit(solution)/shard_map/reshape.152
  243.2 6.0 %fusion.55 = f32[1,1024,64]{1,2,0:T(8,128)} fusion(bf16[12,512,1024]{1,2,0:T(8,128)(2,1)S(1)} %fusion.7, bf16[1,1024,12,64]{3,1,2,0:T(8,128)(2,1)} %copy-done, f32[1,512,64]{1,2,0:T(8,128)S(1)} %fusion.64), kind=kOutput, calls=%fused_computation.79 | convolution fusion | flops 805437440 | bytes 14548992 | tf_op jit(solution)/shard_map/rhqk,rqhd->rkd/dot_general | solution.py:733
  249.3 2.3 multiply_bitcast_fusion
  253.5 1.4 fusion.41
  255.0 1.4 fusion.46
  256.5 0.8 copy-done.36
  257.3 2.3 fusion.105
  259.8 2.2 fusion.32
  262.2 1.4 pad_maximum_fusion.refs_0_
  263.6 72.1 %scatter.1 = (f32[24,1024]{1,0:T(8,128)}, f32[24,768]{1,0:T(8,128)}, f32[24,3072]{1,0:T(8,128)}, f32[96,768]{1,0:T(8,128)}) custom-call(bf16[4,2,2,1,48,1024]{5,4,3,2,1,0:T(8,128)(2,1)} %pad_maximum_fusion.refs_0_, bf16[4,2,2,1,48,768]{5,4,3,2,1,0:T(8,128)(2,1)} %bitcast.269, bf16[4,2,2,1,48,3072]{5,4,3,2,1,0:T(8,128)(2,1)} %bitcast.259, ...), custom_call_target="tpu_custom_call" | custom-call | tf_op jit(solution)/shard_map/scatter/pallas_call | solution.py:559
  336.4 1.3 slice.196
  337.7 1.5 slice.195
  340.6 1.5 copy.133
  342.1 1.7 copy.134
  343.8 1.7 copy.135
  (113 shorter events, 7.1 us)
Async XLA Ops:
  0.6 5.2 %copy-start.27 = (f32[2,24]{1,0:T(2,128)S(1)}, f32[2,24]{1,0:T(2,128)}, u32[]{:S(2)}) copy-start(f32[2,24]{1,0:T(2,128)} %param.30) | copy-start | bytes 580
  0.7 5.1 %copy-start.26 = (f32[2,24]{1,0:T(2,128)S(1)}, f32[2,24]{1,0:T(2,128)}, u32[]{:S(2)}) copy-start(f32[2,24]{1,0:T(2,128)} %param.29) | copy-start | bytes 580
  1.3 9.2 %copy-start.24 = (f32[8]{0:T(128)}, f32[8]{0:T(128)S(1)}, u32[]{:S(2)}) copy-start(f32[8]{0:T(128)S(1)} %multiply_power_fusion) | copy-start | bytes 100
  3.1 2.6 copy-start.19
  13.4 93.5 %copy-start.28 = (f32[22]{0:T(128)S(1)}, f32[22]{0:T(128)}, u32[]{:S(2)}) copy-start(f32[22]{0:T(128)} %param.33) | copy-start | bytes 268
  13.4 95.4 %copy-start.10 = (bf16[1024,768]{1,0:T(8,128)(2,1)S(1)}, bf16[1024,768]{1,0:T(8,128)(2,1)}, u32[]{:S(2)}) copy-start(bf16[1024,768]{1,0:T(8,128)(2,1)} %param.31) | copy-start | bytes 4718596
  108.8 9.0 %copy-start.29 = (bf16[1024,3072]{1,0:T(8,128)(2,1)S(1)}, bf16[1024,3072]{1,0:T(8,128)(2,1)}, u32[]{:S(2)}) copy-start(bf16[1024,3072]{1,0:T(8,128)(2,1)} %get-tuple-element.92) | copy-start | bytes 18874372
  108.8 9.0 %copy-start.30 = (bf16[4,2,2,2,96,768]{5,4,3,2,1,0:T(8,128)(2,1)S(1)}, bf16[4,2,2,2,96,768]{5,4,3,2,1,0:T(8,128)(2,1)}, u32[]{:S(2)}) copy-start(bf16[4,2,2,2,96,768]{5,4,3,2,1,0:T(8,128)(2,1)} %get-tuple-element.93) | copy-start | bytes 14155780
  117.8 14.7 %slice-start = ((s8[4718592]{0:T(1024)(128)(4,1)}), s8[4194304]{0:T(1024)(128)(4,1)S(1)}, s32[]{:S(2)}) async-start(s8[4718592]{0:T(1024)(128)(4,1)} %bitcast.276), calls=%async_computation | async-start | bytes 8388608
  122.9 7.0 %copy-start.1 = (bf16[1024,768]{1,0:T(8,128)(2,1)S(1)}, bf16[1024,768]{1,0:T(8,128)(2,1)}, u32[]{:S(2)}) copy-start(bf16[1024,768]{1,0:T(8,128)(2,1)} %refs_0_.1) | copy-start | bytes 4718596
  122.9 7.0 %copy-start.32 = (bf16[1024,768]{1,0:T(8,128)(2,1)S(1)}, bf16[1024,768]{1,0:T(8,128)(2,1)}, u32[]{:S(2)}) copy-start(bf16[1024,768]{1,0:T(8,128)(2,1)} %get-tuple-element.90) | copy-start | bytes 4718596
  122.9 7.0 %copy-start.34 = (bf16[4,2,2,1,48,768]{5,4,3,2,1,0:T(8,128)(2,1)S(1)}, bf16[4,2,2,1,48,768]{5,4,3,2,1,0:T(8,128)(2,1)}, u32[]{:S(2)}) copy-start(bf16[4,2,2,1,48,768]{5,4,3,2,1,0:T(8,128)(2,1)} %get-tuple-element.91) | copy-start | bytes 3538948
  122.9 9.6 %slice-start.1 = ((s8[4718592]{0:T(1024)(128)(4,1)}), s8[524288]{0:T(1024)(128)(4,1)S(1)}, s32[]{:S(2)}) async-start(s8[4718592]{0:T(1024)(128)(4,1)} %bitcast.276), calls=%async_computation.1 | async-start | bytes 1048576
  132.5 6.7 %copy-start.33 = (bf16[1024,768]{1,0:T(8,128)(2,1)S(1)}, bf16[1024,768]{1,0:T(8,128)(2,1)}, u32[]{:S(2)}) copy-start(bf16[1024,768]{1,0:T(8,128)(2,1)} %get-tuple-element.102) | copy-start | bytes 4718596
  146.5 2.5 copy-start.18
  149.7 2.6 copy-start.5
  152.3 3.7 %copy-start.4 = (bf16[12,1024,128]{2,1,0:T(8,128)(2,1)S(1)}, bf16[12,1024,128]{2,1,0:T(8,128)(2,1)}, u32[]{:S(2)}) copy-start(bf16[12,1024,128]{2,1,0:T(8,128)(2,1)} %get-tuple-element.96) | copy-start | bytes 9437188
  156.0 1.4 copy-start.13
  157.4 23.8 %copy-start = (bf16[1,1024,12,64]{3,1,2,0:T(8,128)(2,1)}, bf16[1,1024,12,64]{3,1,2,0:T(8,128)(2,1)S(1)}, u32[]{:S(2)}) copy-start(bf16[1,1024,12,64]{3,1,2,0:T(8,128)(2,1)S(1)} %fusion.37) | copy-start | bytes 4718596
  157.4 1.8 copy-start.7
  157.4 2.6 copy-start.8
  160.0 3.1 copy-start.14
  181.1 11.7 %copy-start.6 = (pred[512,1024]{0,1:T(8,128)(4,1)S(1)}, pred[512,1024]{0,1:T(8,128)(4,1)}, u32[]{:S(2)}) copy-start(pred[512,1024]{0,1:T(8,128)(4,1)} %iota_compare_fusion.1) | copy-start | bytes 1572868
  181.1 11.7 %copy-start.15 = (f32[12,512]{1,0:T(8,128)S(1)}, f32[12,512]{1,0:T(8,128)}, u32[]{:S(2)}) copy-start(f32[12,512]{1,0:T(8,128)} %get-tuple-element.155) | copy-start | bytes 73732
  249.3 2.3 copy-start.12
  249.3 2.4 copy-start.25
  249.3 2.6 copy-start.9
  249.3 2.7 copy-start.35
  251.6 1.4 copy-start.3
  251.7 1.4 copy-start.16
  251.7 1.4 copy-start.17
  253.5 1.4 copy-start.31
  254.9 1.5 copy-start.2
  254.9 1.5 copy-start.20
  254.9 1.5 copy-start.21
  254.9 1.5 copy-start.22
  255.0 1.5 copy-start.23
  255.0 2.4 copy-start.36
  257.3 2.4 copy-start.11

commit v3 on v2

v3 whole, which is shorter than its diff:
```python
import functools

import jax
import jax.numpy as jnp
import numpy as np
from jax import lax
from jax.experimental import pallas as pl
from jax.experimental.pallas import tpu as pltpu
from jax.sharding import PartitionSpec as P

D = 768
H = 12
HD = 64
ROT = 16
SUBSETS = 22
SEQ = 1024
PACK = 1024
TILE = 256
LOG2E = 1.4426950408889634
MESH = pl.DeviceIdType.MESH


eps_norm = 1e-05


def place():
    dp, fs = lax.axis_index("dp"), lax.axis_index("fsdp")
    return dp // 2, dp % 2, fs // 2, fs % 2


def device(z, x, y, c):
    return (z * 2 + x, y * 2 + c)


def partners():
    z, x, y, c = place()
    xa, ya = jnp.where(c == 0, 1 - x, x), jnp.where(c == 0, y, 1 - y)
    xb, yb = jnp.where(c == 0, x, 1 - x), jnp.where(c == 0, 1 - y, y)
    return xa, ya, xb, yb


def greet(lines):
    z, x, y, c = place()
    barrier = pltpu.get_barrier_semaphore()
    others = [device(lax.rem(z + d, lines), x, y, c) for d in range(1, lines)]
    others += [device(z, 1 - x, y, c), device(z, x, 1 - y, c), device(z, x, y, 1 - c)]
    for other in others:
        pl.semaphore_signal(barrier, inc=1, device_id=other, device_id_type=MESH)
    pl.semaphore_wait(barrier, len(others))


def remote(src, dst, send, recv, where):
    return pltpu.make_async_remote_copy(
        src_ref=src, dst_ref=dst, send_sem=send, recv_sem=recv, device_id=where, device_id_type=MESH
    )


def layout(rows, rows_down):
    blocks = [(1, 2 * rows, PACK), (1, 2 * rows, D), (1, 2 * rows, 4 * D), (2, rows_down, D)]
    return blocks


def pieces_of(blocks):
    (_, r0, _), (_, r1, _), (_, r2, _), (_, r3, _) = blocks
    up, third = D // 2, r3 // 3 // 16 * 16
    downs = [(0, third), (third, third), (2 * third, r3 - 2 * third)]
    return (
        [(0, 0, r0, 0, PACK // 2)]
        + [(2, 0, r2, k * up, up) for k in range(4)]
        + [(1, 0, r1, 0, D // 2)]
        + [(3, r, n, 0, D // 2) for r, n in downs]
    )


def lanes(start, size):
    return pl.ds(pl.multiple_of(start, 128), size)


def part(piece, halves, ref, z, x, y, c):
    t, r0, nr, c0, w = piece
    return ref.at[z, x, y, :, pl.ds(r0, nr), lanes(c * halves[t] + c0, w)]


class Gather:
    def __init__(self, lines, rows, blocks, sources, stages, whole, sems):
        self.lines, self.rows, self.blocks = lines, rows, blocks
        self.sources, self.stages, self.whole = sources, stages, whole
        self.swap_send, self.swap_recv, self.send, self.recv = sems
        self.pieces = pieces_of(blocks)
        self.halves = [b[2] // 2 for b in blocks]
        self.z, self.x, self.y, self.c = place()
        self.xa, self.ya, self.xb, self.yb = partners()
        self.sibling = device(self.z, self.x, self.y, 1 - self.c)
        self.started = []

    def go(self, make):
        make().start()
        self.started.append(make)

    def stage_rows(self, t, core):
        if self.blocks[t][0] == 2:
            return self.stages[t].at[core]
        return self.stages[t].at[0, pl.ds(pl.multiple_of(core * self.rows, 8), self.rows)]

    def swap(self, t):
        h = self.halves[t]
        return remote(
            self.sources[t].at[:, lanes((1 - self.c) * h, h)],
            self.stage_rows(t, self.c),
            self.swap_send.at[t],
            self.swap_recv.at[t],
            self.sibling,
        )

    def direct(self, p, d, received=False):
        z, n = self.z, self.lines
        at = lax.rem(z + n - d, n) if received else z
        block = part(self.pieces[p], self.halves, self.whole[self.pieces[p][0]], at, self.x, self.y, self.c)
        where = device(lax.rem(z + d, n), self.x, self.y, self.c)
        return remote(block, block, self.send.at[p, d - 1], self.recv.at[p, d - 1], where)

    def share(self, p, k, sx, sy, half, where):
        column = part(self.pieces[p], self.halves, self.whole[self.pieces[p][0]], slice(None), sx, sy, half)
        k = k + self.lines - 1
        return remote(column, column, self.send.at[p, k], self.recv.at[p, k], where)

    def begin(self):
        for t in (0, 2, 1, 3):
            self.go(functools.partial(self.swap, t))
        for t in (0, 2, 1, 3):
            h = self.halves[t]
            self.stage_rows(t, self.c)[...] = jnp.where(self.c == 0, self.sources[t][:, :h], self.sources[t][:, h:])
            self.swap(t).wait_recv()
            self.whole[t][self.z, self.x, self.y, :, :, lanes(self.c * h, h)] = self.stages[t][...].astype(jnp.bfloat16)
            for p, piece in enumerate(self.pieces):
                if piece[0] == t:
                    for d in range(1, self.lines):
                        self.go(functools.partial(self.direct, p, d))

    def first(self, p):
        for d in range(1, self.lines):
            self.direct(p, d, received=True).wait_recv()
        x, y, c, z = self.x, self.y, self.c, self.z
        self.go(lambda: self.share(p, 0, x, y, c, device(z, self.xa, self.ya, c)))
        self.go(lambda: self.share(p, 1, x, y, c, device(z, self.xb, self.yb, c)))
        self.go(lambda: self.share(p, 3, x, y, c, self.sibling))

    def second(self, p):
        c, z = self.c, self.z
        self.share(p, 0, self.xa, self.ya, c, self.sibling).wait_recv()
        self.go(lambda: self.share(p, 2, self.xa, self.ya, c, device(z, self.xb, self.yb, c)))
        self.go(lambda: self.share(p, 4, self.xa, self.ya, c, self.sibling))

    def third(self, p):
        x, y, c = self.x, self.y, self.c
        self.share(p, 1, self.xb, self.yb, c, self.sibling).wait_recv()
        self.go(lambda: self.share(p, 5, self.xb, self.yb, c, self.sibling))
        self.share(p, 2, 1 - x, 1 - y, c, self.sibling).wait_recv()
        self.go(lambda: self.share(p, 6, 1 - x, 1 - y, c, self.sibling))

    def fourth(self, p):
        x, y, c = self.x, self.y, 1 - self.c
        for k, sx, sy in ((3, x, y), (4, self.xb, self.yb), (5, self.xa, self.ya), (6, 1 - x, 1 - y)):
            self.share(p, k, sx, sy, c, self.sibling).wait_recv()

    def events(self):
        count, order = len(self.pieces), []
        for s in range(count + 3):
            for k, step in enumerate((self.first, self.second, self.third, self.fourth)):
                if 0 <= s - k < count:
                    order.append((functools.partial(step, s - k), (k, s - k)))
        cut = order.index(next(o for o in order if o[1] == (3, 0))) + 1
        return order[:cut], order[cut:]


def spread(events, slots):
    plan = [[] for _ in range(slots)]
    for k, event in enumerate(events):
        plan[k * slots // max(len(events), 1)].append(event)
    return plan


def run_at(index, values):
    for value, events in values:
        if events:

            @pl.when(index == value)
            def _(events=events):
                for event in events:
                    event()


def columns(ref, start, size):
    return ref[:, :, :, :, :, pl.ds(start, size)].reshape(-1, size)


def turned(a, b):
    return lax.dot_general(a, b, (((1,), (1,)), ((), ())), preferred_element_type=jnp.float32)


def swapped(block, cosine, sine):
    lane = lax.broadcasted_iota(jnp.int32, block.shape, 1)
    other = jnp.where(lane % 16 < 8, pltpu.roll(block, 120, 1), pltpu.roll(block, 8, 1))
    return block * cosine + other * sine


def forward_kernel(lines, rows, blocks, linked, *refs):
    f32, bf16 = jnp.float32, jnp.bfloat16
    tokens, cosine, sine = refs[:3]
    given = refs[3:11] if linked else refs[3:7]
    refs = refs[11:] if linked else refs[7:]
    results, refs = refs[: 9 + 4 * linked], refs[9 + 4 * linked :]
    small, first_in, second_in, queries, kv, attended, logsums, hidden, slope, *rest = refs
    normed, keys, values_t, mask, out_sems, *rest = rest
    held = [small, first_in, second_in, queries, kv, attended, logsums, hidden, slope]
    flushed = []

    def flush(*which):
        for k in which:
            copy = pltpu.make_async_copy(held[k], results[k], out_sems.at[k])
            copy.start()
            flushed.append(copy)

    if linked:
        query, pair, out, up, down, gains, biases, tags = given
        whole, packed, stages, sems, square = rest[:4], rest[4], rest[5:9], rest[9:13], rest[13]
        held += whole
        packed[:, :D] = query[...]
        packed[:, D : D + 2 * HD] = pair[...]
        square[...] = jnp.zeros_like(square)
        square[0:2, 0:rows] = gains[...]
        square[2:4, 0:rows] = biases[...]
        spot = lax.broadcasted_iota(jnp.int32, (rows, 128), 1) == tags[0] + 4
        spot = jnp.where(lax.broadcasted_iota(jnp.int32, (rows, 128), 0) == 0, spot.astype(f32), 0.0)
        packed[:, D + 2 * HD :] = square[...].T[:rows] + spot
        greet(lines)
        gather = Gather(lines, rows, blocks, [packed, out, up, down], stages, whole, sems)
        gather.begin()
        urgent, later = gather.events()
        cut = later.index(next(e for e in later if e[1] == (3, 4))) + 1
        early, late = [e[0] for e in later[:cut]], [e[0] for e in later[cut:]]
    else:
        whole, early, late = given, [], []
    packed_w, up_w = whole[0], whole[2]

    row = lax.broadcasted_iota(jnp.int32, (TILE, TILE), 0)
    column = lax.broadcasted_iota(jnp.int32, (TILE, TILE), 1)
    mask[...] = jnp.where(row <= column, 0.0, -1e30)
    tiles = SEQ // TILE

    def tile(k):
        return pl.ds(pl.multiple_of(k * TILE, TILE), TILE)

    @pl.loop(0, tiles)
    def _(k):
        inputs = tokens[tile(k), :].astype(f32)
        centred = inputs - jnp.mean(inputs, axis=-1, keepdims=True)
        normed[tile(k), :] = centred * lax.rsqrt(jnp.mean(centred * centred, axis=-1, keepdims=True) + eps_norm)

    if linked:
        for event, _ in urgent:
            event()
    small[...] = columns(packed_w, D + 2 * HD, 128).astype(f32).T
    plan = spread(early, 28)

    @pl.loop(0, tiles)
    def _(k):
        norm = normed[tile(k), :]
        a1 = (norm * small[0:1, :] + small[2:3, :]).astype(bf16)
        first_in[tile(k), :] = a1
        second_in[tile(k), :] = (norm * small[1:2, :] + small[3:4, :]).astype(bf16)
        mixed = jnp.dot(a1, columns(packed_w, 0, D + 2 * HD), preferred_element_type=f32)
        cos_t, sin_t = cosine[tile(k), :], sine[tile(k), :]
        left = lax.broadcasted_iota(jnp.int32, (TILE, 2 * HD), 1) < HD
        for p in range(H // 2):
            turn = swapped(mixed[:, 2 * HD * p : 2 * HD * (p + 1)], cos_t, sin_t).astype(bf16).astype(f32)
            turn = turn * (LOG2E / 8)
            high = turn.astype(bf16).astype(f32)
            low = turn - high
            queries[2 * p, tile(k), :] = jnp.where(left, high, pltpu.roll(low, HD, 1)).astype(bf16)
            queries[2 * p + 1, tile(k), :] = jnp.where(left, pltpu.roll(high, HD, 1), low).astype(bf16)
        pair_t = mixed[:, D : D + 2 * HD]
        pair_t = jnp.where(left, swapped(pair_t, cos_t, sin_t), pair_t).astype(bf16).astype(f32)
        kv[tile(k), :] = pair_t.astype(bf16)
        other = pltpu.roll(pair_t, HD, 1)
        keys[tile(k), :] = jnp.where(left, pair_t, other).astype(bf16)
        lane = lax.broadcasted_iota(jnp.int32, (TILE, 2 * HD), 1)
        ones = jnp.where(lane == HD, 1.0, 0.0)
        values_t[:, tile(k)] = jnp.where(left, other, ones).T.astype(bf16)
        run_at(k, [(v, plan[v]) for v in range(tiles)])

    flush(0, 1, 2, 3, 4)
    plan = plan[tiles:]

    @pl.loop(0, H // 2)
    def _(pr):
        for i in range(tiles):
            count = TILE * (i + 1)
            heads = []
            for hh in range(2):
                head = pr * 2 + hh
                scores = turned(keys[0:count, :], queries[head, i * TILE : count, :])
                last = scores[count - TILE :] + mask[...]
                peak = jnp.max(last, axis=0, keepdims=True)
                if i:
                    peak = jnp.maximum(peak, jnp.max(scores[: count - TILE], axis=0, keepdims=True))
                probs = jnp.exp2(last - peak).astype(bf16)
                if i:
                    probs = jnp.concatenate([jnp.exp2(scores[: count - TILE] - peak).astype(bf16), probs], axis=0)
                got = jnp.dot(values_t[:, 0:count], probs, preferred_element_type=f32)
                total = got[HD : HD + 1]
                heads.append(got[:HD] * (1.0 / total))
                logsums[head, :, i * TILE : count] = peak + jnp.log2(total)
            both = jnp.concatenate(heads, axis=0).T
            attended[i * TILE : count, lanes(pr * 2 * HD, 2 * HD)] = both.astype(bf16)
            run_at(pr, [(v, plan[v * tiles + i]) for v in range(H // 2)])

    flush(5, 6)
    plan = spread(late, 4 * tiles)

    @pl.loop(0, 4 * tiles)
    def _(s):
        chunk, k = s // tiles, s % tiles
        pre = jnp.dot(second_in[tile(k), :], columns(up_w, pl.multiple_of(chunk * D, D), D), preferred_element_type=f32)
        cdf = 0.5 + 0.5 * lax.erf(pre * 0.7071067811865476)
        hidden[tile(k), lanes(chunk * D, D)] = (pre * cdf).astype(bf16)
        density = jnp.exp2(pre * pre * (-0.5 * LOG2E)) * 0.3989422804014327
        slope[tile(k), lanes(chunk * D, D)] = (cdf + pre * density).astype(bf16)
        run_at(s, [(v, plan[v]) for v in range(4 * tiles)])

    flush(7, 8)
    if linked:
        flush(9, 10, 11, 12)
        for make in gather.started:
            make().wait_send()
    for copy in flushed:
        copy.wait()


def tables():
    half = ROT // 2
    inverse = np.float32(10000.0) ** (-(np.arange(half, dtype=np.float32) * 2) / ROT)
    phase = np.arange(SEQ, dtype=np.float32)[:, None] * inverse.astype(np.float32)[None, :]
    cos_t, sin_t = np.cos(phase.astype(np.float64)), np.sin(phase.astype(np.float64))
    rest = np.zeros((SEQ, HD - ROT))
    cosine = np.concatenate([cos_t, cos_t, rest + 1.0] * 2, axis=1)
    sine = np.concatenate([-sin_t, sin_t, rest] * 2, axis=1)
    return jnp.asarray(cosine.astype(np.float32)), jnp.asarray(sine.astype(np.float32))


def forward(linked, lines, rows, rows_down, tokens, cosine, sine, weights):
    blocks = layout(rows, rows_down)
    f32, bf16 = jnp.float32, jnp.bfloat16
    shapes = [(lines, 2, 2, g, r, k) for g, r, k in blocks]
    if not linked:
        weights = [a.reshape(shape) for a, shape in zip(weights, shapes)]
    held = [
        ((128, D), f32),
        ((SEQ, D), bf16),
        ((SEQ, D), bf16),
        ((H, SEQ, 2 * HD), bf16),
        ((SEQ, 2 * HD), bf16),
        ((SEQ, D), bf16),
        ((H, 1, SEQ), f32),
        ((SEQ, 4 * D), bf16),
        ((SEQ, 4 * D), bf16),
    ]
    scratch = [pltpu.VMEM(shape, kind) for shape, kind in held]
    scratch += [
        pltpu.VMEM((SEQ, D), f32),
        pltpu.VMEM((SEQ, 2 * HD), bf16),
        pltpu.VMEM((2 * HD, SEQ), bf16),
        pltpu.VMEM((TILE, TILE), f32),
        pltpu.SemaphoreType.DMA((13,)),
    ]
    if linked:
        held += [(shape, bf16) for shape in shapes]
        scratch += [pltpu.VMEM(shape, bf16) for shape in shapes]
        scratch += [pltpu.VMEM((rows, PACK), f32)]
        scratch += [pltpu.VMEM((g, r, k // 2), f32) for g, r, k in blocks]
        count, kinds = len(pieces_of(blocks)), lines + 6
        scratch += [pltpu.SemaphoreType.DMA((4,))] * 2 + [pltpu.SemaphoreType.DMA((count, kinds))] * 2
        scratch += [pltpu.VMEM((128, 128), f32)]
    specs = [pl.BlockSpec(memory_space=pltpu.VMEM)] * (3 + len(weights))
    if linked:
        specs[-1] = pl.BlockSpec(memory_space=pltpu.SMEM)
    got = pl.pallas_call(
        functools.partial(forward_kernel, lines, rows, blocks, linked),
        out_shape=[jax.ShapeDtypeStruct(shape, kind) for shape, kind in held],
        in_specs=specs,
        out_specs=[pl.BlockSpec(memory_space=pl.ANY)] * len(held),
        scratch_shapes=scratch,
        compiler_params=pltpu.CompilerParams(
            collective_id=0 if linked else None, has_side_effects=linked, vmem_limit_bytes=60 * 2**20
        ),
        name="forward",
    )(tokens, cosine, sine, *weights)
    return got[:9], list(got[9:]) if linked else weights


def scatter_pieces(blocks):
    (_, r0, _), (_, r1, _), (_, r2, _), (_, r3, _) = blocks
    w, half = D // 2, r3 // 2 // 16 * 16
    return (
        [(1, 0, r1, 0, w)]
        + [(2, 0, r2, k * w, w) for k in range(4)]
        + [(3, 0, half, 0, w), (3, half, r3 - half, 0, w), (0, 0, r0, 0, PACK // 2)]
    )


SLOTS = 2


class Scatter:
    def __init__(self, lines, rows, blocks, grads, outs, buffers, sems):
        self.lines, self.rows, self.blocks = lines, rows, blocks
        self.grads, self.outs = grads, outs
        self.near, self.near_last = buffers[0:2]
        self.from_b, self.from_a, self.from_z, self.total, self.last = (buffers[2 + 4 * k : 6 + 4 * k] for k in range(5))
        self.send, self.recv, self.credit = sems
        self.pieces = scatter_pieces(blocks)
        self.halves = [b[2] // 2 for b in blocks]
        self.z, self.x, self.y, self.c = place()
        self.xa, self.ya, self.xb, self.yb = partners()
        self.sibling = device(self.z, self.x, self.y, 1 - self.c)
        self.started = []

    def go(self, make):
        make().start()
        self.started.append(make)

    def cut(self, p, ref, *lead):
        t, r0, nr, c0, w = self.pieces[p]
        return ref[t].at[(*lead, slice(None), pl.ds(r0, nr), pl.ds(c0, w))]

    def grad(self, p, z, x, y, half=None):
        half = self.c if half is None else half
        return part(self.pieces[p], self.halves, self.grads[self.pieces[p][0]], z, x, y, half)

    def near_at(self, p):
        t, r0, nr, c0, w = self.pieces[p]
        if t == 0:
            return self.near_last
        return self.near.at[p % SLOTS, :, :, :, pl.ds(0, self.blocks[t][0]), pl.ds(0, nr), pl.ds(0, w)]

    def near_copy(self, p):
        every = slice(None)
        mine = self.grad(p, every, every, every, 1 - self.c)
        return remote(mine, self.near_at(p), self.send.at[p, 0], self.recv.at[p, 0], self.sibling)

    def b_copy(self, p, k):
        at = (self.xb, self.yb) if k == 0 else (1 - self.x, 1 - self.y)
        return remote(
            self.grad(p, slice(None), *at),
            self.cut(p, self.from_b, k, slice(None)),
            self.send.at[p, 1 + k],
            self.recv.at[p, 1 + k],
            device(self.z, self.xb, self.yb, self.c),
        )

    def a_copy(self, p):
        return remote(
            self.grad(p, slice(None), self.xa, self.ya),
            self.cut(p, self.from_a, slice(None)),
            self.send.at[p, 3],
            self.recv.at[p, 3],
            device(self.z, self.xa, self.ya, self.c),
        )

    def z_copy(self, p, d):
        other = lax.rem(self.z + d, self.lines)
        return remote(
            self.grad(p, other, self.x, self.y),
            self.cut(p, self.from_z, d - 1),
            self.send.at[p, 3 + d],
            self.recv.at[p, 3 + d],
            device(other, self.x, self.y, self.c),
        )

    def last_copy(self, p):
        t, r0, nr, c0, w = self.pieces[p]
        if self.blocks[t][0] == 2:
            src = self.total[t].at[1 - self.c, pl.ds(r0, nr), pl.ds(c0, w)]
            dst = self.last[t].at[pl.ds(r0, nr), pl.ds(c0, w)]
        else:
            away = pl.ds(pl.multiple_of((1 - self.c) * self.rows, 8), self.rows)
            src = self.total[t].at[0, away, pl.ds(c0, w)]
            dst = self.last[t].at[:, pl.ds(c0, w)]
        k = 3 + self.lines
        return remote(src, dst, self.send.at[p, k], self.recv.at[p, k], self.sibling)

    def first(self, p):
        if SLOTS <= p < len(self.pieces) - 1:
            pl.semaphore_wait(self.credit, 1)
        self.go(lambda: self.near_copy(p))

    def second(self, p):
        self.near_copy(p).wait_recv()
        near = self.near_at(p)

        @pl.loop(0, self.lines)
        def _(k):
            for x in range(2):
                for y in range(2):
                    kept = self.grad(p, k, x, y)
                    kept[...] = (kept[...].astype(jnp.float32) + near[k, x, y].astype(jnp.float32)).astype(jnp.bfloat16)

        if p + SLOTS < len(self.pieces) - 1:
            pl.semaphore_signal(self.credit, inc=1, device_id=self.sibling, device_id_type=MESH)
        self.go(lambda: self.b_copy(p, 1))
        self.go(lambda: self.b_copy(p, 0))

    def third(self, p):
        self.b_copy(p, 1).wait_recv()

        @pl.loop(0, self.lines)
        def _(k):
            kept, got = self.grad(p, k, self.xa, self.ya), self.cut(p, self.from_b, 1, k)
            kept[...] = (kept[...].astype(jnp.float32) + got[...].astype(jnp.float32)).astype(jnp.bfloat16)

        self.go(lambda: self.a_copy(p))

    def mine(self, p, k):
        got = self.cut(p, self.from_b, 0, k)[...].astype(jnp.float32) + self.cut(p, self.from_a, k)[...].astype(jnp.float32)
        return self.grad(p, k, self.x, self.y)[...].astype(jnp.float32) + got

    def fourth(self, p):
        self.b_copy(p, 0).wait_recv()
        self.a_copy(p).wait_recv()

        @pl.loop(1, self.lines)
        def _(d):
            k = lax.rem(self.z + d, self.lines)
            self.grad(p, k, self.x, self.y)[...] = self.mine(p, k).astype(jnp.bfloat16)

        for d in range(1, self.lines):
            self.go(functools.partial(self.z_copy, p, d))
        self.cut(p, self.total)[...] = self.mine(p, self.z)

    def fifth(self, p):
        for d in range(1, self.lines):
            self.z_copy(p, d).wait_recv()
        total = self.cut(p, self.total)
        acc = total[...]
        for d in range(1, self.lines):
            acc = acc + self.cut(p, self.from_z, d - 1)[...].astype(jnp.float32)
        total[...] = acc
        self.go(lambda: self.last_copy(p))

    def sixth(self, p):
        t, r0, nr, c0, w = self.pieces[p]
        self.last_copy(p).wait_recv()
        if self.blocks[t][0] == 2:
            kept = self.total[t][self.c, r0 : r0 + nr, c0 : c0 + w]
            got = self.last[t][r0 : r0 + nr, c0 : c0 + w]
            to = slice(r0, r0 + nr)
        else:
            kept = self.total[t][0, pl.ds(pl.multiple_of(self.c * self.rows, 8), self.rows), c0 : c0 + w]
            got = self.last[t][:, c0 : c0 + w]
            to = slice(None)
        h = self.halves[t]
        self.outs[t][to, c0 : c0 + w] = jnp.where(self.c == 0, kept, got)
        self.outs[t][to, h + c0 : h + c0 + w] = jnp.where(self.c == 0, got, kept)

    def steps(self):
        return [self.first, self.second, self.third, self.fourth, self.fifth, self.sixth]

    def events(self):
        count, steps = len(self.pieces) - 1, self.steps()
        return [
            [functools.partial(step, s - k) for k, step in enumerate(steps) if 0 <= s - k < count]
            for s in range(count + len(steps) - 1)
        ]


def crossed(a, b):
    return lax.dot_general(a, b, (((0,), (0,)), ((), ())), preferred_element_type=jnp.float32)


def backward_kernel(lines, rows, blocks, linked, total_rows, *refs):
    f32, bf16 = jnp.float32, jnp.bfloat16
    tags, subset_w, cosine, sine = refs[:4]
    (tokens_h, cotan_h, small_h, first_h, second_h, queries_h, kv_h, attended_h, logsums_h, hidden_h, slope_h) = refs[4:15]
    packed_h, out_h, up_h, down_h = refs[15:19]
    mixed_h, grad_tokens_h = refs[19:21]
    results, refs = refs[21:25], refs[25:]
    (tokens, cotan, small, ins, queries, kv, attended, logsums, hidden, slope, packed_w, out_w, up_w, down_w) = refs[:14]
    (branch, d_second, scaled, d_heads, keys, keys_t, values, d_keys, d_values, d_pair, mask, sums) = refs[14:26]
    grads, load_sems, chunk_sems, out_sems = refs[26:30], refs[30], refs[31], refs[32]
    refs = refs[33:]
    tiles, wide = SEQ // TILE, D // 2
    qkv = D + 2 * HD

    def tile(k):
        return pl.ds(pl.multiple_of(k * TILE, TILE), TILE)

    def load(k, src, dst):
        return pltpu.make_async_copy(src, dst, load_sems.at[k])

    loads = [
        load(0, small_h, small),
        load(1, cotan_h, cotan),
        load(2, out_h, out_w),
        load(3, tokens_h, tokens),
        load(4, attended_h, attended),
        load(5, second_h, ins),
        load(6, kv_h, kv),
        load(7, logsums_h, logsums),
        load(8, queries_h, queries),
        load(9, packed_h, packed_w),
    ]

    def chunk_of(j):
        return (j % 2) * 2 + j // 2

    def chunk_loads(j):
        q, slot = chunk_of(j), j % 2
        cols = lanes(q * D, D)
        pairs = [
            (hidden_h.at[:, cols], hidden.at[slot]),
            (slope_h.at[:, cols], slope.at[slot]),
            (up_h.at[:, :, :, :, :, cols], up_w.at[slot]),
            (down_h.at[q], down_w.at[slot]),
        ]
        return [pltpu.make_async_copy(a, b, chunk_sems.at[slot, k]) for k, (a, b) in enumerate(pairs)]

    for copy in loads[:5]:
        copy.start()
    for copy in chunk_loads(0):
        copy.start()
    for copy in loads[5:]:
        copy.start()
    if linked:
        greet(lines)
        scatter = Scatter(lines, rows, blocks, grads, results, refs[:22], refs[22:25])
        turns = scatter.events()
    else:
        scatter, turns = None, []

    def turn(a, b):
        return [event for events in turns[a:b] for event in events]

    row = lax.broadcasted_iota(jnp.int32, (TILE, TILE), 0)
    column = lax.broadcasted_iota(jnp.int32, (TILE, TILE), 1)
    mask[...] = jnp.where(row <= column, 0.0, -1e30)
    sums[...] = jnp.zeros_like(sums)
    d_keys[...] = jnp.zeros_like(d_keys)
    d_values[...] = jnp.zeros_like(d_values)
    lane = lax.broadcasted_iota(jnp.int32, (TILE, 2 * HD), 1)
    left = lane < HD

    for copy in loads[:5]:
        copy.wait()
    kind = lax.broadcasted_iota(jnp.int32, (128, D), 0)
    count = jnp.sum(jnp.where(kind == tags[0] + 4, small[...], 0.0), keepdims=True)
    subset = lax.broadcasted_iota(jnp.int32, subset_w.shape, 1)
    weight = jnp.sum(jnp.where(subset == tags[0], subset_w[...], 0.0), keepdims=True)
    scale = weight / count * (total_rows / SUBSETS)

    @pl.loop(0, tiles)
    def _(k):
        grad_out = (cotan[tile(k), :].astype(f32) * scale).astype(bf16)
        scaled[tile(k), :] = grad_out
        heads = attended[tile(k), :]
        out_m = out_w[...].reshape(D, D)
        branch[tile(k), :] = tokens[tile(k), :].astype(f32) + jnp.dot(heads, out_m, preferred_element_type=f32)
        d_heads_t = turned(grad_out, out_m).astype(bf16).astype(f32)
        for p in range(H // 2):
            block = d_heads_t[:, 2 * HD * p : 2 * HD * (p + 1)]
            product = block * heads[:, 2 * HD * p : 2 * HD * (p + 1)].astype(f32)
            for hh, (mine, there) in enumerate(((left, block), (~left, pltpu.roll(block, HD, 1)))):
                delta = jnp.sum(jnp.where(mine, product, 0.0), axis=1, keepdims=True)
                high = delta.astype(bf16).astype(f32)
                extra = jnp.where(lane == HD, high, jnp.where(lane == HD + 1, delta - high, 0.0))
                d_heads[2 * p + hh, tile(k), :] = jnp.where(left, there, extra).astype(bf16)

    @pl.loop(0, 2)
    def _(k):
        got = crossed(attended[:, lanes(k * wide, wide)], scaled[...]).astype(bf16)
        grads[1][pl.ds(2 * k, 2)] = got.reshape(2, 2, 2, 1, D // 16, D)

    for event in turn(0, 1):
        event()
    loads[5].wait()

    @pl.loop(0, 4)
    def _(j):
        slot, q = j % 2, chunk_of(j)
        for copy in chunk_loads(j):
            copy.wait()

        @pl.when(j < 3)
        def _():
            for copy in chunk_loads(j + 1):
                copy.start()

        run_at(j, [(2, turn(1, 2)), (3, turn(2, 3))])
        down_m, up_m = down_w[slot].reshape(D, D), up_w[slot].reshape(D, D)

        @pl.loop(0, tiles)
        def _(k):
            branch[tile(k), :] += jnp.dot(hidden[slot, tile(k), :], down_m, preferred_element_type=f32)
            d_hidden = turned(scaled[tile(k), :], down_m)
            d_up = (d_hidden * slope[slot, tile(k), :].astype(f32)).astype(bf16)
            slope[slot, tile(k), :] = d_up
            got = turned(d_up, up_m)
            d_second[tile(k), :] = jnp.where(j == 0, got, got + d_second[tile(k), :])

        @pl.loop(0, 2)
        def _(k):
            got = crossed(hidden[slot, :, lanes(k * wide, wide)], scaled[...]).astype(bf16)
            grads[3][q, k] = got.reshape(2, 2, 4 * D // 32, D)
            got = crossed(ins[:, lanes(k * wide, wide)], slope[slot]).astype(bf16)
            grads[2][pl.ds(2 * k, 2), :, :, :, :, lanes(q * D, D)] = got.reshape(2, 2, 2, 1, D // 16, D)

    copy_first = load(5, first_h, ins)
    copy_first.start()

    @pl.loop(0, tiles)
    def _(k):
        attended[tile(k), :] = branch[tile(k), :].astype(bf16)

    flushed = [pltpu.make_async_copy(attended, mixed_h, out_sems.at[0])]
    flushed[0].start()
    for copy in loads[6:9]:
        copy.wait()

    @pl.loop(0, tiles)
    def _(k):
        pair_t = kv[tile(k), :].astype(f32)
        other = pltpu.roll(pair_t, HD, 1)
        both = jnp.where(left, pair_t, other)
        keys[tile(k), :] = both.astype(bf16)
        keys_t[:, tile(k)] = both.T[:HD].astype(bf16)
        ones = jnp.where(lane < HD + 2, -1.0, 0.0)
        values[tile(k), :] = jnp.where(left, other, ones).astype(bf16)

    plan = spread(turn(3, len(turns)), 6 * tiles)

    @pl.loop(0, H // 2)
    def _(pr):
        for i in range(tiles):
            count = TILE * (i + 1)
            span = slice(i * TILE, count)
            probs_all, d_scores_all, d_query = [], [], []
            for hh in range(2):
                head = pr * 2 + hh
                scores = turned(keys[0:count, :], queries[head, span, :])
                shift = logsums[head, :, span]
                probs = jnp.exp2(scores[count - TILE :] + mask[...] - shift)
                if i:
                    probs = jnp.concatenate([jnp.exp2(scores[: count - TILE] - shift), probs], axis=0)
                d_probs = turned(values[0:count, :], d_heads[head, span, :])
                d_scores = (probs * d_probs).astype(bf16)
                probs_all.append(probs.astype(bf16))
                d_scores_all.append(d_scores)
                d_query.append(jnp.dot(keys_t[:, 0:count], d_scores, preferred_element_type=f32))
            for acc, parts, other in ((d_values, probs_all, d_heads), (d_keys, d_scores_all, queries)):
                two = jnp.concatenate([other[pr * 2, span, :], other[pr * 2 + 1, span, :]], axis=0)
                acc[0:count, :] += jnp.dot(jnp.concatenate(parts, axis=1), two, preferred_element_type=f32)
            d_q = jnp.concatenate(d_query, axis=0).T * 0.125
            d_q = swapped(d_q, cosine[span, :], -sine[span, :])
            scaled[span, lanes(pr * 2 * HD, 2 * HD)] = d_q.astype(bf16)
            run_at(pr, [(v, plan[v * tiles + i]) for v in range(H // 2)])

    copy_first.wait()
    loads[9].wait()

    @pl.loop(0, tiles)
    def _(k):
        d_key = d_keys[tile(k), :]
        d_key = (d_key + pltpu.roll(d_key, HD, 1)) * (1.0 / LOG2E)
        d_key = swapped(d_key, cosine[tile(k), :], -sine[tile(k), :])
        d_pair[tile(k), :] = jnp.where(left, d_key, pltpu.roll(d_values[tile(k), :], HD, 1)).astype(bf16)
        inputs = tokens[tile(k), :].astype(f32)
        centred = inputs - jnp.mean(inputs, axis=-1, keepdims=True)
        norm = centred * lax.rsqrt(jnp.mean(centred * centred, axis=-1, keepdims=True) + eps_norm)
        both = jnp.concatenate([scaled[tile(k), :], d_pair[tile(k), :]], axis=1)
        d_first = turned(both, columns(packed_w, 0, qkv))
        branch[tile(k), :] = d_first
        second = d_second[tile(k), :]
        for n, value in enumerate((d_first * norm, second * norm, d_first, second)):
            sums[n : n + 1, :] += jnp.sum(value, axis=0, keepdims=True)

    @pl.loop(0, 2)
    def _(k):
        side = ins[:, lanes(k * wide, wide)]
        got = crossed(side, scaled[...]).astype(bf16)
        grads[0][pl.ds(2 * k, 2), :, :, :, :, 0:D] = got.reshape(2, 2, 2, 1, D // 16, D)
        got = crossed(side, d_pair[...]).astype(bf16)
        grads[0][pl.ds(2 * k, 2), :, :, :, :, D:qkv] = got.reshape(2, 2, 2, 1, D // 16, 2 * HD)

    grads[0][:, :, :, :, :, qkv:PACK] = sums[...].T.astype(bf16).reshape(4, 2, 2, 1, D // 16, 128)
    if linked:
        steps = scatter.steps()
        last = [functools.partial(step, len(scatter.pieces) - 1) for step in steps]
    else:
        last = []
    plan = spread(last[1:3], tiles)
    for event in last[:1]:
        event()

    @pl.loop(0, tiles)
    def _(k):
        inputs = tokens[tile(k), :].astype(f32)
        centred = inputs - jnp.mean(inputs, axis=-1, keepdims=True)
        inv_std = lax.rsqrt(jnp.mean(centred * centred, axis=-1, keepdims=True) + eps_norm)
        norm = centred * inv_std
        d_normed = branch[tile(k), :] * small[0:1, :] + d_second[tile(k), :] * small[1:2, :]
        inner = jnp.mean(d_normed * norm, axis=-1, keepdims=True)
        d_inputs = inv_std * (d_normed - jnp.mean(d_normed, axis=-1, keepdims=True) - norm * inner)
        cotan[tile(k), :] = (cotan[tile(k), :].astype(f32) * scale + d_inputs).astype(bf16)
        run_at(k, [(v, plan[v]) for v in range(tiles)])

    flushed.append(pltpu.make_async_copy(cotan, grad_tokens_h, out_sems.at[1]))
    flushed[-1].start()
    for event in last[3:]:
        event()
    if linked:
        for make in scatter.started:
            make().wait_send()
    else:
        for t in range(4):
            flushed.append(pltpu.make_async_copy(grads[t], results[t], out_sems.at[2 + t]))
            flushed[-1].start()
    for copy in flushed:
        copy.wait()


def backward(linked, lines, rows, rows_down, total_rows, tags, subset_w, cosine, sine, tokens, cotan, kept, whole):
    blocks = layout(rows, rows_down)
    f32, bf16 = jnp.float32, jnp.bfloat16
    shapes = [(lines, 2, 2, g, r, k) for g, r, k in blocks]
    own_rows = [r if g == 2 else rows for g, r, k in blocks]
    vmem = pl.BlockSpec(memory_space=pltpu.VMEM)
    anywhere = pl.BlockSpec(memory_space=pl.ANY)
    if linked:
        results = [jax.ShapeDtypeStruct((o, k), f32) for o, (g, r, k) in zip(own_rows, blocks)]
    else:
        results = [jax.ShapeDtypeStruct(shape, bf16) for shape in shapes]
    tall = (SEQ, D)
    scratch = [
        pltpu.VMEM(tall, bf16),
        pltpu.VMEM(tall, bf16),
        pltpu.VMEM((128, D), f32),
        pltpu.VMEM(tall, bf16),
        pltpu.VMEM((H, SEQ, 2 * HD), bf16),
        pltpu.VMEM((SEQ, 2 * HD), bf16),
        pltpu.VMEM(tall, bf16),
        pltpu.VMEM((H, 1, SEQ), f32),
        pltpu.VMEM((2, *tall), bf16),
        pltpu.VMEM((2, *tall), bf16),
        pltpu.VMEM(shapes[0], bf16),
        pltpu.VMEM(shapes[1], bf16),
        pltpu.VMEM((2, *shapes[2][:-1], D), bf16),
        pltpu.VMEM((2, *shapes[3][1:]), bf16),
        pltpu.VMEM(tall, f32),
        pltpu.VMEM(tall, f32),
        pltpu.VMEM(tall, bf16),
        pltpu.VMEM((H, SEQ, 2 * HD), bf16),
        pltpu.VMEM((SEQ, 2 * HD), bf16),
        pltpu.VMEM((HD, SEQ), bf16),
        pltpu.VMEM((SEQ, 2 * HD), bf16),
        pltpu.VMEM((SEQ, 2 * HD), f32),
        pltpu.VMEM((SEQ, 2 * HD), f32),
        pltpu.VMEM((SEQ, 2 * HD), bf16),
        pltpu.VMEM((TILE, TILE), f32),
        pltpu.VMEM((128, D), f32),
    ]
    scratch += [pltpu.VMEM(shape, bf16) for shape in shapes]
    scratch += [pltpu.SemaphoreType.DMA((10,)), pltpu.SemaphoreType.DMA((2, 4)), pltpu.SemaphoreType.DMA((6,))]
    if linked:
        pieces = scatter_pieces(blocks)
        tallest = max(p[2] for p in pieces if p[0] == 3)
        scratch += [pltpu.VMEM((SLOTS, lines, 2, 2, 2, max(tallest, 2 * rows), D // 2), bf16)]
        scratch += [pltpu.VMEM((lines, 2, 2, 1, 2 * rows, PACK // 2), bf16)]
        for lead in ((2, lines), (lines,), (lines - 1,)):
            scratch += [pltpu.VMEM((*lead, g, r, k // 2), bf16) for g, r, k in blocks]
        scratch += [pltpu.VMEM((g, r, k // 2), f32) for g, r, k in blocks]
        scratch += [pltpu.VMEM((o, k // 2), f32) for o, (g, r, k) in zip(own_rows, blocks)]
        scratch += [pltpu.SemaphoreType.DMA((len(pieces), lines + 4))] * 2 + [pltpu.SemaphoreType.REGULAR]
    return pl.pallas_call(
        functools.partial(backward_kernel, lines, rows, blocks, linked, total_rows),
        out_shape=[jax.ShapeDtypeStruct(tall, bf16)] * 2 + results,
        in_specs=[pl.BlockSpec(memory_space=pltpu.SMEM)] + [vmem] * 3 + [anywhere] * 15,
        out_specs=[anywhere] * 2 + [vmem if linked else anywhere] * 4,
        scratch_shapes=scratch,
        compiler_params=pltpu.CompilerParams(
            collective_id=1 if linked else None, has_side_effects=linked, vmem_limit_bytes=63 * 2**20
        ),
        name="backward",
    )(tags, subset_w, cosine, sine, tokens, cotan, *kept, *whole)


def finish_kernel(rows, *refs):
    packed, *rest = refs[:5]
    query, pair, gains, biases, *to = refs[5:]
    query[...] = packed[:, :D]
    pair[...] = packed[:, D : D + 2 * HD]
    turned_back = packed[:, D + 2 * HD :].T
    gains[...] = turned_back[0:2]
    biases[...] = turned_back[2:4]
    for a, b in zip(rest, to):
        b[...] = a[...]


def finish(rows, packed, *rest):
    f32 = jnp.float32
    vmem = pl.BlockSpec(memory_space=pltpu.VMEM)
    shapes = [(rows, D), (rows, 2 * HD), (2, rows), (2, rows)]
    return pl.pallas_call(
        functools.partial(finish_kernel, rows),
        out_shape=[jax.ShapeDtypeStruct(a, f32) for a in shapes] + [jax.ShapeDtypeStruct(a.shape, a.dtype) for a in rest],
        in_specs=[vmem] * (1 + len(rest)),
        out_specs=[vmem] * (4 + len(rest)),
        compiler_params=pltpu.CompilerParams(vmem_limit_bytes=32 * 2**20),
        name="finish",
    )(packed, *rest)


def is_linked(rows):
    return lax.axis_size("dp") >= 4 and lax.axis_size("fsdp") == 4 and rows % 8 == 0


def fetch_weights(query_w, pair_w, out_w, up_w, down_w, gains, biases, tags):
    onehot = (tags[0] == jnp.arange(SUBSETS, dtype=jnp.int32)).astype(jnp.float32)
    own_counts = jnp.where((jnp.arange(query_w.shape[0]) == 0)[:, None], onehot[None, :], 0.0)
    small = jnp.concatenate([gains.T, biases.T, own_counts], axis=1)
    small = jnp.pad(small, ((0, 0), (0, 128 - small.shape[1])))
    packed = jnp.concatenate([query_w, pair_w, small], axis=1)
    return [
        lax.all_gather(a.astype(jnp.bfloat16), ("dp", "fsdp"), axis=0, tiled=True)
        for a in (packed, out_w, up_w, down_w)
    ]


def body(
    tokens,
    w_query,
    w_pair,
    w_attn_out,
    w_up,
    w_down,
    ln_gains,
    ln_biases,
    cotangent,
    subset_tags,
    subset_weights,
):
    cosine, sine = tables()
    linked = is_linked(w_query.shape[0])
    shards = (w_query, w_pair, w_attn_out, w_up, w_down, ln_gains, ln_biases, subset_tags)
    total_rows = lax.axis_size("dp") * lax.axis_size("fsdp")
    if linked:
        lines, rows, rows_down = lax.axis_size("dp") // 2, w_query.shape[0], w_down.shape[0]
    else:
        lines, rows, rows_down = 4, D // 32, 4 * D // 32
        shards = fetch_weights(*shards)
    kept, whole = forward(linked, lines, rows, rows_down, tokens, cosine, sine, shards)
    subset_w = subset_weights.reshape(1, SUBSETS)
    mixed, grad_tokens, packed_g, out_g, up_g, down_g = backward(
        linked, lines, rows, rows_down, total_rows, subset_tags, subset_w, cosine, sine, tokens, cotangent, kept, whole
    )
    if not linked:
        packed_g, out_g, up_g, down_g = [
            lax.psum_scatter(
                g.astype(jnp.float32).reshape(-1, g.shape[-1]), ("dp", "fsdp"), scatter_dimension=0, tiled=True
            )
            for g in (packed_g, out_g, up_g, down_g)
        ]
    query_g, pair_g, gains_g, biases_g, out_g, up_g, down_g, grad_tokens = finish(
        w_query.shape[0], packed_g, out_g, up_g, down_g, grad_tokens
    )
    return mixed, grad_tokens, query_g, pair_g, out_g, up_g, down_g, gains_g, biases_g


def solution(mesh):
    in_specs = (
        P(("dp", "fsdp"), None),
        P(("dp", "fsdp"), None),
        P(("dp", "fsdp"), None),
        P(("dp", "fsdp"), None),
        P(("dp", "fsdp"), None),
        P(("dp", "fsdp"), None),
        P(None, ("dp", "fsdp")),
        P(None, ("dp", "fsdp")),
        P(("dp", "fsdp"), None),
        P(("dp", "fsdp")),
        P(),
    )
    out_specs = (
        P(("dp", "fsdp"), None),
        P(("dp", "fsdp"), None),
        P(("dp", "fsdp"), None),
        P(("dp", "fsdp"), None),
        P(("dp", "fsdp"), None),
        P(("dp", "fsdp"), None),
        P(("dp", "fsdp"), None),
        P(None, ("dp", "fsdp")),
        P(None, ("dp", "fsdp")),
    )
    return jax.shard_map(body, mesh=mesh, in_specs=in_specs, out_specs=out_specs, check_vma=False)
```

time: 352 us -> 221 us (0.63)
  matrix products: 117 us -> 0 us
  Pallas kernels: 161 us -> 210 us
  other arithmetic: 40.5 us -> 0 us
  local copies, waits for them, and re-layouts: 23.6 us -> 7.05 us
    dot_general x22 -> x0, matrix products: 117 us -> none  [the longest x2 27.7 us: body(): jnp.einsum('rqhd,rkd->rhqk', d_attended[:, block_start:block_stop], value...]
    pallas_call x1 -> x2, Pallas kernels: 72.1 us -> 121 us  [the longest x1 120 us: backward(): pl.pallas_call(functools.partial(backward_kernel, lines, rows, blocks, li...]
    another operation x3 -> x0, other arithmetic: 24.5 us -> none
    reduce_sum x4 -> x0, other arithmetic: 5.31 us -> none  [the longest x1 2.01 us: body(): jnp.mean(centred * centred, axis=-1, keepdims=True) + eps_norm]
    slice x6 -> x0, local copies, waits for them, and re-layouts: 4.97 us -> none  [the longest x1 1.52 us: body(): packed_g[:, :D]]
    concatenate x3 -> x0, local copies, waits for them, and re-layouts: 3.68 us -> none  [the longest x1 1.92 us: tables(): sine = jnp.concatenate([-sin_t, sin_t, rest] * 2, axis=1)]
    unnamed x87 -> x13, local copies, waits for them, and re-layouts: 8.88 us -> 7.05 us
where the time goes in v3:
time: 221 us; the launch traced here: 218 us
  Pallas kernels  210 us (95%)
  local copies, waits for them, and re-layouts  7.05 us (3%)
    pallas_call x1, Pallas kernels, backward(): pl.pallas_call(functools.partial(backward_kernel, lines, rows, blocks, li...  120 us
    pallas_call x1, Pallas kernels, forward(): pl.pallas_call(functools.partial(forward_kernel, lines, rows, blocks, lin...  88.6 us
    unnamed x13, local copies, waits for them, and re-layouts  7.05 us

profile of v3, /device:TPU:25, one launch (start us, length us, event | category | flops | bytes accessed | tf_op | source)
XLA Modules:
  0.0 218.2 jit_solution(12545867827087071084)
XLA Ops:
  1.3 88.6 %forward.1 = (f32[128,768]{1,0:T(8,128)}, bf16[1024,768]{1,0:T(8,128)(2,1)}, bf16[1024,768]{1,0:T(8,128)(2,1)}, bf16[12,1024,128]{2,1,0:T(8,128)(2,1)}, bf16[102...) custom-call(bf16[1024,768]{1,0:T(8,128)(2,1)} %refs_4_.3, ...), custom_call_target="tpu_custom_call" | custom-call | tf_op jit(solution)/shard_map/forward/pallas_call | solution.py:387
  89.9 119.8 %backward.1 = (bf16[1024,768]{1,0:T(8,128)(2,1)}, bf16[1024,768]{1,0:T(8,128)(2,1)}, f32[24,1024]{1,0:T(8,128)}, f32[24,768]{1,0:T(8,128)}, f32[24,3072]{1,0:T(8,128)}, /*index=5*/f32[96,768]{1,0:T(8,128)}) custom-call(s32[1]{0:T(128)S(6)} %copy.23.refs_10_.refs_0_, f32[1,22]{1,0:T(1,128)} %bitcast.1, f32[1024,128]{1,0:T(8,128)} %constant.4.clone.refs_1_.refs_2_, ...), custom_call_target="tpu_custom_call" | custom-call | tf_op jit(solution)/shard_map/backward/pallas_call | solution.py:882
  209.7 0.0 copy-start
  209.7 1.4 copy-done
  211.1 0.0 copy-start.1
  211.1 1.0 copy-done.1
  212.1 0.0 copy-start.2
  212.1 1.0 copy-done.2
  213.0 0.0 copy-start.3
  213.0 0.9 copy-done.3
  213.9 0.0 copy-start.4
  213.9 0.9 copy-done.4
  214.8 0.0 copy-start.5
  214.8 1.4 finish.1
  216.2 0.8 copy-done.5
  217.0 1.1 copy.24
Async XLA Ops:
  209.7 1.4 copy-start
  211.1 1.0 copy-start.1
  212.1 1.0 copy-start.2
  213.0 0.9 copy-start.3
  213.9 0.9 copy-start.4
  214.8 2.2 %copy-start.5 = (bf16[1024,768]{1,0:T(8,128)(2,1)S(1)}, bf16[1024,768]{1,0:T(8,128)(2,1)}, u32[]{:S(2)}) copy-start(bf16[1024,768]{1,0:T(8,128)(2,1)} %get-tuple-element.72) | copy-start | bytes 4718596

commit v4 on v0

v4 whole, which is shorter than its diff:
```python
import functools

import jax
import jax.numpy as jnp
import numpy as np
from jax import lax
from jax.experimental import pallas as pl
from jax.experimental.pallas import tpu as pltpu
from jax.sharding import PartitionSpec as P

D = 768
H = 12
HD = 64
ROT = 16
SUBSETS = 22
SEQ = 1024
PACK = 1024
TILE = 256
LOG2E = 1.4426950408889634
PAIR = 3 * 128
SMALL = 256
GATHER_STARTS = (0.0, 0.0, 2.0, 7.0, 16.0, 21.0, 30.0, 35.0)
GATHER_LAGS = (0.0, 8.0, 16.0, 18.0)
SCATTER_LAGS = (0.0, 2.0, 8.0, 14.0, 20.0, 23.0)
PROJECT_STEPS = (1.25,) * 4
ATTEND_STEPS = (1.2, 2.8) * 6
OUTWARD_STEPS = (1.2,) * 4 + (0.85,) * 2
CLOSE_STEPS = (0.7,) * 4 + (1.0,)
CHUNK_STEPS = (1.6,) * 4 + (0.7,) * 4
TOKEN_STEPS = (0.7,) * 4
MESH = pl.DeviceIdType.MESH


eps_norm = 1e-05


def place_of(p):
    return (p % 2) * (PACK // 2) + (p // 2) * 2 * HD


def place():
    dp, fs = lax.axis_index("dp"), lax.axis_index("fsdp")
    return dp // 2, dp % 2, fs // 2, fs % 2


def device(z, x, y, c):
    return (z * 2 + x, y * 2 + c)


def partners():
    z, x, y, c = place()
    xa, ya = jnp.where(c == 0, 1 - x, x), jnp.where(c == 0, y, 1 - y)
    xb, yb = jnp.where(c == 0, x, 1 - x), jnp.where(c == 0, 1 - y, y)
    return xa, ya, xb, yb


def greet(lines):
    z, x, y, c = place()
    barrier = pltpu.get_barrier_semaphore()
    others = [device(lax.rem(z + d, lines), x, y, c) for d in range(1, lines)]
    others += [device(z, 1 - x, y, c), device(z, x, 1 - y, c), device(z, x, y, 1 - c)]
    for other in others:
        pl.semaphore_signal(barrier, inc=1, device_id=other, device_id_type=MESH)
    pl.semaphore_wait(barrier, len(others))


def remote(src, dst, send, recv, where):
    return pltpu.make_async_remote_copy(
        src_ref=src, dst_ref=dst, send_sem=send, recv_sem=recv, device_id=where, device_id_type=MESH
    )


def layout(rows, rows_down):
    return [(1, 2 * rows, PACK), (1, 2 * rows, D), (1, 2 * rows, 4 * D), (2, rows_down, D), (1, 2 * rows, SMALL)]


HALF = (PACK // 2, D // 2, D // 2, D // 2, SMALL // 2)


def lanes(start, size):
    return pl.ds(pl.multiple_of(start, 128), size)


def part(piece, ref, z, x, y, half):
    t, r0, nr, c0, _, w = piece
    return ref.at[z, x, y, :, pl.ds(r0, nr), lanes(half * HALF[t] + c0, w)]


def gather_pieces(blocks):
    r0, r1, r2, r3 = (r for _, r, _ in blocks[:4])
    w, half = D // 2, r3 // 2 // 16 * 16
    ups = [(2, 0, r2, 2 * w * k, w * k, w) for k in range(4)]
    downs = [(3, 0, half, 0, 0, w), (3, half, r3 - half, 0, 0, w)]
    return [(0, 0, r0, 0, 0, PACK // 2), (1, 0, r1, 0, 0, w), ups[0], downs[0], ups[1], downs[1], ups[2], ups[3]]


class Gather:
    def __init__(self, lines, rows, blocks, sources, stages, whole, sems):
        self.lines, self.rows, self.blocks = lines, rows, blocks
        self.sources, self.stages, self.whole = sources, stages, whole
        self.swap_send, self.swap_recv, self.send, self.recv = sems
        self.pieces = gather_pieces(blocks)
        self.z, self.x, self.y, self.c = place()
        self.xa, self.ya, self.xb, self.yb = partners()
        self.sibling = device(self.z, self.x, self.y, 1 - self.c)
        self.started = []

    def go(self, p, make):
        make().start()
        self.started.append((self.pieces[p][0], make))

    def stage_rows(self, p, core):
        t, r0, nr, _, l0, w = self.pieces[p]
        if self.blocks[t][0] == 2:
            return self.stages[t].at[core, pl.ds(r0, nr), pl.ds(l0, w)]
        return self.stages[t].at[0, pl.ds(pl.multiple_of(core * self.rows, 8), self.rows), pl.ds(l0, w)]

    def source(self, p):
        t, r0, nr, c0, _, w = self.pieces[p]
        return self.sources[t].at[pl.ds(r0, nr) if self.blocks[t][0] == 2 else slice(None)], c0, w

    def swap(self, p):
        source, c0, w = self.source(p)
        mine = source.at[:, lanes((1 - self.c) * HALF[self.pieces[p][0]] + c0, w)]
        return remote(mine, self.stage_rows(p, self.c), self.swap_send.at[p], self.swap_recv.at[p], self.sibling)

    def block(self, p, d, x, y):
        z = lax.rem(self.z + self.lines - d, self.lines)
        return part(self.pieces[p], self.whole[self.pieces[p][0]], z, x, y, self.c)

    def direct(self, p, d, back=0):
        block = self.block(p, back, self.x, self.y)
        where = device(lax.rem(self.z + d, self.lines), self.x, self.y, self.c)
        return remote(block, block, self.send.at[p, d - 1], self.recv.at[p, d - 1], where)

    def to_a(self, p, d, x, y):
        block, k = self.block(p, d, x, y), self.lines - 1 + d
        return remote(block, block, self.send.at[p, k], self.recv.at[p, k], device(self.z, self.xa, self.ya, self.c))

    def to_b(self, p, d, x, y, second=0):
        block, k = self.block(p, d, x, y), self.lines * (2 + second) - 1 + d
        return remote(block, block, self.send.at[p, k], self.recv.at[p, k], device(self.z, self.xb, self.yb, self.c))

    def share(self, p, k, x, y, half):
        column = part(self.pieces[p], self.whole[self.pieces[p][0]], slice(None), x, y, half)
        k = 4 * self.lines - 1 + k
        return remote(column, column, self.send.at[p, k], self.recv.at[p, k], self.sibling)

    def own(self, p):
        x, y = self.x, self.y
        self.go(p, lambda: self.to_a(p, 0, x, y))
        self.go(p, lambda: self.to_b(p, 0, x, y))

    def begin(self, ahead):
        for p in range(len(self.pieces)):
            self.go(p, functools.partial(self.swap, p))
        for p, piece in enumerate(self.pieces):
            t, r0, nr, c0, l0, w = piece
            source, _, _ = self.source(p)
            kept = jnp.where(self.c == 0, source[:, c0 : c0 + w], source[:, HALF[t] + c0 : HALF[t] + c0 + w])
            self.stage_rows(p, self.c)[...] = kept
            self.swap(p).wait_recv()
            held = self.stages[t][:, r0 : r0 + nr, l0 : l0 + w]
            self.block(p, 0, self.x, self.y)[...] = held.astype(jnp.bfloat16)
            for d in range(1, self.lines):
                self.go(p, functools.partial(self.direct, p, d))
            if p < ahead:
                self.own(p)
        self.ahead = ahead

    def first(self, p):
        x, y, c = self.x, self.y, self.c
        if p >= self.ahead:
            self.own(p)
        for d in range(1, self.lines):
            self.direct(p, d, back=d).wait_recv()
            self.go(p, functools.partial(self.to_a, p, d, x, y))
            self.go(p, functools.partial(self.to_b, p, d, x, y))
        self.go(p, lambda: self.share(p, 0, x, y, c))

    def second(self, p):
        for d in range(self.lines):
            self.to_a(p, d, self.xa, self.ya).wait_recv()
            self.go(p, functools.partial(self.to_b, p, d, self.xa, self.ya, 1))
        self.go(p, lambda: self.share(p, 1, self.xa, self.ya, self.c))

    def third(self, p):
        x, y = self.x, self.y
        for d in range(self.lines):
            self.to_b(p, d, self.xb, self.yb).wait_recv()
        self.go(p, lambda: self.share(p, 2, self.xb, self.yb, self.c))
        for d in range(self.lines):
            self.to_b(p, d, 1 - x, 1 - y, 1).wait_recv()
        self.go(p, lambda: self.share(p, 3, 1 - x, 1 - y, self.c))

    def fourth(self, p):
        x, y, c = self.x, self.y, 1 - self.c
        for k, sx, sy in ((0, x, y), (1, self.xb, self.yb), (2, self.xa, self.ya), (3, 1 - x, 1 - y)):
            self.share(p, k, sx, sy, c).wait_recv()

    def events(self):
        steps = (self.first, self.second, self.third, self.fourth)
        urgent = [(0, 0), (0, 1), (1, 0), (2, 0), (3, 0)]
        timed = []
        for p in range(1, len(self.pieces)):
            for k, lag in enumerate(GATHER_LAGS):
                if (k, p) not in urgent:
                    timed.append((GATHER_STARTS[p] + lag, len(timed), functools.partial(steps[k], p)))
        return [functools.partial(steps[k], p) for k, p in urgent], timed

    def sent(self, t):
        for kind, make in self.started:
            if kind == t:
                make().wait_send()


def deal(timed, times):
    plan = [[] for _ in range(len(times) + 1)]
    for when, _, event in sorted(timed, key=lambda e: e[:2]):
        plan[next((k for k, t in enumerate(times) if t >= when), len(times))].append(event)
    return plan


def ends(start, *steps):
    out = []
    for step in steps:
        start += step
        out.append(start)
    return out


def run_at(index, values):
    for value, events in values:
        if events:

            @pl.when(index == value)
            def _(events=events):
                for event in events:
                    event()


def columns(ref, start, size):
    return ref[:, :, :, :, :, pl.ds(start, size)].reshape(-1, size)


def turned(a, b):
    return lax.dot_general(a, b, (((1,), (1,)), ((), ())), preferred_element_type=jnp.float32)


def swapped(block, cosine, sine):
    lane = lax.broadcasted_iota(jnp.int32, block.shape, 1)
    other = jnp.where(lane % 16 < 8, pltpu.roll(block, 120, 1), pltpu.roll(block, 8, 1))
    return block * cosine + other * sine


def tables():
    half = ROT // 2
    inverse = np.float32(10000.0) ** (-(np.arange(half, dtype=np.float32) * 2) / ROT)
    phase = np.arange(SEQ, dtype=np.float32)[:, None] * inverse.astype(np.float32)[None, :]
    cos_t, sin_t = np.cos(phase.astype(np.float64)), np.sin(phase.astype(np.float64))
    rest = np.zeros((SEQ, HD - ROT))
    cosine = np.concatenate([cos_t, cos_t, rest + 1.0] * 2, axis=1)
    sine = np.concatenate([-sin_t, sin_t, rest] * 2, axis=1)
    return jnp.asarray(cosine.astype(np.float32)), jnp.asarray(sine.astype(np.float32))


def scatter_pieces(blocks):
    r0, r1, r2, r3, r4 = (r for _, r, _ in blocks)
    w, q = D // 2, PACK // 4
    pieces = [(1, 0, r1, 0, 0, w), (0, 0, r0, 0, 0, q), (0, 0, r0, q, q, q)]
    for k in range(4):
        pieces += [(3, 0, r3, 0, 0, w), (2, 0, r2, 2 * w * k, w * k, w)]
    return pieces + [(4, 0, r4, 0, 0, SMALL // 2)]


SLOTS = 2


class Scatter:
    def __init__(self, lines, rows, blocks, grads, outs, buffers, sems):
        self.lines, self.rows, self.blocks = lines, rows, blocks
        self.grads, self.outs = grads, outs
        kinds = len(blocks)
        self.near, self.from_b, self.from_a, self.from_z, self.total, self.last = (
            buffers[kinds * k : kinds * (k + 1)] for k in range(6)
        )
        self.send, self.recv, self.credit = sems
        self.pieces = scatter_pieces(blocks)
        self.only = [(p - 3) // 2 if piece[0] == 3 else None for p, piece in enumerate(self.pieces)]
        self.z, self.x, self.y, self.c = place()
        self.xa, self.ya, self.xb, self.yb = partners()
        self.sibling = device(self.z, self.x, self.y, 1 - self.c)
        self.started = []

    def go(self, make):
        make().start()
        self.started.append((None, make))

    def where(self, p, body):
        if self.only[p] is None:
            body()
        else:
            pl.when(self.z == self.only[p])(body)

    def every(self, p):
        return slice(None) if self.only[p] is None else pl.ds(self.only[p], 1)

    def planes(self, p, body):
        if self.only[p] is None:
            pl.loop(0, self.lines)(body)
        else:
            body(self.only[p])

    def cut(self, p, ref, *lead):
        t, r0, nr, _, l0, w = self.pieces[p]
        return ref[t].at[(*lead, slice(None), pl.ds(r0, nr), pl.ds(l0, w))]

    def grad(self, p, z, x, y, half=None):
        half = self.c if half is None else half
        return part(self.pieces[p], self.grads[self.pieces[p][0]], z, x, y, half)

    def slot(self, p):
        t, _, _, _, l0, w = self.pieces[p]
        return {0: l0 // w, 1: 0, 2: l0 // w % SLOTS, 3: (p - 3) // 2 % SLOTS, 4: 0}[t]

    def near_copy(self, p):
        every = slice(None)
        mine = self.grad(p, self.every(p), every, every, 1 - self.c)
        near = self.near[self.pieces[p][0]].at[self.slot(p)]
        return remote(mine, near, self.send.at[p, 0], self.recv.at[p, 0], self.sibling)

    def b_copy(self, p, k):
        at = (self.xb, self.yb) if k == 0 else (1 - self.x, 1 - self.y)
        return remote(
            self.grad(p, self.every(p), *at),
            self.cut(p, self.from_b, k, self.every(p)),
            self.send.at[p, 1 + k],
            self.recv.at[p, 1 + k],
            device(self.z, self.xb, self.yb, self.c),
        )

    def a_copy(self, p):
        return remote(
            self.grad(p, self.every(p), self.xa, self.ya),
            self.cut(p, self.from_a, self.every(p)),
            self.send.at[p, 3],
            self.recv.at[p, 3],
            device(self.z, self.xa, self.ya, self.c),
        )

    def z_copy(self, p, d):
        other = lax.rem(self.z + d, self.lines)
        return remote(
            self.grad(p, other, self.x, self.y),
            self.cut(p, self.from_z, d - 1),
            self.send.at[p, 3 + d],
            self.recv.at[p, 3 + d],
            device(other, self.x, self.y, self.c),
        )

    def last_copy(self, p):
        t, r0, nr, _, l0, w = self.pieces[p]
        if self.blocks[t][0] == 2:
            src = self.total[t].at[1 - self.c, pl.ds(r0, nr), pl.ds(l0, w)]
            dst = self.last[t].at[pl.ds(r0, nr), pl.ds(l0, w)]
        else:
            away = pl.ds(pl.multiple_of((1 - self.c) * self.rows, 8), self.rows)
            src = self.total[t].at[0, away, pl.ds(l0, w)]
            dst = self.last[t].at[:, pl.ds(l0, w)]
        k = 3 + self.lines
        return remote(src, dst, self.send.at[p, k], self.recv.at[p, k], self.sibling)

    def uses(self, p):
        t = self.pieces[p][0]
        if t not in (2, 3):
            return False, False
        return p - 2 * SLOTS >= 3, p + 2 * SLOTS <= 10

    def first(self, p):
        if self.uses(p)[0]:
            pl.semaphore_wait(self.credit.at[self.pieces[p][0] - 2], 1)
        self.go(lambda: self.near_copy(p))

    def second(self, p):
        f32 = jnp.float32
        self.near_copy(p).wait_recv()
        near = self.near[self.pieces[p][0]].at[self.slot(p)]

        def add(k):
            for x in range(2):
                for y in range(2):
                    kept = self.grad(p, k, x, y)
                    got = near[0 if self.only[p] is not None else k, x, y]
                    kept[...] = (kept[...].astype(f32) + got.astype(f32)).astype(jnp.bfloat16)

        self.planes(p, add)
        if self.uses(p)[1]:
            credit = self.credit.at[self.pieces[p][0] - 2]
            pl.semaphore_signal(credit, inc=1, device_id=self.sibling, device_id_type=MESH)
        self.go(lambda: self.b_copy(p, 1))
        self.go(lambda: self.b_copy(p, 0))

    def third(self, p):
        self.b_copy(p, 1).wait_recv()

        def add(k):
            kept, got = self.grad(p, k, self.xa, self.ya), self.cut(p, self.from_b, 1, k)
            kept[...] = (kept[...].astype(jnp.float32) + got[...].astype(jnp.float32)).astype(jnp.bfloat16)

        self.planes(p, add)
        self.go(lambda: self.a_copy(p))

    def mine(self, p, k):
        got = self.cut(p, self.from_b, 0, k)[...].astype(jnp.float32) + self.cut(p, self.from_a, k)[...].astype(jnp.float32)
        return self.grad(p, k, self.x, self.y)[...].astype(jnp.float32) + got

    def fourth(self, p):
        self.b_copy(p, 0).wait_recv()
        self.a_copy(p).wait_recv()
        q = self.only[p]

        def send():
            for d in range(1, self.lines):
                self.go(functools.partial(self.z_copy, p, d))

        def round_off(k):
            self.grad(p, k, self.x, self.y)[...] = self.mine(p, k).astype(jnp.bfloat16)

        if q is None:

            @pl.loop(1, self.lines)
            def _(d):
                round_off(lax.rem(self.z + d, self.lines))

            send()
        else:

            def to_owner():
                return self.z_copy(p, lax.rem(q - self.z + self.lines, self.lines))

            @pl.when(self.z != q)
            def _():
                round_off(q)
                to_owner().start()

            self.started.append((lambda: self.z != q, to_owner))

        def keep():
            self.cut(p, self.total)[...] = self.mine(p, self.z if q is None else q)

        self.where(p, keep)

    def fifth(self, p):
        def body():
            for d in range(1, self.lines):
                self.z_copy(p, d).wait_recv()
            total = self.cut(p, self.total)
            acc = total[...]
            for d in range(1, self.lines):
                acc = acc + self.cut(p, self.from_z, d - 1)[...].astype(jnp.float32)
            total[...] = acc
            self.last_copy(p).start()

        self.where(p, body)
        q = self.only[p]
        self.started.append((None if q is None else lambda: self.z == q, lambda: self.last_copy(p)))

    def sixth(self, p):
        t, r0, nr, c0, l0, w = self.pieces[p]

        def body():
            self.last_copy(p).wait_recv()
            if self.blocks[t][0] == 2:
                kept = self.total[t][self.c, r0 : r0 + nr, l0 : l0 + w]
                got = self.last[t][r0 : r0 + nr, l0 : l0 + w]
                to = slice(r0, r0 + nr)
            else:
                kept = self.total[t][0, pl.ds(pl.multiple_of(self.c * self.rows, 8), self.rows), l0 : l0 + w]
                got = self.last[t][:, l0 : l0 + w]
                to = slice(None)
            h = HALF[t] + c0
            self.outs[t][to, c0 : c0 + w] = jnp.where(self.c == 0, kept, got)
            self.outs[t][to, h : h + w] = jnp.where(self.c == 0, got, kept)

        self.where(p, body)

    def steps(self):
        return [self.first, self.second, self.third, self.fourth, self.fifth, self.sixth]

    def timed(self, p, start):
        return [(start + lag, p, functools.partial(step, p)) for step, lag in zip(self.steps(), SCATTER_LAGS)]

    def finish(self):
        for condition, make in self.started:
            if condition is None:
                make().wait_send()
            else:

                @pl.when(condition())
                def _(make=make):
                    make().wait_send()


def crossed(a, b):
    return lax.dot_general(a, b, (((0,), (0,)), ((), ())), preferred_element_type=jnp.float32)


def layer_kernel(lines, rows, blocks, linked, total_rows, *refs):
    f32, bf16 = jnp.float32, jnp.bfloat16
    tags, subset_w, tokens_h, cotan_h, cosine_h, sine_h = refs[:6]
    given, refs = (refs[6:13], refs[13:]) if linked else (refs[6:10], refs[10:])
    mixed_h, grad_tokens_h, *results = refs[:7]
    tokens, cotan, cosine, sine, normed, small, first_in, second_in, queries, pool, keys, keys_t = refs[7:19]
    values, values_t, attended, logsums, scaled, packed_d, mask, sums, d_keys, d_values, branch, d_second = refs[19:31]
    whole, grad_packed, grad_small, load_sems, out_sems = refs[31:35], refs[35], refs[36], refs[37], refs[38]
    refs = refs[39:]
    grads = [grad_packed, *whole[1:], grad_small]
    tiles, wide, qkv = SEQ // TILE, D // 2, D + 2 * HD

    def tile(k):
        return pl.ds(pl.multiple_of(k * TILE, TILE), TILE)

    pairs = [(tokens_h, tokens), (cosine_h, cosine), (sine_h, sine), (cotan_h, cotan)]
    if not linked:
        pairs += list(zip(given, whole))
    loads = [pltpu.make_async_copy(a, b, load_sems.at[k]) for k, (a, b) in enumerate(pairs)]
    for copy in loads:
        copy.start()
    if linked:
        query, pair, out, up, down, gains, biases = given
        packed, stages, square, gather_sems, refs = refs[0], refs[1:5], refs[5], refs[6:10], refs[10:]
        for p in range(H // 2):
            packed[:, place_of(p) : place_of(p) + 2 * HD] = query[:, 2 * HD * p : 2 * HD * (p + 1)]
        packed[:, PAIR : PAIR + 2 * HD] = pair[...]
        square[...] = jnp.zeros_like(square)
        square[0:2, 0:rows] = gains[...]
        square[2:4, 0:rows] = biases[...]
        spot = lax.broadcasted_iota(jnp.int32, (rows, 128), 1) == tags[0] + 4
        spot = jnp.where(lax.broadcasted_iota(jnp.int32, (rows, 128), 0) == 0, spot.astype(f32), 0.0)
        packed[:, qkv:] = square[...].T[:rows] + spot
        greet(lines)
        gather = Gather(lines, rows, blocks, [packed, out, up, down], stages, whole, gather_sems)
        scatter = Scatter(lines, rows, blocks, grads, results, refs[:30], refs[30:33])
        gather.begin(2)
        urgent, timed = gather.events()
    else:
        urgent, timed = [], []
    packed_w, out_w, up_w, down_w = whole

    steps = (PROJECT_STEPS, ATTEND_STEPS, OUTWARD_STEPS, ATTEND_STEPS, CLOSE_STEPS, CHUNK_STEPS * 4, TOKEN_STEPS)
    starts, slots = [0], [0]
    for part_steps in steps:
        starts.append(starts[-1] + sum(part_steps))
        slots.append(slots[-1] + len(part_steps))
    if linked:
        timed += scatter.timed(0, starts[3])
        ready = starts[3] + 4 * sum(ATTEND_STEPS[:2])
        timed += [(ready - 0.01, 100, lambda: query_grads(0, PACK // 4))] + scatter.timed(1, ready)
        timed += scatter.timed(2, starts[5])
        for q in range(4):
            start = starts[5] + q * sum(CHUNK_STEPS) + sum(CHUNK_STEPS[:6])
            timed += scatter.timed(3 + 2 * q, start) + scatter.timed(4 + 2 * q, start + sum(CHUNK_STEPS[6:]))
        timed += scatter.timed(11, starts[6])
    plan = deal(timed, ends(0.0, *(step for part_steps in steps for step in part_steps)))

    def slot(section, index, values):
        run_at(index, [(v, plan[slots[section] + v]) for v in values])

    row = lax.broadcasted_iota(jnp.int32, (TILE, TILE), 0)
    column = lax.broadcasted_iota(jnp.int32, (TILE, TILE), 1)
    mask[...] = jnp.where(row <= column, 0.0, -1e30)
    sums[...] = jnp.zeros_like(sums)
    d_keys[...] = jnp.zeros_like(d_keys)
    d_values[...] = jnp.zeros_like(d_values)
    lane = lax.broadcasted_iota(jnp.int32, (TILE, 2 * HD), 1)
    left = lane < HD
    loads[0].wait()

    @pl.loop(0, tiles)
    def _(k):
        inputs = tokens[tile(k), :].astype(f32)
        centred = inputs - jnp.mean(inputs, axis=-1, keepdims=True)
        normed[tile(k), :] = centred * lax.rsqrt(jnp.mean(centred * centred, axis=-1, keepdims=True) + eps_norm)

    for copy in loads[1:]:
        copy.wait()
    for event in urgent:
        event()
    small[...] = columns(packed_w, qkv, 128).astype(f32).T

    @pl.loop(0, tiles)
    def _(k):
        norm = normed[tile(k), :]
        a1 = (norm * small[0:1, :] + small[2:3, :]).astype(bf16)
        first_in[tile(k), :] = a1
        second_in[tile(k), :] = (norm * small[1:2, :] + small[3:4, :]).astype(bf16)
        mixed = jnp.dot(a1, columns(packed_w, 0, qkv), preferred_element_type=f32)
        cos_t, sin_t = cosine[tile(k), :], sine[tile(k), :]
        for p in range(H // 2):
            turn = swapped(mixed[:, place_of(p) : place_of(p) + 2 * HD], cos_t, sin_t).astype(bf16).astype(f32)
            turn = turn * (LOG2E / 8)
            high = turn.astype(bf16).astype(f32)
            low = turn - high
            queries[2 * p, tile(k), :] = jnp.where(left, high, pltpu.roll(low, HD, 1)).astype(bf16)
            queries[2 * p + 1, tile(k), :] = jnp.where(left, pltpu.roll(high, HD, 1), low).astype(bf16)
        pair_t = mixed[:, PAIR : PAIR + 2 * HD]
        pair_t = jnp.where(left, swapped(pair_t, cos_t, sin_t), pair_t).astype(bf16).astype(f32)
        other = pltpu.roll(pair_t, HD, 1)
        both = jnp.where(left, pair_t, other)
        keys[tile(k), :] = both.astype(bf16)
        keys_t[:, tile(k)] = both.T[:HD].astype(bf16)
        values[tile(k), :] = jnp.where(left, other, jnp.where(lane < HD + 2, -1.0, 0.0)).astype(bf16)
        values_t[:, tile(k)] = jnp.where(left, other, jnp.where(lane == HD, 1.0, 0.0)).T.astype(bf16)
        slot(0, k, range(tiles))

    @pl.loop(0, H // 2)
    def _(pr):
        for i in range(tiles):
            count = TILE * (i + 1)
            heads = []
            for hh in range(2):
                head = pr * 2 + hh
                scores = turned(keys[0:count, :], queries[head, i * TILE : count, :])
                last = scores[count - TILE :] + mask[...]
                peak = jnp.max(last, axis=0, keepdims=True)
                if i:
                    peak = jnp.maximum(peak, jnp.max(scores[: count - TILE], axis=0, keepdims=True))
                probs = jnp.exp2(last - peak).astype(bf16)
                if i:
                    probs = jnp.concatenate([jnp.exp2(scores[: count - TILE] - peak).astype(bf16), probs], axis=0)
                got = jnp.dot(values_t[:, 0:count], probs, preferred_element_type=f32)
                total = got[HD : HD + 1]
                heads.append(got[:HD] * (1.0 / total))
                logsums[head, :, i * TILE : count] = peak + jnp.log2(total)
            both = jnp.concatenate(heads, axis=0).T
            attended[i * TILE : count, lanes(pr * 2 * HD, 2 * HD)] = both.astype(bf16)
            if i % 2:
                slot(1, pr * 2 + i // 2, range(i // 2, 2 * (H // 2), 2))

    kind = lax.broadcasted_iota(jnp.int32, (128, D), 0)
    count = jnp.sum(jnp.where(kind == tags[0] + 4, small[...], 0.0), keepdims=True)
    subset = lax.broadcasted_iota(jnp.int32, subset_w.shape, 1)
    weight = jnp.sum(jnp.where(subset == tags[0], subset_w[...], 0.0), keepdims=True)
    scale = weight / count * (total_rows / SUBSETS)

    @pl.loop(0, tiles)
    def _(k):
        grad_out = (cotan[tile(k), :].astype(f32) * scale).astype(bf16)
        scaled[tile(k), :] = grad_out
        heads = attended[tile(k), :]
        out_m = out_w[...].reshape(D, D)
        branch[tile(k), :] = tokens[tile(k), :].astype(f32) + jnp.dot(heads, out_m, preferred_element_type=f32)
        d_heads_t = turned(grad_out, out_m).astype(bf16).astype(f32)
        for p in range(H // 2):
            block = d_heads_t[:, 2 * HD * p : 2 * HD * (p + 1)]
            product = block * heads[:, 2 * HD * p : 2 * HD * (p + 1)].astype(f32)
            for hh, (mine, there) in enumerate(((left, block), (~left, pltpu.roll(block, HD, 1)))):
                delta = jnp.sum(jnp.where(mine, product, 0.0), axis=1, keepdims=True)
                high = delta.astype(bf16).astype(f32)
                extra = jnp.where(lane == HD, high, jnp.where(lane == HD + 1, delta - high, 0.0))
                pool[2 * p + hh, tile(k), :] = jnp.where(left, there, extra).astype(bf16)
        slot(2, k, range(tiles))

    if linked:
        gather.sent(1)

    @pl.loop(0, 2)
    def _(k):
        got = crossed(attended[:, lanes(k * wide, wide)], scaled[...]).astype(bf16)
        grads[1][pl.ds(2 * k, 2)] = got.reshape(2, 2, 2, 1, D // 16, D)
        slot(2, tiles + k, range(tiles, tiles + 2))

    def query_grads(start, stop):
        for span in (slice(start, stop), slice(PACK // 2 + start, min(PACK // 2 + stop, qkv))):
            for k in range(2):
                got = crossed(first_in[:, k * wide : (k + 1) * wide], packed_d[:, span]).astype(bf16)
                grad_packed[2 * k : 2 * k + 2, :, :, :, :, span] = got.reshape(2, 2, 2, 1, D // 16, -1)

    @pl.loop(0, H // 2)
    def _(pr):
        for i in range(tiles):
            count = TILE * (i + 1)
            span = slice(i * TILE, count)
            probs_all, d_scores_all, d_query, ours = [], [], [], []
            d_out = [pool[pr * 2, span, :], pool[pr * 2 + 1, span, :]]
            for hh in range(2):
                query_t = queries[pr * 2 + hh, span, :]
                ours.append(query_t)
                scores = turned(keys[0:count, :], query_t)
                shift = logsums[pr * 2 + hh, :, span]
                probs = jnp.exp2(scores[count - TILE :] + mask[...] - shift)
                if i:
                    probs = jnp.concatenate([jnp.exp2(scores[: count - TILE] - shift), probs], axis=0)
                d_probs = turned(values[0:count, :], d_out[hh])
                d_scores = (probs * d_probs).astype(bf16)
                probs_all.append(probs.astype(bf16))
                d_scores_all.append(d_scores)
                d_query.append(jnp.dot(keys_t[:, 0:count], d_scores, preferred_element_type=f32))
            for acc, parts, other in ((d_values, probs_all, d_out), (d_keys, d_scores_all, ours)):
                two = jnp.concatenate(other, axis=0)
                acc[0:count, :] += jnp.dot(jnp.concatenate(parts, axis=1), two, preferred_element_type=f32)
            d_q = jnp.concatenate(d_query, axis=0).T * 0.125
            d_q = swapped(d_q, cosine[span, :], -sine[span, :])
            packed_d[span, lanes(place_of(pr), 2 * HD)] = d_q.astype(bf16)
            if i % 2:
                slot(3, pr * 2 + i // 2, range(i // 2, 2 * (H // 2), 2))

    @pl.loop(0, tiles)
    def _(k):
        d_key = d_keys[tile(k), :]
        d_key = (d_key + pltpu.roll(d_key, HD, 1)) * (1.0 / LOG2E)
        d_key = swapped(d_key, cosine[tile(k), :], -sine[tile(k), :])
        d_pair = jnp.where(left, d_key, pltpu.roll(d_values[tile(k), :], HD, 1)).astype(bf16)
        packed_d[tile(k), PAIR : PAIR + 2 * HD] = d_pair
        d_first = turned(packed_d[tile(k), 0:qkv], columns(packed_w, 0, qkv))
        sums[0:1, :] += jnp.sum(d_first * normed[tile(k), :], axis=0, keepdims=True)
        sums[2:3, :] += jnp.sum(d_first, axis=0, keepdims=True)
        slot(4, k, range(tiles))

    if not linked:
        query_grads(0, PACK // 4)
    query_grads(PACK // 4, PACK // 2)
    grad_packed[:, :, :, :, :, qkv:] = jnp.zeros((4, 2, 2, 1, D // 16, PACK - qkv), bf16)
    for event in plan[slots[4] + tiles]:
        event()
    if linked:
        gather.sent(2)
        gather.sent(3)

    @pl.loop(0, 4)
    def _(q):
        def up_m():
            return columns(up_w, pl.multiple_of(q * D, D), D)

        def down_m():
            return down_w[q].reshape(D, D)

        @pl.loop(0, tiles)
        def _(k):
            pre = jnp.dot(second_in[tile(k), :], up_m(), preferred_element_type=f32)
            d_hidden = turned(scaled[tile(k), :], down_m())
            cdf = 0.5 + 0.5 * lax.erf(pre * 0.7071067811865476)
            density = jnp.exp2(pre * pre * (-0.5 * LOG2E)) * 0.3989422804014327
            active = (pre * cdf).astype(bf16)
            d_up = (d_hidden * (cdf + pre * density)).astype(bf16)
            for b in range(6):
                pool[b, tile(k), :] = active[:, 128 * b : 128 * (b + 1)]
                pool[6 + b, tile(k), :] = d_up[:, 128 * b : 128 * (b + 1)]
            branch[tile(k), :] += jnp.dot(active, down_m(), preferred_element_type=f32)
            got = turned(d_up, up_m())
            d_second[tile(k), :] = jnp.where(q == 0, got, got + d_second[tile(k), :])
            slot(5, q * 8 + k, [v for v in range(32) if v % 8 < 4])

        @pl.loop(0, 2)
        def _(k):
            three = jnp.concatenate([pool[3 * k + b] for b in range(3)], axis=1)
            got = crossed(three, scaled[...]).astype(bf16)
            down_w[q, k] = got.reshape(2, 2, 4 * D // 32, D)
            slot(5, q * 8 + 4 + k, [v for v in range(32) if v % 8 in (4, 5)])

        @pl.loop(0, 2)
        def _(k):
            six = jnp.concatenate([pool[6 + b] for b in range(6)], axis=1)
            got = crossed(second_in[:, lanes(k * wide, wide)], six).astype(bf16)
            up_w[pl.ds(2 * k, 2), :, :, :, :, lanes(q * D, D)] = got.reshape(2, 2, 2, 1, D // 16, D)
            slot(5, q * 8 + 6 + k, [v for v in range(32) if v % 8 in (6, 7)])

    @pl.loop(0, tiles)
    def _(k):
        second = d_second[tile(k), :]
        sums[1:2, :] += jnp.sum(second * normed[tile(k), :], axis=0, keepdims=True)
        sums[3:4, :] += jnp.sum(second, axis=0, keepdims=True)
        attended[tile(k), :] = branch[tile(k), :].astype(bf16)

    flushed = [pltpu.make_async_copy(attended, mixed_h, out_sems.at[0])]
    flushed[0].start()
    grad_small[:, :, :, :, :, 0:128] = sums[...].T.astype(bf16).reshape(4, 2, 2, 1, D // 16, 128)
    grad_small[:, :, :, :, :, 128:] = jnp.zeros((4, 2, 2, 1, D // 16, SMALL - 128), bf16)

    @pl.loop(0, tiles)
    def _(k):
        inputs = tokens[tile(k), :].astype(f32)
        centred = inputs - jnp.mean(inputs, axis=-1, keepdims=True)
        inv_std = lax.rsqrt(jnp.mean(centred * centred, axis=-1, keepdims=True) + eps_norm)
        norm = centred * inv_std
        d_first = turned(packed_d[tile(k), 0:qkv], columns(packed_w, 0, qkv))
        d_normed = d_first * small[0:1, :] + d_second[tile(k), :] * small[1:2, :]
        inner = jnp.mean(d_normed * norm, axis=-1, keepdims=True)
        d_inputs = inv_std * (d_normed - jnp.mean(d_normed, axis=-1, keepdims=True) - norm * inner)
        first_in[tile(k), :] = (cotan[tile(k), :].astype(f32) * scale + d_inputs).astype(bf16)
        slot(6, k, range(tiles))

    flushed.append(pltpu.make_async_copy(first_in, grad_tokens_h, out_sems.at[1]))
    flushed[-1].start()
    for event in plan[-1]:
        event()
    if linked:
        gather.sent(0)
        scatter.finish()
    else:
        for t in range(5):
            flushed.append(pltpu.make_async_copy(grads[t], results[t], out_sems.at[2 + t]))
            flushed[-1].start()
    for copy in flushed:
        copy.wait()


def layer(linked, lines, rows, rows_down, total_rows, tags, subset_w, tokens, cotan, cosine, sine, weights):
    blocks = layout(rows, rows_down)
    f32, bf16 = jnp.float32, jnp.bfloat16
    shapes = [(lines, 2, 2, g, r, k) for g, r, k in blocks]
    own_rows = [r if g == 2 else rows for g, r, k in blocks]
    vmem = pl.BlockSpec(memory_space=pltpu.VMEM)
    anywhere = pl.BlockSpec(memory_space=pl.ANY)
    if linked:
        results = [jax.ShapeDtypeStruct((o, k), f32) for o, (g, r, k) in zip(own_rows, blocks)]
    else:
        weights = [a.reshape(shape) for a, shape in zip(weights, shapes)]
        results = [jax.ShapeDtypeStruct(shape, bf16) for shape in shapes]
    tall = (SEQ, D)
    buffers = [
        (tall, bf16),
        (tall, bf16),
        ((SEQ, 2 * HD), f32),
        ((SEQ, 2 * HD), f32),
        (tall, f32),
        ((128, D), f32),
        (tall, bf16),
        (tall, bf16),
        ((H, SEQ, 2 * HD), bf16),
        ((H, SEQ, 2 * HD), bf16),
        ((SEQ, 2 * HD), bf16),
        ((HD, SEQ), bf16),
        ((SEQ, 2 * HD), bf16),
        ((2 * HD, SEQ), bf16),
        (tall, bf16),
        ((H, 1, SEQ), f32),
        (tall, bf16),
        ((SEQ, D + 2 * HD), bf16),
        ((TILE, TILE), f32),
        ((128, D), f32),
        ((SEQ, 2 * HD), f32),
        ((SEQ, 2 * HD), f32),
        (tall, f32),
        (tall, f32),
    ]
    buffers += [(shape, bf16) for shape in shapes[:4]] + [(shapes[0], bf16), (shapes[4], bf16)]
    scratch = [pltpu.VMEM(shape, kind) for shape, kind in buffers]
    scratch += [pltpu.SemaphoreType.DMA((8,)), pltpu.SemaphoreType.DMA((7,))]
    if linked:
        scratch += [pltpu.VMEM((rows, PACK), f32)]
        scratch += [pltpu.VMEM((g, r, k // 2), f32) for g, r, k in blocks[:4]]
        scratch += [pltpu.VMEM((128, 128), f32)]
        count, kinds = len(gather_pieces(blocks)), 4 * lines + 3
        scratch += [pltpu.SemaphoreType.DMA((count,))] * 2 + [pltpu.SemaphoreType.DMA((count, kinds))] * 2
        near = [(2, lines, PACK // 4), (1, lines, D // 2), (SLOTS, lines, D // 2), (SLOTS, 1, D // 2), (1, lines, SMALL // 2)]
        scratch += [pltpu.VMEM((n, z, 2, 2, g, r, w), bf16) for (n, z, w), (g, r, k) in zip(near, blocks)]
        for lead in ((2, lines), (lines,), (lines - 1,)):
            scratch += [pltpu.VMEM((*lead, g, r, k // 2), bf16) for g, r, k in blocks]
        scratch += [pltpu.VMEM((g, r, k // 2), f32) for g, r, k in blocks]
        scratch += [pltpu.VMEM((o, k // 2), f32) for o, (g, r, k) in zip(own_rows, blocks)]
        count = len(scatter_pieces(blocks))
        scratch += [pltpu.SemaphoreType.DMA((count, lines + 4))] * 2 + [pltpu.SemaphoreType.REGULAR((2,))]
    return pl.pallas_call(
        functools.partial(layer_kernel, lines, rows, blocks, linked, total_rows),
        out_shape=[jax.ShapeDtypeStruct(tall, bf16)] * 2 + results,
        in_specs=[pl.BlockSpec(memory_space=pltpu.SMEM), vmem] + [anywhere] * 4 + [vmem if linked else anywhere] * len(weights),
        out_specs=[anywhere] * 2 + [vmem if linked else anywhere] * 5,
        scratch_shapes=scratch,
        compiler_params=pltpu.CompilerParams(
            collective_id=0 if linked else None, has_side_effects=linked, vmem_limit_bytes=63 * 2**20
        ),
        name="layer",
    )(tags, subset_w, tokens, cotan, cosine, sine, *weights)


def finish_kernel(rows, *refs):
    packed, small, *rest = refs[:7]
    query, pair, gains, biases, *to = refs[7:]
    for p in range(H // 2):
        query[:, 2 * HD * p : 2 * HD * (p + 1)] = packed[:, place_of(p) : place_of(p) + 2 * HD]
    pair[...] = packed[:, PAIR : PAIR + 2 * HD]
    turned_back = small[:, 0:128].T
    gains[...] = turned_back[0:2]
    biases[...] = turned_back[2:4]
    for a, b in zip(rest, to):
        b[...] = a[...]


def finish(rows, packed, small, *rest):
    f32 = jnp.float32
    vmem = pl.BlockSpec(memory_space=pltpu.VMEM)
    shapes = [(rows, D), (rows, 2 * HD), (2, rows), (2, rows)]
    return pl.pallas_call(
        functools.partial(finish_kernel, rows),
        out_shape=[jax.ShapeDtypeStruct(a, f32) for a in shapes] + [jax.ShapeDtypeStruct(a.shape, a.dtype) for a in rest],
        in_specs=[vmem] * (2 + len(rest)),
        out_specs=[vmem] * (4 + len(rest)),
        compiler_params=pltpu.CompilerParams(vmem_limit_bytes=63 * 2**20),
        name="finish",
    )(packed, small, *rest)


def is_linked(rows):
    return lax.axis_size("dp") == 8 and lax.axis_size("fsdp") == 4 and rows % 8 == 0


def fetch_weights(query_w, pair_w, out_w, up_w, down_w, gains, biases, tags):
    onehot = (tags[0] == jnp.arange(SUBSETS, dtype=jnp.int32)).astype(jnp.float32)
    own_counts = jnp.where((jnp.arange(query_w.shape[0]) == 0)[:, None], onehot[None, :], 0.0)
    small = jnp.concatenate([gains.T, biases.T, own_counts], axis=1)
    small = jnp.pad(small, ((0, 0), (0, 128 - small.shape[1])))
    pairs = [query_w[:, 2 * HD * p : 2 * HD * (p + 1)] for p in range(H // 2)]
    packed = jnp.concatenate([*pairs[0::2], pair_w, *pairs[1::2], small], axis=1)
    return [
        lax.all_gather(a.astype(jnp.bfloat16), ("dp", "fsdp"), axis=0, tiled=True)
        for a in (packed, out_w, up_w, down_w)
    ]


def body(
    tokens,
    w_query,
    w_pair,
    w_attn_out,
    w_up,
    w_down,
    ln_gains,
    ln_biases,
    cotangent,
    subset_tags,
    subset_weights,
):
    cosine, sine = tables()
    linked = is_linked(w_query.shape[0])
    shards = (w_query, w_pair, w_attn_out, w_up, w_down, ln_gains, ln_biases)
    total_rows = lax.axis_size("dp") * lax.axis_size("fsdp")
    if linked:
        lines, rows, rows_down = lax.axis_size("dp") // 2, w_query.shape[0], w_down.shape[0]
    else:
        lines, rows, rows_down = 4, D // 32, 4 * D // 32
        shards = fetch_weights(*shards, subset_tags)
    subset_w = subset_weights.reshape(1, SUBSETS)
    mixed, grad_tokens, *grads = layer(
        linked, lines, rows, rows_down, total_rows, subset_tags, subset_w, tokens, cotangent, cosine, sine, shards
    )
    if not linked:
        grads = [
            lax.psum_scatter(
                g.astype(jnp.float32).reshape(-1, g.shape[-1]), ("dp", "fsdp"), scatter_dimension=0, tiled=True
            )
            for g in grads
        ]
    packed_g, out_g, up_g, down_g, small_g = grads
    query_g, pair_g, gains_g, biases_g, out_g, up_g, down_g, grad_tokens, mixed = finish(
        w_query.shape[0], packed_g, small_g, out_g, up_g, down_g, grad_tokens, mixed
    )
    return mixed, grad_tokens, query_g, pair_g, out_g, up_g, down_g, gains_g, biases_g


def solution(mesh):
    in_specs = (
        P(("dp", "fsdp"), None),
        P(("dp", "fsdp"), None),
        P(("dp", "fsdp"), None),
        P(("dp", "fsdp"), None),
        P(("dp", "fsdp"), None),
        P(("dp", "fsdp"), None),
        P(None, ("dp", "fsdp")),
        P(None, ("dp", "fsdp")),
        P(("dp", "fsdp"), None),
        P(("dp", "fsdp")),
        P(),
    )
    out_specs = (
        P(("dp", "fsdp"), None),
        P(("dp", "fsdp"), None),
        P(("dp", "fsdp"), None),
        P(("dp", "fsdp"), None),
        P(("dp", "fsdp"), None),
        P(("dp", "fsdp"), None),
        P(("dp", "fsdp"), None),
        P(None, ("dp", "fsdp")),
        P(None, ("dp", "fsdp")),
    )
    return jax.shard_map(body, mesh=mesh, in_specs=in_specs, out_specs=out_specs, check_vma=False)
```

time: 902 us -> 185 us (0.21); the launches traced: 892 us -> 185 us
  waiting for transfers between devices: 412 us -> 0 us
  matrix products: 201 us -> 0 us
  blocking collectives: 193 us -> 0 us
  Pallas kernels: 0 us -> 183 us
  other arithmetic: 52.5 us -> 0 us
  between operations: 17.2 us -> 1.3 us
  local copies, waits for them, and re-layouts: 15.1 us -> 0 us
    reduce_scatter x4 -> x0, waiting for transfers between devices: 412 us -> none  [the longest x1 142 us: send_grads(): lax.psum_scatter(up_g, ('dp', 'fsdp'), scatter_dimension=0, tiled=True)]
    dot_general x27 -> x0, matrix products: 201 us -> none  [the longest x1 35.7 us: body(): up_pre = jnp.dot(second_in, up_w, preferred_element_type=f32)]
    pallas_call x0 -> x2, Pallas kernels: none -> 183 us  [the longest x1 179 us: layer(): pl.pallas_call(functools.partial(layer_kernel, lines, rows, blocks, linke...]
    all_gather x3 -> x0, blocking collectives: 109 us -> none  [the longest x1 37.9 us: fetch_weights(): lax.all_gather(pair_w, ('dp', 'fsdp'), axis=0, tiled=True)]
    psum x1 -> x0, blocking collectives: 44.2 us -> none  [body(): counts = lax.psum(jnp.sum(onehot, axis=0), ('dp', 'fsdp'))]
    unnamed x1 -> x0, blocking collectives: 40.3 us -> none
    another operation x9 -> x0, other arithmetic: 25.1 us -> none
    unnamed x133 -> x0, local copies, waits for them, and re-layouts: 12.5 us -> none
  transfers between devices with their start and end apart: 9 -> 0, of which waited for: 4 -> 0; matrix products, arithmetic and copies ran while one was open for 29% -> 0% of each run, Pallas kernels for 0% -> 0%
where the time goes in v4:
time: 185 us
  Pallas kernels  183 us (99%)
    pallas_call x1, Pallas kernels, layer(): pl.pallas_call(functools.partial(layer_kernel, lines, rows, blocks, linke...  179 us
    pallas_call x1, Pallas kernels, finish(): pl.pallas_call(functools.partial(finish_kernel, rows), out_shape=[jax.Sha...  4.08 us

profile of v4, /device:TPU:25, one launch (start us, length us, event | category | flops | bytes accessed | tf_op | source)
XLA Modules:
  0.0 184.8 jit_solution(4822269491291869929)
XLA Ops:
  1.3 179.4 %layer.1 = (bf16[1024,768]{1,0:T(8,128)(2,1)}, bf16[1024,768]{1,0:T(8,128)(2,1)}, f32[24,1024]{1,0:T(8,128)}, f32[24,768]{1,0:T(8,128)}, f32[24,3072]{1,0:T(8,12...) custom-call(s32[1]{0:T(128)S(6)} %copy.22.refs_0_, f32[1,22]{1,0:T(1,128)} %bitcast.1, bf16[1024,768]{1,0:T(8,128)(2,1)} %refs_2_.1, ...), custom_call_target="tpu_custom_call" | custom-call | tf_op jit(solution)/shard_map/layer/pallas_call | solution.py:864
  180.7 4.1 %finish.1 = (f32[24,768]{1,0:T(8,128)}, f32[24,128]{1,0:T(8,128)}, f32[2,24]{1,0:T(2,128)}, f32[2,24]{1,0:T(2,128)}, f32[24,768]{1,0:T(8,128)}, /*index=5*/f32[2...) custom-call(f32[24,1024]{1,0:T(8,128)} %get-tuple-element.25.refs_0_, ...), custom_call_target="tpu_custom_call" | custom-call | tf_op jit(solution)/shard_map/finish/pallas_call | solution.py:894

commit v5 on v4

--- a/solution.py
+++ b/solution.py
@@ -19,15 +19,16 @@
 LOG2E = 1.4426950408889634
 PAIR = 3 * 128
 SMALL = 256
-GATHER_STARTS = (0.0, 0.0, 2.0, 7.0, 16.0, 21.0, 30.0, 35.0)
-GATHER_LAGS = (0.0, 8.0, 16.0, 18.0)
-SCATTER_LAGS = (0.0, 2.0, 8.0, 14.0, 20.0, 23.0)
-PROJECT_STEPS = (1.25,) * 4
-ATTEND_STEPS = (1.2, 2.8) * 6
-OUTWARD_STEPS = (1.2,) * 4 + (0.85,) * 2
+GATHER_STARTS = (0.0, -6.0, 0.0, 8.0, 17.0, 22.0, 27.0, 32.0)
+GATHER_LAGS = (0.0, 10.0, 20.0, 22.0)
+SCATTER_LAGS = (0.0, 2.5, 10.0, 17.0, 24.0, 27.0)
+PROJECT_STEPS = (1.5,) * 4
+FORWARD_STEPS = (1.7, 0.1) * 6
+OUTWARD_STEPS = (1.5,) * 4 + (0.85,) * 2
+BACKWARD_STEPS = (3.2, 0.1) * 6
 CLOSE_STEPS = (0.7,) * 4 + (1.0,)
-CHUNK_STEPS = (1.6,) * 4 + (0.7,) * 4
-TOKEN_STEPS = (0.7,) * 4
+CHUNK_STEPS = (1.4, 1.4, 1.4, 1.4, 1.2, 0.1, 1.2, 0.1)
+TOKEN_STEPS = (0.9,) * 4
 MESH = pl.DeviceIdType.MESH
 
 
@@ -91,7 +92,7 @@
     w, half = D // 2, r3 // 2 // 16 * 16
     ups = [(2, 0, r2, 2 * w * k, w * k, w) for k in range(4)]
     downs = [(3, 0, half, 0, 0, w), (3, half, r3 - half, 0, 0, w)]
-    return [(0, 0, r0, 0, 0, PACK // 2), (1, 0, r1, 0, 0, w), ups[0], downs[0], ups[1], downs[1], ups[2], ups[3]]
+    return [(0, 0, r0, 0, 0, PACK // 2), (1, 0, r1, 0, 0, w), *downs, *ups]
 
 
 class Gather:
@@ -107,7 +108,7 @@
 
     def go(self, p, make):
         make().start()
-        self.started.append((self.pieces[p][0], make))
+        self.started.append((p, make))
 
     def stage_rows(self, p, core):
         t, r0, nr, _, l0, w = self.pieces[p]
@@ -208,9 +209,9 @@
                     timed.append((GATHER_STARTS[p] + lag, len(timed), functools.partial(steps[k], p)))
         return [functools.partial(steps[k], p) for k, p in urgent], timed
 
-    def sent(self, t):
-        for kind, make in self.started:
-            if kind == t:
+    def sent(self, *pieces):
+        for p, make in self.started:
+            if p in pieces:
                 make().wait_send()
 
 
@@ -245,6 +246,11 @@
 
 def turned(a, b):
     return lax.dot_general(a, b, (((1,), (1,)), ((), ())), preferred_element_type=jnp.float32)
+
+
+def tallest(scores):
+    part_max = jnp.max(scores.reshape(-1, 64, scores.shape[1]), axis=0)
+    return jnp.max(part_max, axis=0, keepdims=True)
 
 
 def swapped(block, cosine, sine):
@@ -510,8 +516,8 @@
     tags, subset_w, tokens_h, cotan_h, cosine_h, sine_h = refs[:6]
     given, refs = (refs[6:13], refs[13:]) if linked else (refs[6:10], refs[10:])
     mixed_h, grad_tokens_h, *results = refs[:7]
-    tokens, cotan, cosine, sine, normed, small, first_in, second_in, queries, pool, keys, keys_t = refs[7:19]
-    values, values_t, attended, logsums, scaled, packed_d, mask, sums, d_keys, d_values, branch, d_second = refs[19:31]
+    tokens, cotan, cosine, sine, d_second, small, first_t, second_in, queries, pool, keys, keys_t = refs[7:19]
+    values, values_t, attended, logsums, scaled, packed_d, mask, sums, d_keys, d_values, branch, second_t = refs[19:31]
     whole, grad_packed, grad_small, load_sems, out_sems = refs[31:35], refs[35], refs[36], refs[37], refs[38]
     refs = refs[39:]
     grads = [grad_packed, *whole[1:], grad_small]
@@ -547,20 +553,21 @@
         urgent, timed = [], []
     packed_w, out_w, up_w, down_w = whole
 
-    steps = (PROJECT_STEPS, ATTEND_STEPS, OUTWARD_STEPS, ATTEND_STEPS, CLOSE_STEPS, CHUNK_STEPS * 4, TOKEN_STEPS)
+    steps = (PROJECT_STEPS, FORWARD_STEPS, OUTWARD_STEPS, BACKWARD_STEPS, CLOSE_STEPS, CHUNK_STEPS * 4, TOKEN_STEPS)
     starts, slots = [0], [0]
     for part_steps in steps:
         starts.append(starts[-1] + sum(part_steps))
         slots.append(slots[-1] + len(part_steps))
     if linked:
-        timed += scatter.timed(0, starts[3])
-        ready = starts[3] + 4 * sum(ATTEND_STEPS[:2])
-        timed += [(ready - 0.01, 100, lambda: query_grads(0, PACK // 4))] + scatter.timed(1, ready)
-        timed += scatter.timed(2, starts[5])
+        edge = 0.01
+        timed += scatter.timed(0, starts[3] - edge)
+        ready = starts[3] + 4 * sum(BACKWARD_STEPS[:2])
+        timed += [(ready - 2 * edge, 100, lambda: query_grads(0, PACK // 4))] + scatter.timed(1, ready - edge)
+        timed += scatter.timed(2, starts[5] - edge)
         for q in range(4):
-            start = starts[5] + q * sum(CHUNK_STEPS) + sum(CHUNK_STEPS[:6])
+            start = starts[5] + q * sum(CHUNK_STEPS) + sum(CHUNK_STEPS[:6]) - edge
             timed += scatter.timed(3 + 2 * q, start) + scatter.timed(4 + 2 * q, start + sum(CHUNK_STEPS[6:]))
-        timed += scatter.timed(11, starts[6])
+        timed += scatter.timed(11, starts[6] + edge)
     plan = deal(timed, ends(0.0, *(step for part_steps in steps for step in part_steps)))
 
     def slot(section, index, values):
@@ -576,11 +583,15 @@
     left = lane < HD
     loads[0].wait()
 
+    def normed(k):
+        inputs = tokens[tile(k), :].astype(f32)
+        centred = inputs - jnp.mean(inputs, axis=-1, keepdims=True)
+        inv_std = lax.rsqrt(jnp.mean(centred * centred, axis=-1, keepdims=True) + eps_norm)
+        return centred * inv_std, inv_std
+
     @pl.loop(0, tiles)
     def _(k):
-        inputs = tokens[tile(k), :].astype(f32)
-        centred = inputs - jnp.mean(inputs, axis=-1, keepdims=True)
-        normed[tile(k), :] = centred * lax.rsqrt(jnp.mean(centred * centred, axis=-1, keepdims=True) + eps_norm)
+        d_second[tile(k), :] = normed(k)[0]
 
     for copy in loads[1:]:
         copy.wait()
@@ -590,10 +601,12 @@
 
     @pl.loop(0, tiles)
     def _(k):
-        norm = normed[tile(k), :]
+        norm = d_second[tile(k), :]
         a1 = (norm * small[0:1, :] + small[2:3, :]).astype(bf16)
-        first_in[tile(k), :] = a1
-        second_in[tile(k), :] = (norm * small[1:2, :] + small[3:4, :]).astype(bf16)
+        a2 = norm * small[1:2, :] + small[3:4, :]
+        first_t[:, tile(k)] = a1.T
+        second_in[tile(k), :] = a2.astype(bf16)
+        second_t[:, tile(k)] = a2.astype(bf16).T
         mixed = jnp.dot(a1, columns(packed_w, 0, qkv), preferred_element_type=f32)
         cos_t, sin_t = cosine[tile(k), :], sine[tile(k), :]
         for p in range(H // 2):
@@ -615,27 +628,49 @@
 
     @pl.loop(0, H // 2)
     def _(pr):
-        for i in range(tiles):
+        work = [(i, hh) for i in range(tiles) for hh in range(2)]
+        ready, shares, heads = {}, {}, {}
+
+        def score(n):
+            i, hh = work[n]
             count = TILE * (i + 1)
-            heads = []
-            for hh in range(2):
-                head = pr * 2 + hh
-                scores = turned(keys[0:count, :], queries[head, i * TILE : count, :])
-                last = scores[count - TILE :] + mask[...]
-                peak = jnp.max(last, axis=0, keepdims=True)
-                if i:
-                    peak = jnp.maximum(peak, jnp.max(scores[: count - TILE], axis=0, keepdims=True))
-                probs = jnp.exp2(last - peak).astype(bf16)
-                if i:
-                    probs = jnp.concatenate([jnp.exp2(scores[: count - TILE] - peak).astype(bf16), probs], axis=0)
-                got = jnp.dot(values_t[:, 0:count], probs, preferred_element_type=f32)
-                total = got[HD : HD + 1]
-                heads.append(got[:HD] * (1.0 / total))
-                logsums[head, :, i * TILE : count] = peak + jnp.log2(total)
-            both = jnp.concatenate(heads, axis=0).T
-            attended[i * TILE : count, lanes(pr * 2 * HD, 2 * HD)] = both.astype(bf16)
-            if i % 2:
-                slot(1, pr * 2 + i // 2, range(i // 2, 2 * (H // 2), 2))
+            ready[n] = turned(keys[0:count, :], queries[pr * 2 + hh, i * TILE : count, :])
+
+        def weigh(n):
+            i, hh = work[n]
+            count = TILE * (i + 1)
+            scores = ready.pop(n)
+            last = scores[count - TILE :] + mask[...]
+            peak = tallest(last)
+            if i:
+                peak = jnp.maximum(peak, tallest(scores[: count - TILE]))
+            probs = jnp.exp2(last - peak).astype(bf16)
+            if i:
+                probs = jnp.concatenate([jnp.exp2(scores[: count - TILE] - peak).astype(bf16), probs], axis=0)
+            shares[n] = peak, probs
+
+        def collect(n):
+            i, hh = work[n]
+            count = TILE * (i + 1)
+            peak, probs = shares.pop(n)
+            got = jnp.dot(values_t[0:80, 0:count], probs, preferred_element_type=f32)
+            total = got[HD : HD + 1]
+            heads[hh] = got[:HD] * (1.0 / total)
+            logsums[pr * 2 + hh, :, i * TILE : count] = peak + jnp.log2(total)
+            if hh:
+                both = jnp.concatenate([heads[0], heads[1]], axis=0).T
+                attended[i * TILE : count, lanes(pr * 2 * HD, 2 * HD)] = both.astype(bf16)
+
+        ahead = 2
+        for n in range(len(work) + ahead + 2):
+            if n < len(work):
+                score(n)
+            if 0 <= n - ahead < len(work):
+                weigh(n - ahead)
+            if 0 <= n - ahead - 2 < len(work):
+                collect(n - ahead - 2)
+        for i in (0, 1):
+            slot(1, pr * 2 + i, range(i, 2 * (H // 2), 2))
 
     kind = lax.broadcasted_iota(jnp.int32, (128, D), 0)
     count = jnp.sum(jnp.where(kind == tags[0] + 4, small[...], 0.0), keepdims=True)
@@ -673,37 +708,53 @@
     def query_grads(start, stop):
         for span in (slice(start, stop), slice(PACK // 2 + start, min(PACK // 2 + stop, qkv))):
             for k in range(2):
-                got = crossed(first_in[:, k * wide : (k + 1) * wide], packed_d[:, span]).astype(bf16)
+                got = jnp.dot(first_t[k * wide : (k + 1) * wide, :], packed_d[:, span], preferred_element_type=f32).astype(bf16)
                 grad_packed[2 * k : 2 * k + 2, :, :, :, :, span] = got.reshape(2, 2, 2, 1, D // 16, -1)
 
     @pl.loop(0, H // 2)
     def _(pr):
-        for i in range(tiles):
-            count = TILE * (i + 1)
-            span = slice(i * TILE, count)
-            probs_all, d_scores_all, d_query, ours = [], [], [], []
-            d_out = [pool[pr * 2, span, :], pool[pr * 2 + 1, span, :]]
-            for hh in range(2):
-                query_t = queries[pr * 2 + hh, span, :]
-                ours.append(query_t)
-                scores = turned(keys[0:count, :], query_t)
-                shift = logsums[pr * 2 + hh, :, span]
-                probs = jnp.exp2(scores[count - TILE :] + mask[...] - shift)
-                if i:
-                    probs = jnp.concatenate([jnp.exp2(scores[: count - TILE] - shift), probs], axis=0)
-                d_probs = turned(values[0:count, :], d_out[hh])
-                d_scores = (probs * d_probs).astype(bf16)
-                probs_all.append(probs.astype(bf16))
-                d_scores_all.append(d_scores)
-                d_query.append(jnp.dot(keys_t[:, 0:count], d_scores, preferred_element_type=f32))
-            for acc, parts, other in ((d_values, probs_all, d_out), (d_keys, d_scores_all, ours)):
-                two = jnp.concatenate(other, axis=0)
-                acc[0:count, :] += jnp.dot(jnp.concatenate(parts, axis=1), two, preferred_element_type=f32)
-            d_q = jnp.concatenate(d_query, axis=0).T * 0.125
-            d_q = swapped(d_q, cosine[span, :], -sine[span, :])
-            packed_d[span, lanes(place_of(pr), 2 * HD)] = d_q.astype(bf16)
-            if i % 2:
-                slot(3, pr * 2 + i // 2, range(i // 2, 2 * (H // 2), 2))
+        work = [(i, hh) for i in range(tiles) for hh in range(2)]
+        ready, shares, d_query = {}, {}, {}
+
+        def score(n):
+            i, hh = work[n]
+            count, span = TILE * (i + 1), slice(i * TILE, TILE * (i + 1))
+            head = pr * 2 + hh
+            ready[n] = turned(keys[0:count, :], queries[head, span, :]), turned(values[0:count, :], pool[head, span, :])
+
+        def weigh(n):
+            i, hh = work[n]
+            count, span = TILE * (i + 1), slice(i * TILE, TILE * (i + 1))
+            scores, d_probs = ready.pop(n)
+            shift = logsums[pr * 2 + hh, :, span]
+            probs = jnp.exp2(scores[count - TILE :] + mask[...] - shift)
+            if i:
+                probs = jnp.concatenate([jnp.exp2(scores[: count - TILE] - shift), probs], axis=0)
+            shares[n] = probs.astype(bf16), (probs * d_probs).astype(bf16)
+
+        def collect(n):
+            i, hh = work[n]
+            count, span = TILE * (i + 1), slice(i * TILE, TILE * (i + 1))
+            d_query[hh] = jnp.dot(keys_t[:, 0:count], shares[n][1], preferred_element_type=f32)
+            if hh:
+                both = [shares.pop(n - 1), shares.pop(n)]
+                for acc, k, other in ((d_values, 0, pool), (d_keys, 1, queries)):
+                    two = jnp.concatenate([other[pr * 2, span, :], other[pr * 2 + 1, span, :]], axis=0)
+                    parts = jnp.concatenate([both[0][k], both[1][k]], axis=1)
+                    acc[0:count, :] += jnp.dot(parts, two, preferred_element_type=f32)
+                d_q = jnp.concatenate([d_query[0], d_query[1]], axis=0).T * 0.125
+                d_q = swapped(d_q, cosine[span, :], -sine[span, :])
+                packed_d[span, lanes(place_of(pr), 2 * HD)] = d_q.astype(bf16)
+
+        for n in range(len(work) + 2 + 1):
+            if n < len(work):
+                score(n)
+            if 0 <= n - 2 < len(work):
+                weigh(n - 2)
+            if 0 <= n - 2 - 1 < len(work):
+                collect(n - 2 - 1)
+        for i in (0, 1):
+            slot(3, pr * 2 + i, range(i, 2 * (H // 2), 2))
 
     @pl.loop(0, tiles)
     def _(k):
@@ -713,7 +764,7 @@
         d_pair = jnp.where(left, d_key, pltpu.roll(d_values[tile(k), :], HD, 1)).astype(bf16)
         packed_d[tile(k), PAIR : PAIR + 2 * HD] = d_pair
         d_first = turned(packed_d[tile(k), 0:qkv], columns(packed_w, 0, qkv))
-        sums[0:1, :] += jnp.sum(d_first * normed[tile(k), :], axis=0, keepdims=True)
+        sums[0:1, :] += jnp.sum(d_first * normed(k)[0], axis=0, keepdims=True)
         sums[2:3, :] += jnp.sum(d_first, axis=0, keepdims=True)
         slot(4, k, range(tiles))
 
@@ -724,8 +775,7 @@
     for event in plan[slots[4] + tiles]:
         event()
     if linked:
-        gather.sent(2)
-        gather.sent(3)
+        gather.sent(2, 3)
 
     @pl.loop(0, 4)
     def _(q):
@@ -743,32 +793,33 @@
             density = jnp.exp2(pre * pre * (-0.5 * LOG2E)) * 0.3989422804014327
             active = (pre * cdf).astype(bf16)
             d_up = (d_hidden * (cdf + pre * density)).astype(bf16)
+            active_t = active.T
+            for b in range(2):
+                queries[2 * k + b, 0:D, :] = active_t[:, 128 * b : 128 * (b + 1)]
             for b in range(6):
-                pool[b, tile(k), :] = active[:, 128 * b : 128 * (b + 1)]
-                pool[6 + b, tile(k), :] = d_up[:, 128 * b : 128 * (b + 1)]
+                pool[b, tile(k), :] = d_up[:, 128 * b : 128 * (b + 1)]
             branch[tile(k), :] += jnp.dot(active, down_m(), preferred_element_type=f32)
             got = turned(d_up, up_m())
             d_second[tile(k), :] = jnp.where(q == 0, got, got + d_second[tile(k), :])
             slot(5, q * 8 + k, [v for v in range(32) if v % 8 < 4])
 
-        @pl.loop(0, 2)
-        def _(k):
-            three = jnp.concatenate([pool[3 * k + b] for b in range(3)], axis=1)
-            got = crossed(three, scaled[...]).astype(bf16)
-            down_w[q, k] = got.reshape(2, 2, 4 * D // 32, D)
-            slot(5, q * 8 + 4 + k, [v for v in range(32) if v % 8 in (4, 5)])
-
-        @pl.loop(0, 2)
-        def _(k):
-            six = jnp.concatenate([pool[6 + b] for b in range(6)], axis=1)
-            got = crossed(second_in[:, lanes(k * wide, wide)], six).astype(bf16)
-            up_w[pl.ds(2 * k, 2), :, :, :, :, lanes(q * D, D)] = got.reshape(2, 2, 2, 1, D // 16, D)
-            slot(5, q * 8 + 6 + k, [v for v in range(32) if v % 8 in (6, 7)])
+        hidden_t = jnp.concatenate([queries[b, 0:D, :] for b in range(8)], axis=1)
+        got = jnp.dot(hidden_t, scaled[...], preferred_element_type=f32).astype(bf16)
+        down_w[q] = got.reshape(2, 2, 2, 4 * D // 32, D)
+        for v in (4, 5):
+            slot(5, q * 8 + v, [8 * p + v for p in range(4)])
+        if linked:
+            run_at(q, [(v, [functools.partial(gather.sent, 4 + v)]) for v in range(4)])
+        d_ups = jnp.concatenate([pool[b] for b in range(6)], axis=1)
+        got = jnp.dot(second_t[...], d_ups, preferred_element_type=f32).astype(bf16)
+        up_w[:, :, :, :, :, lanes(q * D, D)] = got.reshape(4, 2, 2, 1, D // 16, D)
+        for v in (6, 7):
+            slot(5, q * 8 + v, [8 * p + v for p in range(4)])
 
     @pl.loop(0, tiles)
     def _(k):
         second = d_second[tile(k), :]
-        sums[1:2, :] += jnp.sum(second * normed[tile(k), :], axis=0, keepdims=True)
+        sums[1:2, :] += jnp.sum(second * normed(k)[0], axis=0, keepdims=True)
         sums[3:4, :] += jnp.sum(second, axis=0, keepdims=True)
         attended[tile(k), :] = branch[tile(k), :].astype(bf16)
 
@@ -779,18 +830,15 @@
 
     @pl.loop(0, tiles)
     def _(k):
-        inputs = tokens[tile(k), :].astype(f32)
-        centred = inputs - jnp.mean(inputs, axis=-1, keepdims=True)
-        inv_std = lax.rsqrt(jnp.mean(centred * centred, axis=-1, keepdims=True) + eps_norm)
-        norm = centred * inv_std
+        norm, inv_std = normed(k)
         d_first = turned(packed_d[tile(k), 0:qkv], columns(packed_w, 0, qkv))
         d_normed = d_first * small[0:1, :] + d_second[tile(k), :] * small[1:2, :]
         inner = jnp.mean(d_normed * norm, axis=-1, keepdims=True)
         d_inputs = inv_std * (d_normed - jnp.mean(d_normed, axis=-1, keepdims=True) - norm * inner)
-        first_in[tile(k), :] = (cotan[tile(k), :].astype(f32) * scale + d_inputs).astype(bf16)
+        second_in[tile(k), :] = (cotan[tile(k), :].astype(f32) * scale + d_inputs).astype(bf16)
         slot(6, k, range(tiles))
 
-    flushed.append(pltpu.make_async_copy(first_in, grad_tokens_h, out_sems.at[1]))
+    flushed.append(pltpu.make_async_copy(second_in, grad_tokens_h, out_sems.at[1]))
     flushed[-1].start()
     for event in plan[-1]:
         event()
@@ -825,7 +873,7 @@
         ((SEQ, 2 * HD), f32),
         (tall, f32),
         ((128, D), f32),
-        (tall, bf16),
+        ((D, SEQ), bf16),
         (tall, bf16),
         ((H, SEQ, 2 * HD), bf16),
         ((H, SEQ, 2 * HD), bf16),
@@ -842,7 +890,7 @@
         ((SEQ, 2 * HD), f32),
         ((SEQ, 2 * HD), f32),
         (tall, f32),
-        (tall, f32),
+        ((D, SEQ), bf16),
     ]
     buffers += [(shape, bf16) for shape in shapes[:4]] + [(shapes[0], bf16), (shapes[4], bf16)]
     scratch = [pltpu.VMEM(shape, kind) for shape, kind in buffers]

time: 185 us -> 165 us (0.89)
  Pallas kernels: 183 us -> 164 us
    pallas_call x1, Pallas kernels: 179 us -> 160 us  [layer(): pl.pallas_call(functools.partial(layer_kernel, lines, rows, blocks, linke...]
where the time goes in v5:
time: 165 us
  Pallas kernels  164 us (99%)
    pallas_call x1, Pallas kernels, layer(): pl.pallas_call(functools.partial(layer_kernel, lines, rows, blocks, linke...  160 us
    pallas_call x1, Pallas kernels, finish(): pl.pallas_call(functools.partial(finish_kernel, rows), out_shape=[jax.Sha...  4.08 us

profile of v5, /device:TPU:25, one launch (start us, length us, event | category | flops | bytes accessed | tf_op | source)
XLA Modules:
  0.0 165.0 jit_solution(18087866267366405248)
XLA Ops:
  1.3 159.6 %layer.1 = (bf16[1024,768]{1,0:T(8,128)(2,1)}, bf16[1024,768]{1,0:T(8,128)(2,1)}, f32[24,1024]{1,0:T(8,128)}, f32[24,768]{1,0:T(8,128)}, f32[24,3072]{1,0:T(8,12...) custom-call(s32[1]{0:T(128)S(6)} %copy.22.refs_0_, f32[1,22]{1,0:T(1,128)} %bitcast.1, bf16[1024,768]{1,0:T(8,128)(2,1)} %refs_2_.1, ...), custom_call_target="tpu_custom_call" | custom-call | tf_op jit(solution)/shard_map/layer/pallas_call | solution.py:912
  160.9 4.1 %finish.1 = (f32[24,768]{1,0:T(8,128)}, f32[24,128]{1,0:T(8,128)}, f32[2,24]{1,0:T(2,128)}, f32[2,24]{1,0:T(2,128)}, f32[24,768]{1,0:T(8,128)}, /*index=5*/f32[2...) custom-call(f32[24,1024]{1,0:T(8,128)} %get-tuple-element.25.refs_0_, ...), custom_call_target="tpu_custom_call" | custom-call | tf_op jit(solution)/shard_map/finish/pallas_call | solution.py:942

commit v6 on v5

--- a/solution.py
+++ b/solution.py
@@ -26,9 +26,9 @@
 FORWARD_STEPS = (1.7, 0.1) * 6
 OUTWARD_STEPS = (1.5,) * 4 + (0.85,) * 2
 BACKWARD_STEPS = (3.2, 0.1) * 6
-CLOSE_STEPS = (0.7,) * 4 + (1.0,)
+CLOSE_STEPS = (0.2,) * 4 + (1.0,)
 CHUNK_STEPS = (1.4, 1.4, 1.4, 1.4, 1.2, 0.1, 1.2, 0.1)
-TOKEN_STEPS = (0.9,) * 4
+TOKEN_STEPS = (0.7,) * 4 + (0.5,) * 4
 MESH = pl.DeviceIdType.MESH
 
 
@@ -155,8 +155,12 @@
     def begin(self, ahead):
         for p in range(len(self.pieces)):
             self.go(p, functools.partial(self.swap, p))
-        for p, piece in enumerate(self.pieces):
-            t, r0, nr, c0, l0, w = piece
+        self.ahead = ahead
+        self.place_own(range(ahead))
+
+    def place_own(self, some):
+        for p in some:
+            t, r0, nr, c0, l0, w = self.pieces[p]
             source, _, _ = self.source(p)
             kept = jnp.where(self.c == 0, source[:, c0 : c0 + w], source[:, HALF[t] + c0 : HALF[t] + c0 + w])
             self.stage_rows(p, self.c)[...] = kept
@@ -165,9 +169,8 @@
             self.block(p, 0, self.x, self.y)[...] = held.astype(jnp.bfloat16)
             for d in range(1, self.lines):
                 self.go(p, functools.partial(self.direct, p, d))
-            if p < ahead:
+            if p < self.ahead:
                 self.own(p)
-        self.ahead = ahead
 
     def first(self, p):
         x, y, c = self.x, self.y, self.c
@@ -207,7 +210,9 @@
             for k, lag in enumerate(GATHER_LAGS):
                 if (k, p) not in urgent:
                     timed.append((GATHER_STARTS[p] + lag, len(timed), functools.partial(steps[k], p)))
-        return [functools.partial(steps[k], p) for k, p in urgent], timed
+        urgent = [functools.partial(steps[k], p) for k, p in urgent]
+        rest = functools.partial(self.place_own, range(self.ahead, len(self.pieces)))
+        return urgent[:1] + [rest] + urgent[1:], timed
 
     def sent(self, *pieces):
         for p, make in self.started:
@@ -567,7 +572,7 @@
         for q in range(4):
             start = starts[5] + q * sum(CHUNK_STEPS) + sum(CHUNK_STEPS[:6]) - edge
             timed += scatter.timed(3 + 2 * q, start) + scatter.timed(4 + 2 * q, start + sum(CHUNK_STEPS[6:]))
-        timed += scatter.timed(11, starts[6] + edge)
+        timed += scatter.timed(11, starts[6] + sum(TOKEN_STEPS[:4]) + edge)
     plan = deal(timed, ends(0.0, *(step for part_steps in steps for step in part_steps)))
 
     def slot(section, index, values):
@@ -763,9 +768,6 @@
         d_key = swapped(d_key, cosine[tile(k), :], -sine[tile(k), :])
         d_pair = jnp.where(left, d_key, pltpu.roll(d_values[tile(k), :], HD, 1)).astype(bf16)
         packed_d[tile(k), PAIR : PAIR + 2 * HD] = d_pair
-        d_first = turned(packed_d[tile(k), 0:qkv], columns(packed_w, 0, qkv))
-        sums[0:1, :] += jnp.sum(d_first * normed(k)[0], axis=0, keepdims=True)
-        sums[2:3, :] += jnp.sum(d_first, axis=0, keepdims=True)
         slot(4, k, range(tiles))
 
     if not linked:
@@ -818,10 +820,13 @@
 
     @pl.loop(0, tiles)
     def _(k):
-        second = d_second[tile(k), :]
-        sums[1:2, :] += jnp.sum(second * normed(k)[0], axis=0, keepdims=True)
-        sums[3:4, :] += jnp.sum(second, axis=0, keepdims=True)
         attended[tile(k), :] = branch[tile(k), :].astype(bf16)
+        d_first = turned(packed_d[tile(k), 0:qkv], columns(packed_w, 0, qkv))
+        branch[tile(k), :] = d_first
+        second, norm = d_second[tile(k), :], normed(k)[0]
+        for n, value in enumerate((d_first * norm, second * norm, d_first, second)):
+            sums[n : n + 1, :] += jnp.sum(value, axis=0, keepdims=True)
+        slot(6, k, range(tiles))
 
     flushed = [pltpu.make_async_copy(attended, mixed_h, out_sems.at[0])]
     flushed[0].start()
@@ -831,12 +836,11 @@
     @pl.loop(0, tiles)
     def _(k):
         norm, inv_std = normed(k)
-        d_first = turned(packed_d[tile(k), 0:qkv], columns(packed_w, 0, qkv))
-        d_normed = d_first * small[0:1, :] + d_second[tile(k), :] * small[1:2, :]
+        d_normed = branch[tile(k), :] * small[0:1, :] + d_second[tile(k), :] * small[1:2, :]
         inner = jnp.mean(d_normed * norm, axis=-1, keepdims=True)
         d_inputs = inv_std * (d_normed - jnp.mean(d_normed, axis=-1, keepdims=True) - norm * inner)
         second_in[tile(k), :] = (cotan[tile(k), :].astype(f32) * scale + d_inputs).astype(bf16)
-        slot(6, k, range(tiles))
+        slot(6, tiles + k, range(tiles, 2 * tiles))
 
     flushed.append(pltpu.make_async_copy(second_in, grad_tokens_h, out_sems.at[1]))
     flushed[-1].start()

time: 165 us -> 163 us (0.988)
  Pallas kernels: 164 us -> 161 us
    pallas_call x1, Pallas kernels: 160 us -> 157 us  [layer(): pl.pallas_call(functools.partial(layer_kernel, lines, rows, blocks, linke...]
where the time goes in v6:
time: 163 us; the launch traced here: 162 us
  Pallas kernels  161 us (99%)
    pallas_call x1, Pallas kernels, layer(): pl.pallas_call(functools.partial(layer_kernel, lines, rows, blocks, linke...  157 us
    pallas_call x1, Pallas kernels, finish(): pl.pallas_call(functools.partial(finish_kernel, rows), out_shape=[jax.Sha...  4.08 us

profile of v6, /device:TPU:25, one launch (start us, length us, event | category | flops | bytes accessed | tf_op | source)
XLA Modules:
  0.0 162.2 jit_solution(10414940295778061908)
XLA Ops:
  1.3 156.9 %layer.1 = (bf16[1024,768]{1,0:T(8,128)(2,1)}, bf16[1024,768]{1,0:T(8,128)(2,1)}, f32[24,1024]{1,0:T(8,128)}, f32[24,768]{1,0:T(8,128)}, f32[24,3072]{1,0:T(8,12...) custom-call(s32[1]{0:T(128)S(6)} %copy.22.refs_0_, f32[1,22]{1,0:T(1,128)} %bitcast.1, bf16[1024,768]{1,0:T(8,128)(2,1)} %refs_2_.1, ...), custom_call_target="tpu_custom_call" | custom-call | tf_op jit(solution)/shard_map/layer/pallas_call | solution.py:916
  158.2 4.1 %finish.1 = (f32[24,768]{1,0:T(8,128)}, f32[24,128]{1,0:T(8,128)}, f32[2,24]{1,0:T(2,128)}, f32[2,24]{1,0:T(2,128)}, f32[24,768]{1,0:T(8,128)}, /*index=5*/f32[2...) custom-call(f32[24,1024]{1,0:T(8,128)} %get-tuple-element.25.refs_0_, ...), custom_call_target="tpu_custom_call" | custom-call | tf_op jit(solution)/shard_map/finish/pallas_call | solution.py:946

commit v7 on v6

--- a/solution.py
+++ b/solution.py
@@ -23,7 +23,7 @@
 GATHER_LAGS = (0.0, 10.0, 20.0, 22.0)
 SCATTER_LAGS = (0.0, 2.5, 10.0, 17.0, 24.0, 27.0)
 PROJECT_STEPS = (1.5,) * 4
-FORWARD_STEPS = (1.7, 0.1) * 6
+FORWARD_STEPS = (3.3, 0.1, 0.1, 0.1) * 3
 OUTWARD_STEPS = (1.5,) * 4 + (0.85,) * 2
 BACKWARD_STEPS = (3.2, 0.1) * 6
 CLOSE_STEPS = (0.2,) * 4 + (1.0,)
@@ -631,18 +631,20 @@
         values_t[:, tile(k)] = jnp.where(left, other, jnp.where(lane == HD, 1.0, 0.0)).T.astype(bf16)
         slot(0, k, range(tiles))
 
-    @pl.loop(0, H // 2)
-    def _(pr):
-        work = [(i, hh) for i in range(tiles) for hh in range(2)]
+    @pl.loop(0, H // 4)
+    def _(two):
+        work = [(i, hh, pp) for pp in range(2) for i in range(tiles) for hh in range(2)]
         ready, shares, heads = {}, {}, {}
 
         def score(n):
-            i, hh = work[n]
+            i, hh, pp = work[n]
+            pr = two * 2 + pp
             count = TILE * (i + 1)
             ready[n] = turned(keys[0:count, :], queries[pr * 2 + hh, i * TILE : count, :])
 
         def weigh(n):
-            i, hh = work[n]
+            i, hh, pp = work[n]
+            pr = two * 2 + pp
             count = TILE * (i + 1)
             scores = ready.pop(n)
             last = scores[count - TILE :] + mask[...]
@@ -655,7 +657,8 @@
             shares[n] = peak, probs
 
         def collect(n):
-            i, hh = work[n]
+            i, hh, pp = work[n]
+            pr = two * 2 + pp
             count = TILE * (i + 1)
             peak, probs = shares.pop(n)
             got = jnp.dot(values_t[0:80, 0:count], probs, preferred_element_type=f32)
@@ -674,8 +677,8 @@
                 weigh(n - ahead)
             if 0 <= n - ahead - 2 < len(work):
                 collect(n - ahead - 2)
-        for i in (0, 1):
-            slot(1, pr * 2 + i, range(i, 2 * (H // 2), 2))
+        for i in range(4):
+            slot(1, two * 4 + i, range(i, 2 * (H // 2), 4))
 
     kind = lax.broadcasted_iota(jnp.int32, (128, D), 0)
     count = jnp.sum(jnp.where(kind == tags[0] + 4, small[...], 0.0), keepdims=True)

time: 163 us -> 163 us (level)
  no operation moved by 1% of the time
where the time goes in v7:
time: 163 us; the launch traced here: 162 us
  Pallas kernels  161 us (99%)
    pallas_call x1, Pallas kernels, layer(): pl.pallas_call(functools.partial(layer_kernel, lines, rows, blocks, linke...  157 us
    pallas_call x1, Pallas kernels, finish(): pl.pallas_call(functools.partial(finish_kernel, rows), out_shape=[jax.Sha...  4.08 us

profile of v7, /device:TPU:25, one launch (start us, length us, event | category | flops | bytes accessed | tf_op | source)
XLA Modules:
  0.0 162.2 jit_solution(12869805819697836464)
XLA Ops:
  1.3 156.8 %layer.1 = (bf16[1024,768]{1,0:T(8,128)(2,1)}, bf16[1024,768]{1,0:T(8,128)(2,1)}, f32[24,1024]{1,0:T(8,128)}, f32[24,768]{1,0:T(8,128)}, f32[24,3072]{1,0:T(8,12...) custom-call(s32[1]{0:T(128)S(6)} %copy.22.refs_0_, f32[1,22]{1,0:T(1,128)} %bitcast.1, bf16[1024,768]{1,0:T(8,128)(2,1)} %refs_2_.1, ...), custom_call_target="tpu_custom_call" | custom-call | tf_op jit(solution)/shard_map/layer/pallas_call | solution.py:919
  158.1 4.1 %finish.1 = (f32[24,768]{1,0:T(8,128)}, f32[24,128]{1,0:T(8,128)}, f32[2,24]{1,0:T(2,128)}, f32[2,24]{1,0:T(2,128)}, f32[24,768]{1,0:T(8,128)}, /*index=5*/f32[2...) custom-call(f32[24,1024]{1,0:T(8,128)} %get-tuple-element.25.refs_0_, ...), custom_call_target="tpu_custom_call" | custom-call | tf_op jit(solution)/shard_map/finish/pallas_call | solution.py:949
